TPU v7x, 32 devices: a whole 2x2x4 slice. The times are simulated.
32 devices in a mesh: slab: 2 (over x), inline: 8 (over z, y), xline: 2 (over core).
Axes of the slice: x: 2, y: 2, z: 4, core: 2. Of those that a mesh axis runs over, the one named last changes fastest.
Arguments:
- traces: bfloat16 [256, 48, 128], P(('slab', 'inline'), 'xline'), parts along dimension 0, may hold values from -15 to 15
- directions: int32 [10], replicated, may hold values from 0 to 31
- init_means: float32 [32, 20], replicated, may hold values from 0.3 to 2.5
- init_variances: float32 [32, 20], replicated, may hold values from 0.01 to 0.2
- init_weights: float32 [32], replicated, may hold values from 0.01 to 1
Outputs:
- posterior: bfloat16 [256, 32, 48, 128], P(('slab', 'inline'), None, 'xline'), parts along dimension 0
- final_means: float32 [64, 20], P('slab'), parts along dimension 0
- final_variances: float32 [64, 20], P('slab'), parts along dimension 0
- final_weights: float32 [64], P('slab'), parts along dimension 0
There are 2 independent parts, one for each index of `slab`. A program takes and returns all parts, laid end to end along the dimension named above; an argument that names none is the same for every part. Nothing has to cross between parts.
All inputs are finite; a program needn't handle non-finite values.
Results may differ from a plain program's by a relative error of at most 0.001.
The roundings to bfloat16 on the way count: a program that leaves them out, or rounds other values in their place, can miss the bound.
Values may be sent and summed in bfloat16 or wider, within the bound.
No kernel may reach another device: no remote copies, remote signals or barrier semaphores. Data moves between devices by JAX's collectives and lax.ppermute only.
A program may use at most 64 MiB of HBM per device.

v0:
```python
import math

import jax
import jax.numpy as jnp
import numpy as np
from jax import lax
from jax.sharding import PartitionSpec as P

TAPS = 31
HALF = 15
AZIMUTHS = 8
DIPS = 4
ITERS = 2


eps_mag = 0.01
wavenumber = math.pi / 4.0
highest = lax.Precision.HIGHEST
cross_real = np.array([[[1.0, 0.0], [1.0, 0.0]], [[0.0, 1.0], [0.0, -1.0]]], np.float32)
cross_imag = np.array([[[0.0, 1.0], [0.0, 1.0]], [[-1.0, 0.0], [1.0, 0.0]]], np.float32)
inner_real = np.array([[1.0, 0.0], [0.0, 1.0]], np.float32)
inner_imag = np.array([[0.0, 1.0], [-1.0, 0.0]], np.float32)


def with_halo(cells, sides, width):
    for axis, dim in sides:
        count = lax.axis_size(axis)
        ends = count - 1
        head = lax.slice_in_dim(cells, 0, width, axis=dim)
        tail = lax.slice_in_dim(cells, cells.shape[dim] - width, cells.shape[dim], axis=dim)
        cells = jnp.concatenate(
            [
                lax.ppermute(tail, axis, [(i, (i + 1) % count) for i in range(ends)]),
                cells,
                lax.ppermute(head, axis, [((i + 1) % count, i) for i in range(ends)]),
            ],
            axis=dim,
        )
    return cells


def tap_table(directions):
    azimuth = (directions % AZIMUTHS).astype(jnp.float32) * (math.pi / AZIMUTHS)
    dip_angle = (directions // AZIMUTHS + 1).astype(jnp.float32) * (math.pi / (2 * DIPS + 2))
    wave_vector = wavenumber * jnp.stack(
        [
            jnp.sin(dip_angle) * jnp.cos(azimuth),
            jnp.sin(dip_angle) * jnp.sin(azimuth),
            jnp.cos(dip_angle),
        ],
        axis=1,
    )
    offsets = jnp.arange(TAPS).astype(jnp.float32) - HALF
    width_scale = HALF / 3.0
    envelope = jnp.exp(-offsets * offsets / (2.0 * width_scale * width_scale))
    envelope = envelope / jnp.sqrt(jnp.sum(envelope * envelope))
    phases = wave_vector[:, :, None] * offsets[None, None, :]
    return jnp.stack([envelope * jnp.cos(phases), envelope * jnp.sin(phases)], axis=2).astype(
        jnp.bfloat16
    )


def band_onehot(rows_in, rows_out, offset_base):
    difference = jnp.arange(rows_in)[:, None] - jnp.arange(rows_out)[None, :] + offset_base
    return (difference[:, :, None] == jnp.arange(TAPS)[None, None, :]).astype(jnp.float32)


def log_scores(feature_rows, centers, spreads, log_weights):
    inverse = 1.0 / spreads
    offset_term = log_weights - 0.5 * jnp.sum(jnp.log(2.0 * math.pi * spreads), axis=1)
    distance = jnp.sum(
        (feature_rows[None, :, :] - centers[:, :, None]) ** 2 * inverse[:, :, None], axis=1
    )
    return offset_term[:, None] - 0.5 * distance


def posterior_weights(feature_rows, centers, spreads, log_weights):
    scores = log_scores(feature_rows, centers, spreads, log_weights)
    largest = jnp.max(scores, axis=0, keepdims=True)
    exponent = jnp.exp(scores - largest)
    return exponent / jnp.sum(exponent, axis=0, keepdims=True)


def moment_pass(feature_rows, centers, spreads, log_weights):
    posterior = posterior_weights(feature_rows, centers, spreads, log_weights)
    return (
        posterior.astype(jnp.bfloat16),
        jnp.sum(posterior, axis=1),
        jnp.einsum("km,fm->kf", posterior, feature_rows, precision=highest),
        jnp.einsum("km,fm->kf", posterior, feature_rows * feature_rows, precision=highest),
    )


def per_device(traces, directions, init_means, init_variances, init_weights):
    rows_in, cols_in, samples = traces.shape
    orients = directions.shape[0]
    padded_rows = rows_in + 2 * HALF
    padded_cols = cols_in + 2 * HALF
    tap_values = tap_table(directions)
    wide_taps = tap_values.astype(jnp.float32)
    time_mats = jnp.einsum(
        "stn,orn->sort", band_onehot(samples, samples, HALF), wide_taps[:, 2], precision=highest
    )
    time_mats = time_mats.astype(jnp.bfloat16).reshape(samples, orients * 2 * samples)
    xline_taps = jnp.einsum("pqr,on->opqrn", cross_real, wide_taps[:, 1, 0]) + jnp.einsum(
        "pqr,on->opqrn", cross_imag, wide_taps[:, 1, 1]
    )
    xline_mats = jnp.einsum(
        "xyn,opqrn->oxpqry", band_onehot(padded_cols, cols_in, 0), xline_taps, precision=highest
    ).astype(jnp.bfloat16)
    inline_taps = jnp.einsum("rs,on->orsn", inner_real, wide_taps[:, 0, 0]) + jnp.einsum(
        "rs,on->orsn", inner_imag, wide_taps[:, 0, 1]
    )
    inline_mats = jnp.einsum(
        "ijn,orsn->oirsj", band_onehot(padded_rows, rows_in, 0), inline_taps, precision=highest
    ).astype(jnp.bfloat16)
    local_bands = jnp.dot(
        traces.reshape(rows_in * cols_in, samples), time_mats, preferred_element_type=jnp.float32
    )
    local_bands = local_bands.astype(jnp.bfloat16).reshape(rows_in, cols_in, orients * 2 * samples)
    wide_bands = with_halo(local_bands, (("inline", 0), ("xline", 1)), HALF)

    def orient_band(orient):
        picked = lax.dynamic_slice_in_dim(wide_bands, orient * 2 * samples, 2 * samples, 2)
        return picked.reshape(padded_rows, padded_cols, 2, samples)

    def orient_features(orient, buffer):
        band = orient_band(orient)
        across = jnp.einsum(
            "ixpt,xpqry->iqryt", band, xline_mats[orient], preferred_element_type=jnp.float32
        ).astype(jnp.bfloat16)
        inline_sum = jnp.einsum(
            "iqryt,irsj->jqsyt", across, inline_mats[orient], preferred_element_type=jnp.float32
        )
        magnitude = jnp.sqrt(
            inline_sum[:, :, 0] * inline_sum[:, :, 0]
            + inline_sum[:, :, 1] * inline_sum[:, :, 1]
            + eps_mag
        )
        return lax.dynamic_update_slice(
            buffer, magnitude.reshape(rows_in, 2, cols_in * samples), (0, 2 * orient, 0)
        )

    features = lax.fori_loop(
        0,
        orients,
        orient_features,
        jnp.zeros((rows_in, 2 * orients, cols_in * samples), jnp.float32),
    )
    total_cells = lax.axis_size("inline") * rows_in * lax.axis_size("xline") * cols_in * samples
    components = init_weights.shape[0]
    centers = init_means
    spreads = init_variances
    weights = init_weights
    log_weights = jnp.log(init_weights)
    posterior = None
    for iteration in range(ITERS):
        posterior, masses, firsts, seconds = lax.map(
            lambda feature_rows: moment_pass(feature_rows, centers, spreads, log_weights), features
        )
        total_mass, total_first, total_second = lax.psum(
            (jnp.sum(masses, axis=0), jnp.sum(firsts, axis=0), jnp.sum(seconds, axis=0)),
            ("inline", "xline"),
        )
        new_centers = (total_first + centers) / (total_mass + 1.0)[:, None]
        centred_sum = (
            total_second
            - 2.0 * new_centers * total_first
            + new_centers * new_centers * total_mass[:, None]
        )
        new_spreads = (centred_sum + spreads) / (total_mass + 1.0)[:, None]
        weights = (total_mass + 1.0) / (total_cells + components)
        log_weights = jnp.log(weights)
        centers = new_centers
        spreads = new_spreads
    return (posterior.reshape(rows_in, components, cols_in, samples), centers, spreads, weights)


def solution(mesh):
    in_specs = (P(("slab", "inline"), "xline", None), P(), P(), P(), P())
    out_specs = (
        P(("slab", "inline"), None, "xline", None),
        P("slab", None),
        P("slab", None),
        P("slab"),
    )
    return jax.shard_map(
        per_device, mesh=mesh, in_specs=in_specs, out_specs=out_specs, check_vma=False
    )
```

profile of v0, /device:TPU:0, one launch (start us, length us, event | category | flops | bytes accessed | tf_op | source)
XLA Modules:
  0.0 525.6 jit_solution(14991298293549350796)
XLA Ops:
  5.9 5.0 collective-permute-start
  12.8 76.9 %collective-permute-done = bf16[15,24,2560]{2,1,0:T(8,128)(2,1)S(1)} collective-permute-done((bf16[15,24,2560]{2,1,0:T(8,128)(2,1)S(1)}, bf16[15,24,2560]{2,1,0:T(8,128)(2,1)S(1)}, u32[]{:S(2)}, u32[]{:S(2)}) %collective-permute-start) | collective-permute-done | bytes 1843232 | tf_op jit(solution)/shard_map/ppermute | solution.py:33
  90.9 1.9 pad_maximum_fusion.1
  92.9 3.9 fusion.87
  96.9 3.1 collective-permute-start.2
  104.5 4.1 collective-permute-done.3
  108.6 8.8 %pad_maximum_fusion = bf16[46,54,2560]{2,0,1:T(8,128)(2,1)S(1)} fusion(bf16[46,15,2560]{2,0,1:T(8,128)(2,1)} %collective-permute-done.3, bf16[15,24,2560]{2,0,1:T(8,128)(2,1)} %copy-done.3, bf16[16,24,2560]{2,0,1:T(8,128)(2,1)S(1)} %copy.81, bf16[15,24,2560]{2,0,1:T(8,128)(2,1)} %copy-done.2, bf16[46,15,2560]{2,0,1:T(8,128)(2,1)} %collective-permute-done.2), kind=kLoop, calls=%fused_computation.56 | loop fusion | flops 63590400 | bytes 25436160 | tf_op jit(solution)/shard_map/concatenate | solution.py:31
  117.5 9.4 %copy.85 = bf16[46,54,2560]{2,1,0:T(8,128)(2,1)} copy(bf16[46,54,2560]{2,0,1:T(8,128)(2,1)S(1)} %pad_maximum_fusion) | data formatting | bytes 25436160 | tf_op jit(solution)/shard_map/while | solution.py:144
  126.9 2.7 broadcast_in_dim.24.clone
  129.6 53.1 %while.45 = (s32[]{:T(128)}, f32[16,20,3072]{2,1,0:T(8,128)}, bf16[10,46,2,2,16]{1,4,2,3,0:T(8,128)(2,1)S(1)}, bf16[10,54,2,2,2,24]{1,5,2,4,3,0:T(8,128)(2,1)S(1...) while((s32[]{:T(128)}, f32[16,20,3072]{2,1,0:T(8,128)}, ...), condition=%wide.region_2.3_spmd, body=%wide.region_1.2_spmd.sunk | while | flops 159227904 | bytes 13011161 | solution.py:144
  183.4 106.9 %while.46 = (s32[]{:T(128)}, f32[16,32]{1,0:T(8,128)S(1)}, f32[16,32,20]{1,2,0:T(8,128)S(1)}, f32[16,32,20]{1,2,0:T(8,128)}, f32[32,20]{0,1:T(8,128)S(1)}, /*ind...) while((s32[]{:T(128)}, f32[16,32]{1,0:T(8,128)S(1)}, ...), condition=%wide.region_9.10_spmd, body=%wide.region_3.9_spmd.sunk | while | flops 56975232 | bytes 3835885 | solution.py:158
  186.2 2.1 fusion.126
  192.9 2.1 fusion.126
  199.6 2.2 fusion.126
  206.2 2.2 fusion.126
  212.9 2.2 fusion.126
  219.6 2.2 fusion.126
  226.2 2.1 fusion.126
  232.9 2.2 fusion.126
  239.6 2.2 fusion.126
  246.3 2.2 fusion.126
  252.9 2.2 fusion.126
  259.6 2.1 fusion.126
  266.3 2.1 fusion.126
  273.0 2.2 fusion.126
  279.6 2.1 fusion.126
  286.3 2.2 fusion.126
  291.3 61.8 %all-reduce.1 = (f32[32,20]{0,1:T(8,128)S(1)}, f32[32]{0:T(128)S(1)}, f32[32,20]{0,1:T(8,128)S(1)}) all-reduce(f32[32,20]{0,1:T(8,128)S(1)} %reduce_sum.137, f32[32]{0:T(128)S(1)} %reduce_sum.138, f32[32,20]{0,1:T(8,128)S(1)} %reduce_sum.136), channel_id=1, replica_groups=mesh['slab'=2,'inline'=8,'xline'=2] {'inline','xline'}, use_global_device_ids=true, to_apply=%region_13.14 | all-reduce | flops 1312 | bytes 10496 | tf_op jit(solution)/shard_map/psum | solution.py:161
  353.9 109.3 %while.47 = (s32[]{:T(128)}, bf16[16,32,3072]{2,1,0:T(8,128)(2,1)S(1)}, f32[16,32]{1,0:T(8,128)S(1)}, f32[16,32,20]{1,2,0:T(8,128)S(1)}, f32[16,32,20]{1,2,0:T(8...) while((s32[]{:T(128)}, ...), condition=%wide.region_22.23_spmd, body=%wide.region_16.22_spmd.sunk | while | flops 57466752 | bytes 4450809 | solution.py:158
  358.2 2.2 fusion.134
  365.0 2.2 fusion.134
  371.9 2.2 fusion.134
  378.7 2.2 fusion.134
  384.0 1.5 fusion.133
  385.5 2.2 fusion.134
  392.4 2.2 fusion.134
  399.2 2.2 fusion.134
  406.0 2.2 fusion.134
  412.9 2.2 fusion.134
  419.7 2.2 fusion.134
  426.6 2.2 fusion.134
  433.4 2.2 fusion.134
  440.2 2.2 fusion.134
  447.1 2.2 fusion.134
  453.9 2.2 fusion.134
  460.7 2.2 fusion.134
  464.2 57.7 %all-reduce = (f32[32,20]{0,1:T(8,128)S(1)}, f32[32]{0:T(128)S(1)}, f32[32,20]{0,1:T(8,128)S(1)}) all-reduce(f32[32,20]{0,1:T(8,128)S(1)} %reduce_sum.139, f32[32]{0:T(128)S(1)} %reduce_sum.140, f32[32,20]{0,1:T(8,128)S(1)} %reduce_sum.141), channel_id=1, replica_groups=mesh['slab'=2,'inline'=8,'xline'=2] {'inline','xline'}, use_global_device_ids=true, to_apply=%region_24.25 | all-reduce | flops 1312 | bytes 10496 | tf_op jit(solution)/shard_map/psum | solution.py:161
  522.4 2.5 copy.111
  (452 shorter events, 213.7 us)
Async XLA Ops:
  0.6 4.3 copy-start
  5.9 83.8 %collective-permute-start = (bf16[15,24,2560]{2,1,0:T(8,128)(2,1)S(1)}, bf16[15,24,2560]{2,1,0:T(8,128)(2,1)S(1)}, u32[]{:S(2)}, u32[]{:S(2)}) collective-permute-start(bf16[15,24,2560]{2,1,0:T(8,128)(2,1)S(1)} %bitcast.205), channel_id=1, source_target_pairs={{0,2},{2,4},{4,6},{6,8},{8,10},{10,12},{12,14},{1,3},{3,5},{5,7},{... | collective-permute-start | bytes 5529608 | tf_op jit(solution)/shard_map/ppermute | solution.py:33
  10.9 79.4 %collective-permute-start.1 = (bf16[15,24,2560]{2,1,0:T(8,128)(2,1)S(1)}, bf16[15,24,2560]{2,1,0:T(8,128)(2,1)S(1)}, u32[]{:S(2)}, u32[]{:S(2)}) collective-permute-start(bf16[15,24,2560]{2,1,0:T(8,128)(2,1)S(1)} %bitcast.204), channel_id=1, source_target_pairs={{2,0},{4,2},{6,4},{8,6},{10,8},{12,10},{14,12},{3,1},{5,3},{7,5},{... | collective-permute-start | bytes 5529608 | tf_op jit(solution)/shard_map/ppermute | solution.py:35
  90.3 2.5 copy-start.2
  90.9 1.9 copy-start.3
  92.9 8.6 %copy-start.7 = (f32[2,2,2]{2,1,0:T(2,128)S(1)}, f32[2,2,2]{2,1,0:T(2,128)}, u32[]{:S(2)}) copy-start(f32[2,2,2]{2,1,0:T(2,128)} %constant.190.clone) | copy-start | bytes 100
  92.9 8.6 %copy-start.8 = (f32[2,2,2]{2,1,0:T(2,128)S(1)}, f32[2,2,2]{2,1,0:T(2,128)}, u32[]{:S(2)}) copy-start(f32[2,2,2]{2,1,0:T(2,128)} %constant.191.clone) | copy-start | bytes 100
  92.9 9.6 %copy-start.9 = (f32[2,2]{1,0:T(2,128)S(1)}, f32[2,2]{1,0:T(2,128)}, u32[]{:S(2)}) copy-start(f32[2,2]{1,0:T(2,128)} %constant.192.clone) | copy-start | bytes 52
  92.9 9.6 %copy-start.10 = (f32[2,2]{1,0:T(2,128)S(1)}, f32[2,2]{1,0:T(2,128)}, u32[]{:S(2)}) copy-start(f32[2,2]{1,0:T(2,128)} %constant.193.clone) | copy-start | bytes 52
  92.9 10.1 %copy-start.11 = (f32[32]{0:T(128)S(1)}, f32[32]{0:T(128)}, u32[]{:S(2)}) copy-start(f32[32]{0:T(128)} %param.19) | copy-start | bytes 388
  96.9 7.7 %collective-permute-start.2 = (bf16[46,15,2560]{2,0,1:T(8,128)(2,1)}, bf16[46,15,2560]{2,0,1:T(8,128)(2,1)}, u32[]{:S(2)}, u32[]{:S(2)}) collective-permute-start(bf16[46,15,2560]{2,0,1:T(8,128)(2,1)} %get-tuple-element.415), channel_id=1, source_target_pairs={{0,1},{2,3},{4,5},{6,7},{8,9},{10,11},{12,13},{14,15},{16,17},{18,... | collective-permute-start | bytes 10598408 | tf_op jit(solution)/shard_map/ppermute | solution.py:33
  100.0 8.7 %collective-permute-start.3 = (bf16[46,15,2560]{2,0,1:T(8,128)(2,1)}, bf16[46,15,2560]{2,0,1:T(8,128)(2,1)}, u32[]{:S(2)}, u32[]{:S(2)}) collective-permute-start(bf16[46,15,2560]{2,0,1:T(8,128)(2,1)} %get-tuple-element.416), channel_id=1, source_target_pairs={{1,0},{3,2},{5,4},{7,6},{9,8},{11,10},{13,12},{15,14},{17,16},{19,... | collective-permute-start | bytes 10598408 | tf_op jit(solution)/shard_map/ppermute | solution.py:35
  129.6 53.8 %copy-start.5 = (f32[32,20]{0,1:T(8,128)S(1)}, f32[32,20]{0,1:T(8,128)}, u32[]{:S(2)}) copy-start(f32[32,20]{0,1:T(8,128)} %param.18) | copy-start | bytes 7684
  129.6 53.8 %copy-start.6 = (f32[32,20]{0,1:T(8,128)S(1)}, f32[32,20]{0,1:T(8,128)}, u32[]{:S(2)}) copy-start(f32[32,20]{0,1:T(8,128)} %param.17) | copy-start | bytes 7684
  183.4 170.5 %copy-start.4 = (bf16[16,32,3072]{2,1,0:T(8,128)(2,1)S(1)}, bf16[16,32,3072]{2,1,0:T(8,128)(2,1)}, u32[]{:S(2)}) copy-start(bf16[16,32,3072]{2,1,0:T(8,128)(2,1)} %custom-call) | copy-start | bytes 9437188
  463.2 62.4 %copy-start.1 = (bf16[16,24,128]{2,1,0:T(8,128)(2,1)S(1)}, bf16[16,24,128]{2,1,0:T(8,128)(2,1)}, u32[]{:S(2)}) copy-start(bf16[16,24,128]{2,1,0:T(8,128)(2,1)} %param.15) | copy-start | bytes 294916
where the time goes:
time: 530 us; the launch traced here: 526 us
  matrix products  130 us (25%)
  blocking collectives  119 us (22%)
  local copies, waits for them, and re-layouts  97.6 us (18%)
  waiting for transfers between devices  82.5 us (16%)
  other arithmetic  81.9 us (15%)
  starting transfers between devices  10.9 us (2%)
    psum x2, blocking collectives, per_device(): lax.psum((jnp.sum(masses, axis=0), jnp.sum(firsts, axis=0), jnp.sum(secon...  119 us
    ppermute x2, waiting for transfers between devices, with_halo(): lax.ppermute(tail, axis, [(i, (i + 1) % count) for i in range(ends)])  78.4 us
    dot_general x32, matrix products, moment_pass(): jnp.einsum('km,fm->kf', posterior, feature_rows * feature_rows, precision...  69 us
    dot_general x32, matrix products, moment_pass(): jnp.einsum('km,fm->kf', posterior, feature_rows, precision=highest)  49 us
    reduce_sum x32, other arithmetic, log_scores(): jnp.sum((feature_rows[None, :, :] - centers[:, :, None]) ** 2 * inverse[:...  42.6 us
    sub x32, local copies, waits for them, and re-layouts, log_scores(): feature_rows[None, :, :] - centers[:, :, None]  31.7 us
    reshape x10, local copies, waits for them, and re-layouts, orient_band(): return picked.reshape(padded_rows, padded_cols, 2, samples)  15 us
    dynamic_slice x10, local copies, waits for them, and re-layouts, orient_band(): lax.dynamic_slice_in_dim(wide_bands, orient * 2 * samples, 2 * samples, 2)  14.1 us
  transfers between devices with their start and end apart: 4, of which 3 were waited for; matrix products, arithmetic and copies ran while one was open for 0% of the time, Pallas kernels for 0%

commit v1 on v0

v1 whole, which is shorter than its diff:
```python
import functools
import math

import jax
import jax.numpy as jnp
from jax import lax
from jax.experimental import pallas as pl
from jax.experimental.pallas import tpu as pltpu
from jax.sharding import PartitionSpec as P

TAPS = 31
HALF = 15
AZIMUTHS = 8
DIPS = 4
LANES = 128
SUBLANES = 8

eps_mag = 0.01
wavenumber = math.pi / 4.0


def round_up(value, step):
    return (value + step - 1) // step * step


def tap_table(directions):
    azimuth = (directions % AZIMUTHS).astype(jnp.float32) * (math.pi / AZIMUTHS)
    dip_angle = (directions // AZIMUTHS + 1).astype(jnp.float32) * (math.pi / (2 * DIPS + 2))
    wave_vector = wavenumber * jnp.stack(
        [
            jnp.sin(dip_angle) * jnp.cos(azimuth),
            jnp.sin(dip_angle) * jnp.sin(azimuth),
            jnp.cos(dip_angle),
        ],
        axis=1,
    )
    offsets = jnp.arange(TAPS).astype(jnp.float32) - HALF
    width_scale = HALF / 3.0
    envelope = jnp.exp(-offsets * offsets / (2.0 * width_scale * width_scale))
    envelope = envelope / jnp.sqrt(jnp.sum(envelope * envelope))
    phases = wave_vector[:, :, None] * offsets[None, None, :]
    return jnp.stack([envelope * jnp.cos(phases), envelope * jnp.sin(phases)], axis=2).astype(
        jnp.bfloat16
    )


def split3(values):
    high = values.astype(jnp.bfloat16)
    rest = values - high.astype(jnp.float32)
    middle = rest.astype(jnp.bfloat16)
    low = (rest - middle.astype(jnp.float32)).astype(jnp.bfloat16)
    return high, middle, low


def matrices_kernel(dims, taps_ref, time_ref, xline_ref, inline_ref):
    orients, samples, cols, rows, window = dims
    side = lax.axis_index("xline")
    lanes = lax.broadcasted_iota(jnp.int32, (SUBLANES, LANES), 1)[:1]

    def sheared(line, count, shift, width):
        wide = jnp.broadcast_to(line[:, :width], (count, width))
        return pltpu.roll(wide, shift % width, 1, stride=1, stride_axis=0)

    for orient in range(orients):
        line = lambda axis, part: taps_ref[pl.ds(orient * 6 + axis * 2 + part, 1), :]
        for part in range(2):
            time_ref[orient, :, part * samples : (part + 1) * samples] = sheared(
                line(2, part), samples, 2 * samples - HALF, 2 * samples
            )[:, :samples].astype(jnp.bfloat16)

        def xline_half(part, half, slot):
            shift = LANES - HALF + slot * cols
            if half:
                moved = jnp.where(
                    side == 0,
                    sheared(line(1, part), cols, shift + LANES - cols, LANES),
                    sheared(line(1, part), cols, shift + cols, LANES),
                )
            else:
                moved = sheared(line(1, part), cols, shift, LANES)
            return jnp.where((lanes >= slot * cols) & (lanes < (slot + 1) * cols), moved, 0.0)

        cosine = [xline_half(0, 0, p * 2) + xline_half(0, 1, p * 2 + 1) for p in range(2)]
        sine = [xline_half(1, 0, p * 2) + xline_half(1, 1, p * 2 + 1) for p in range(2)]
        xline_ref[orient] = jnp.concatenate(
            [
                cosine[0] - sine[1],
                sine[0] + cosine[1],
                cosine[0] + sine[1],
                sine[0] - cosine[1],
            ],
            axis=0,
        )[:, : 4 * cols].astype(jnp.bfloat16)

        def inline_part(part, slot):
            moved = sheared(line(0, part), rows, slot * window, LANES)
            return jnp.where((lanes >= slot * window) & (lanes < (slot + 1) * window), moved, 0.0)

        inline_ref[orient] = jnp.concatenate(
            [
                inline_part(0, 0) - inline_part(1, 1),
                inline_part(1, 0) + inline_part(0, 1),
            ],
            axis=0,
        )[:, : 2 * window].astype(jnp.bfloat16)


def score_matrix(centers, spreads, log_weights, feats, slot):
    lanes = lax.broadcasted_iota(jnp.int32, centers.shape, 1)
    real = lanes < feats
    inverse = jnp.where(real, 1.0 / spreads, 0.0)
    linear = jnp.where(real, centers * inverse, 0.0)
    logs = jnp.where(real, jnp.log(2.0 * math.pi * spreads), 0.0)
    terms = logs + jnp.where(real, centers * linear, 0.0)
    constant = log_weights - 0.5 * jnp.sum(terms, axis=1, keepdims=True)
    packed = linear + jnp.where(lanes == feats, constant, 0.0)
    packed = packed + pltpu.roll(-0.5 * inverse, slot, 1)
    wide = jnp.concatenate([packed, jnp.zeros_like(packed)], axis=1)
    high, middle, low = [piece.astype(jnp.float32) for piece in split3(wide)]
    second = lambda piece: pltpu.roll(piece, 2 * slot, 1)
    third = lambda piece: pltpu.roll(piece, 4 * slot, 1)
    return jnp.concatenate(
        [high + second(high) + third(high), middle + second(middle), low], axis=0
    )[:, : 6 * slot].astype(jnp.bfloat16)


def column(line, count):
    row_ids = lax.broadcasted_iota(jnp.int32, (count, LANES), 0)
    lane_ids = lax.broadcasted_iota(jnp.int32, (count, LANES), 1)
    return jnp.sum(jnp.where(row_ids == lane_ids, line, 0.0), axis=1, keepdims=True)


def expectation(features, matrix, components):
    both = jnp.concatenate([features, features * features], axis=0)
    data = jnp.concatenate(split3(both), axis=0)
    scores = jnp.dot(matrix, data, preferred_element_type=jnp.float32)
    scores = (
        scores[:components]
        + scores[components : 2 * components]
        + scores[2 * components : 3 * components]
    )
    exponent = jnp.exp(scores - jnp.max(scores, axis=0, keepdims=True))
    shares = exponent * (1.0 / jnp.sum(exponent, axis=0, keepdims=True))
    high = shares.astype(jnp.bfloat16)
    low = (shares - high.astype(jnp.float32)).astype(jnp.bfloat16)
    sums = lax.dot_general(
        jnp.concatenate([high, low], axis=0),
        data,
        (((1,), (1,)), ((), ())),
        preferred_element_type=jnp.float32,
    )
    return shares, sums


def gathered(features_ref, first, count, slot):
    place = lambda k: pl.multiple_of((first + k) * slot, SUBLANES)
    return jnp.concatenate([features_ref[pl.ds(place(k), slot), :] for k in range(count)], axis=1)


def fold_sums(sums, components, slot):
    both = sums[:components] + sums[components:]
    wide = jnp.concatenate(
        [both, jnp.zeros((components, 2 * LANES - 6 * slot), jnp.float32)], axis=1
    )
    total = wide + pltpu.roll(wide, 2 * LANES - 2 * slot, 1) + pltpu.roll(
        wide, 2 * LANES - 4 * slot, 1
    )
    return total[:, :LANES]


def features_kernel(dims, *refs):
    orients, samples, cols, rows, window, components, chunk = dims
    halves, refs = refs[:6], refs[6:]
    time_ref, xline_ref, inline_ref, means_ref, variances_ref, weights_ref = refs[:6]
    features_ref, sums_ref, traces, across, params, total = refs[6:]
    feats = 2 * orients
    slot = round_up(feats + 1, SUBLANES)
    orient = pl.program_id(0)
    @pl.when(orient == 0)
    def _():
        own, other, swap_one, swap_one_other, swap_two, swap_two_other = halves
        even = lax.rem(lax.axis_index("inline"), 2) == 0

        def put(place, near, far):
            traces[pl.ds(place * 2 * cols, 2 * cols), :] = jnp.concatenate(
                [near.astype(jnp.float32), far.astype(jnp.float32)], axis=0
            ).astype(jnp.bfloat16)

        for row in range(rows):
            put(HALF + row, own[row], other[row])
            one = swap_one[row].astype(jnp.float32)
            one_far = swap_one_other[row].astype(jnp.float32)
            two = swap_two[row].astype(jnp.float32)
            two_far = swap_two_other[row].astype(jnp.float32)
            if row >= rows - HALF:
                put(row - (rows - HALF), jnp.where(even, two, one), jnp.where(even, two_far, one_far))
            if row < HALF:
                put(HALF + rows + row, jnp.where(even, one, two), jnp.where(even, one_far, two_far))
        for place in range(rows + 2 * HALF, window):
            traces[pl.ds(place * 2 * cols, 2 * cols), :] = jnp.zeros(
                (2 * cols, samples), jnp.bfloat16
            )
        blank = lax.broadcasted_iota(jnp.int32, (slot - feats, samples), 0) == 0

        @pl.loop(0, rows * cols)
        def _(cell):
            features_ref[pl.ds(cell * slot + feats, slot - feats), :] = blank.astype(jnp.float32)

    lines = 2 * cols
    for pair in range(window // 2):
        block = traces[pl.ds(pair * 2 * lines, 2 * lines), :]
        band = jnp.dot(block, time_ref[0], preferred_element_type=jnp.float32)
        stacked = jnp.concatenate(
            [
                jnp.concatenate(
                    [band[:lines, p * samples : (p + 1) * samples] for p in range(2)], axis=0
                ),
                jnp.concatenate(
                    [band[lines:, p * samples : (p + 1) * samples] for p in range(2)], axis=0
                ),
            ],
            axis=1,
        ).astype(jnp.bfloat16)
        crossed = jnp.dot(xline_ref[0], stacked, preferred_element_type=jnp.float32)
        for k in range(2):
            across[pl.ds(2 * pair + k, 4 * cols, stride=window), :] = crossed[
                :, k * samples : (k + 1) * samples
            ]
    for polarity in range(2):
        for col in range(0, cols, 2):

            def taken(k, part):
                place = ((polarity * 2 + part) * cols + col + k) * window
                return across[pl.ds(place, window), :]

            stacked = jnp.concatenate(
                [jnp.concatenate([taken(k, 0), taken(k, 1)], axis=0) for k in range(2)], axis=1
            ).astype(jnp.bfloat16)
            found = jnp.dot(inline_ref[0], stacked, preferred_element_type=jnp.float32)
            real_part, imag_part = found[:rows], found[rows:]
            size = jnp.sqrt(real_part * real_part + imag_part * imag_part + eps_mag)
            for k in range(2):
                place = (col + k) * slot + 2 * orient + polarity
                features_ref[pl.ds(place, rows, stride=cols * slot), :] = size[
                    :, k * samples : (k + 1) * samples
                ]

    @pl.when(orient == orients - 1)
    def _():
        params[...] = jnp.ones(params.shape, jnp.float32)
        params[:components, :feats] = means_ref[...]
        params[components:, :feats] = variances_ref[...]
        log_weights = jnp.log(column(jnp.concatenate(
            [weights_ref[...], jnp.ones((1, LANES - components), jnp.float32)], axis=1), components))
        matrix = score_matrix(params[:components], params[components:], log_weights, feats, slot)
        total[...] = jnp.zeros(total.shape, jnp.float32)

        @pl.loop(0, rows)
        def _(row):
            partial = jnp.zeros(total.shape, jnp.float32)
            for start in range(0, cols, chunk):
                block = gathered(features_ref, row * cols + start, chunk, slot)
                partial = partial + expectation(block, matrix, components)[1]
            total[...] += partial

        sums_ref[...] = fold_sums(total[...], components, slot)


def new_params(sums, centers, spreads, feats, slot, cells):
    components = centers.shape[0]
    mass = sums[:, feats : feats + 1]
    first = sums
    second = pltpu.roll(sums, LANES - slot, 1)
    scale = 1.0 / (mass + 1.0)
    moved = (first + centers) * scale
    centred = second - 2.0 * moved * first + moved * moved * mass
    return moved, (centred + spreads) * scale, (mass + 1.0) / (cells + components)


def posterior_kernel(dims, *refs):
    orients, samples, cols, rows, components, chunk, cells = dims
    features_ref, means_ref, variances_ref, before_ref = refs[:4]
    posterior_ref, sums_ref, centers_ref, spreads_ref, matrix, total, turned = refs[4:]
    feats = 2 * orients
    slot = round_up(feats + 1, SUBLANES)
    row = pl.program_id(0)
    @pl.when(row == 0)
    def _():
        centers_ref[...] = jnp.zeros(centers_ref.shape, jnp.float32)
        spreads_ref[...] = jnp.ones(spreads_ref.shape, jnp.float32)
        centers_ref[:, :feats] = means_ref[...]
        spreads_ref[:, :feats] = variances_ref[...]
        centers, spreads, weights = new_params(
            before_ref[...], centers_ref[...], spreads_ref[...], feats, slot, cells
        )
        lanes = lax.broadcasted_iota(jnp.int32, centers.shape, 1)
        centers = jnp.where(lanes < feats, centers, 0.0)
        spreads = jnp.where(lanes < feats, spreads, 1.0)
        centers_ref[...] = centers
        spreads_ref[...] = spreads
        matrix[...] = score_matrix(centers, spreads, jnp.log(weights), feats, slot)
        total[...] = jnp.zeros(total.shape, jnp.float32)

    partial = jnp.zeros(total.shape, jnp.float32)
    for start in range(0, cols, chunk):
        shares, sums = expectation(
            gathered(features_ref, start, chunk, slot), matrix[...], components
        )
        partial = partial + sums
        for k in range(chunk):
            turned[pl.ds(start + k, components, stride=cols), :] = shares[
                :, k * samples : (k + 1) * samples
            ]
    total[...] += partial
    for component in range(components):
        posterior_ref[0, component] = turned[pl.ds(component * cols, cols), :].astype(jnp.bfloat16)

    @pl.when(row == pl.num_programs(0) - 1)
    def _():
        sums_ref[...] = fold_sums(total[...], components, slot)


def exchange(values, axis, pairs):
    return lax.ppermute(values, axis, [p for a, b in pairs for p in ((a, b), (b, a))])


def group_sum(values):
    axes = ("inline", "xline")
    count = lax.axis_size("inline") * lax.axis_size("xline")
    if count & (count - 1):
        return lax.psum(values, axes)
    step = 1
    while step < count:
        radix = min(4, count // step)
        arrived = [
            lax.ppermute(values, axes, [(i, i ^ (step * d)) for i in range(count)])
            for d in range(1, radix)
        ]
        if radix == 4:
            values = (values + arrived[0]) + (arrived[1] + arrived[2])
        else:
            values = values + arrived[0]
        step *= radix
    return values


def per_device(traces, directions, init_means, init_variances, init_weights):
    rows, cols, samples = traces.shape
    orients = directions.shape[0]
    components = init_weights.shape[0]
    feats = 2 * orients
    slot = round_up(feats + 1, SUBLANES)
    window = round_up(rows + 2 * HALF, 16)
    inlines = lax.axis_size("inline")
    if lax.axis_size("xline") != 2 or samples != LANES or rows < HALF:
        raise ValueError("unsupported sizes")

    core_pairs = [(0, 1)]
    other = exchange(traces, "xline", core_pairs)
    swap_one = exchange(traces, "inline", [(i, i + 1) for i in range(0, inlines - 1, 2)])
    swap_two = exchange(traces, "inline", [(i, i + 1) for i in range(1, inlines - 1, 2)])
    swap_one_other = exchange(swap_one, "xline", core_pairs)
    swap_two_other = exchange(swap_two, "xline", core_pairs)

    taps = tap_table(directions).astype(jnp.float32)
    taps = jnp.concatenate([taps[:, :2], taps[:, 2:, :, ::-1]], axis=1)
    taps = jnp.pad(taps.reshape(orients * 6, TAPS), ((0, 0), (0, 2 * LANES - TAPS)))
    vmem = pl.BlockSpec(memory_space=pltpu.VMEM)
    time_mats, xline_mats, inline_mats = pl.pallas_call(
        functools.partial(matrices_kernel, (orients, samples, cols, rows, window)),
        out_shape=(
            jax.ShapeDtypeStruct((orients, samples, 2 * samples), jnp.bfloat16),
            jax.ShapeDtypeStruct((orients, 4 * cols, 4 * cols), jnp.bfloat16),
            jax.ShapeDtypeStruct((orients, 2 * rows, 2 * window), jnp.bfloat16),
        ),
        in_specs=[vmem],
        out_specs=(vmem, vmem, vmem),
        name="filter_matrices",
        cost_estimate=pl.CostEstimate(flops=0, bytes_accessed=4_000_000, transcendentals=0),
    )(taps)

    whole = lambda *shape: pl.BlockSpec(shape, lambda o: (0,) * len(shape))
    chunk = 4
    features, sums = pl.pallas_call(
        functools.partial(
            features_kernel, (orients, samples, cols, rows, window, components, chunk)
        ),
        grid=(orients,),
        out_shape=(
            jax.ShapeDtypeStruct((rows * cols * slot, samples), jnp.float32),
            jax.ShapeDtypeStruct((components, LANES), jnp.float32),
        ),
        in_specs=[whole(rows, cols, samples)] * 6
        + [
            pl.BlockSpec((1, samples, 2 * samples), lambda o: (o, 0, 0)),
            pl.BlockSpec((1, 4 * cols, 4 * cols), lambda o: (o, 0, 0)),
            pl.BlockSpec((1, 2 * rows, 2 * window), lambda o: (o, 0, 0)),
            whole(components, feats),
            whole(components, feats),
            whole(1, components),
        ],
        out_specs=(whole(rows * cols * slot, samples), whole(components, LANES)),
        scratch_shapes=[
            pltpu.VMEM((window * 2 * cols, samples), jnp.bfloat16),
            pltpu.VMEM((4 * cols * window, samples), jnp.float32),
            pltpu.VMEM((2 * components, LANES), jnp.float32),
            pltpu.VMEM((2 * components, 6 * slot), jnp.float32),
        ],
        compiler_params=pltpu.CompilerParams(vmem_limit_bytes=40 * 2**20),
        name="features_and_first_moments",
    )(
        traces, other, swap_one, swap_one_other, swap_two, swap_two_other,
        time_mats, xline_mats, inline_mats,
        init_means, init_variances, init_weights.reshape(1, components),
    )
    sums = group_sum(sums)
    cells = inlines * rows * lax.axis_size("xline") * cols * samples
    posterior, sums, centers, spreads = pl.pallas_call(
        functools.partial(
            posterior_kernel, (orients, samples, cols, rows, components, chunk, cells)
        ),
        grid=(rows,),
        out_shape=(
            jax.ShapeDtypeStruct((rows, components, cols, samples), jnp.bfloat16),
            jax.ShapeDtypeStruct((components, LANES), jnp.float32),
            jax.ShapeDtypeStruct((components, LANES), jnp.float32),
            jax.ShapeDtypeStruct((components, LANES), jnp.float32),
        ),
        in_specs=[
            pl.BlockSpec((cols * slot, samples), lambda r: (r, 0)),
            whole(components, feats),
            whole(components, feats),
            whole(components, LANES),
        ],
        out_specs=(
            pl.BlockSpec((1, components, cols, samples), lambda r: (r, 0, 0, 0)),
            whole(components, LANES),
            whole(components, LANES),
            whole(components, LANES),
        ),
        scratch_shapes=[
            pltpu.VMEM((3 * components, 6 * slot), jnp.bfloat16),
            pltpu.VMEM((2 * components, 6 * slot), jnp.float32),
            pltpu.VMEM((components * cols, samples), jnp.float32),
        ],
        compiler_params=pltpu.CompilerParams(vmem_limit_bytes=40 * 2**20),
        name="posterior_and_second_moments",
    )(features, init_means, init_variances, sums)
    sums = group_sum(sums)
    mass = sums[:, feats : feats + 1]
    first = sums[:, :feats]
    second = sums[:, slot : slot + feats]
    centers, spreads = centers[:, :feats], spreads[:, :feats]
    moved = (first + centers) / (mass + 1.0)
    centred = second - 2.0 * moved * first + moved * moved * mass
    final_spreads = (centred + spreads) / (mass + 1.0)
    return posterior, moved, final_spreads, (mass[:, 0] + 1.0) / (cells + components)


def solution(mesh):
    in_specs = (P(("slab", "inline"), "xline", None), P(), P(), P(), P())
    out_specs = (
        P(("slab", "inline"), None, "xline", None),
        P("slab", None),
        P("slab", None),
        P("slab"),
    )
    return jax.shard_map(
        per_device, mesh=mesh, in_specs=in_specs, out_specs=out_specs, check_vma=False
    )
```

time: 530 us -> 98.3 us (0.19)
  matrix products: 130 us -> 0 us
  blocking collectives: 119 us -> 0 us
  local copies, waits for them, and re-layouts: 97.6 us -> 8.23 us
  other arithmetic: 81.9 us -> 3.52 us
  waiting for transfers between devices: 82.5 us -> 10.5 us
  Pallas kernels: 0 us -> 54.6 us
  starting transfers between devices: 10.9 us -> 19.5 us
    dot_general x88 -> x0, matrix products: 130 us -> none  [the longest x32 69 us: moment_pass(): jnp.einsum('km,fm->kf', posterior, feature_rows * feature_rows, precision...]
    psum x2 -> x0, blocking collectives: 119 us -> none  [per_device(): lax.psum((jnp.sum(masses, axis=0), jnp.sum(firsts, axis=0), jnp.sum(secon...]
    ppermute x4 -> x17, waiting for transfers between devices: 82.5 us -> 10.5 us  [the longest x12 10.5 us: group_sum(): lax.ppermute(values, axes, [(i, i ^ step * d) for i in range(count)])]
    reduce_sum x134 -> x0, other arithmetic: 59.6 us -> none  [the longest x32 42.6 us: log_scores(): jnp.sum((feature_rows[None, :, :] - centers[:, :, None]) ** 2 * inverse[:...]
    pallas_call x0 -> x3, Pallas kernels: none -> 54.6 us  [the longest x1 35.6 us: per_device(): pl.pallas_call(functools.partial(features_kernel, (orients, samples, cols...]
    sub x32 -> x0, local copies, waits for them, and re-layouts: 31.7 us -> none  [log_scores(): feature_rows[None, :, :] - centers[:, :, None]]
    reshape x11 -> x1, local copies, waits for them, and re-layouts: 15.6 us -> 0.02 us  [per_device(): taps.reshape(orients * 6, TAPS)]
    dynamic_slice x10 -> x0, local copies, waits for them, and re-layouts: 14.1 us -> none  [orient_band(): lax.dynamic_slice_in_dim(wide_bands, orient * 2 * samples, 2 * samples, 2)]
  transfers between devices with their start and end apart: 4 -> 17, of which waited for: 3 -> 9; matrix products, arithmetic and copies ran while one was open for 0% -> 5% of each run, Pallas kernels for 0% -> 3%
where the time goes in v1:
time: 98.3 us; the launch traced here: 97.9 us
  Pallas kernels  54.6 us (56%)
  starting transfers between devices  19.5 us (20%)
  waiting for transfers between devices  10.5 us (11%)
  local copies, waits for them, and re-layouts  8.23 us (8%)
  other arithmetic  3.52 us (4%)
  between operations  1.47 us (1%)
    pallas_call x1, Pallas kernels, per_device(): pl.pallas_call(functools.partial(features_kernel, (orients, samples, cols...  35.6 us
    pallas_call x1, Pallas kernels, per_device(): pl.pallas_call(functools.partial(posterior_kernel, (orients, samples, col...  16.6 us
    ppermute x12, starting transfers between devices, group_sum(): lax.ppermute(values, axes, [(i, i ^ step * d) for i in range(count)])  15.2 us
    ppermute x12, waiting for transfers between devices, group_sum(): lax.ppermute(values, axes, [(i, i ^ step * d) for i in range(count)])  10.5 us
    unnamed x14, local copies, waits for them, and re-layouts  7.38 us
    ppermute x5, starting transfers between devices, exchange(): lax.ppermute(values, axis, [p for a, b in pairs for p in ((a, b), (b, a))])  4.35 us
    pallas_call x1, Pallas kernels, per_device(): pl.pallas_call(functools.partial(matrices_kernel, (orients, samples, cols...  2.45 us
  transfers between devices with their start and end apart: 17, of which 9 were waited for; matrix products, arithmetic and copies ran while one was open for 5% of the time, Pallas kernels for 3%

profile of v1, /device:TPU:0, one launch (start us, length us, event | category | flops | bytes accessed | tf_op | source)
XLA Modules:
  0.0 97.9 jit_solution(17341246052571549424)
XLA Ops:
  0.6 3.0 %collective-permute-start.1 = (bf16[16,24,128]{2,1,0:T(8,128)(2,1)}, bf16[16,24,128]{2,1,0:T(8,128)(2,1)S(1)}, u32[]{:S(2)}, u32[]{:S(2)}) collective-permute-start(bf16[16,24,128]{2,1,0:T(8,128)(2,1)} %refs_0_.1), channel_id=1, source_target_pairs={{0,2},{2,0},{4,6},{6,4},{8,10},{10,8},{12,14},{14,12},{1,3},{3,1},... | collective-permute-start | bytes 294920 | tf_op jit(solution)/shard_map/ppermute | solution.py:324
  3.7 0.7 collective-permute-start.3
  4.3 0.6 multiply_reduce_fusion
  5.7 0.7 fusion.12
  6.4 0.7 multiply_bitcast_fusion.1
  7.1 0.1 cosine_bitcast_fusion
  7.1 0.1 copy.16
  7.2 0.8 copy.17.refs_9_.refs_1_
  8.0 0.8 copy.18.refs_10_.refs_2_
  8.8 0.5 fusion.4
  9.4 0.1 rev.3
  9.5 0.6 collective-permute-start.2
  10.1 0.1 collective-permute-start.4
  10.3 0.6 pad.4.taps_ref
  10.9 2.5 %filter_matrices.1 = (bf16[10,128,256]{2,1,0:T(8,128)(2,1)}, bf16[10,96,96]{2,1,0:T(8,128)(2,1)}, bf16[10,32,96]{2,1,0:T(8,128)(2,1)}) custom-call(f32[60,256]{1,0:T(8,128)} %pad.4.taps_ref), custom_call_target="tpu_custom_call" | custom-call | bytes 4000000 | tf_op jit(solution)/shard_map/filter_matrices/pallas_call | solution.py:369
  13.4 0.0 copy-start
  13.4 1.1 %copy-done = bf16[10,128,256]{2,1,0:T(8,128)(2,1)S(1)} copy-done((bf16[10,128,256]{2,1,0:T(8,128)(2,1)S(1)}, bf16[10,128,256]{2,1,0:T(8,128)(2,1)}, u32[]{:S(2)}) %copy-start) | copy-done | bytes 655384
  14.4 0.9 copy-done.1
  15.4 0.9 copy-done.2
  16.3 0.9 copy-done.3
  17.2 0.7 copy-done.4
  17.8 35.6 %features_and_first_moments.1 = (f32[9216,128]{1,0:T(8,128)S(1)}, f32[32,128]{1,0:T(8,128)S(1)}) custom-call(bf16[16,24,128]{2,1,0:T(8,128)(2,1)S(1)} %copy-done.2, bf16[16,24,128]{2,1,0:T(8,128)(2,1)S(1)} %collective-permute-done.refs_1_, bf16[16,24,128]{2,1,0:T(8,128)(2,1)S(1)} %collective-permute-done.1.refs_2_, ...), custom_call_target="tpu_custom_call" | custom-call | tf_op jit(solution)/shard_map/features_and_first_moments/pallas_call | solution.py:384
  53.4 4.1 %collective-permute-start.7 = (f32[32,128]{1,0:T(8,128)S(1)}, f32[32,128]{1,0:T(8,128)S(1)}, u32[]{:S(2)}, u32[]{:S(2)}) collective-permute-start(f32[32,128]{1,0:T(8,128)S(1)} %get-tuple-element.17), channel_id=1, source_target_pairs={{0,3},{1,2},{2,1},{3,0},{4,7},{5,6},{6,5},{7,4},{8,11},{9,10},{10,... | collective-permute-start | bytes 49160 | tf_op jit(solution)/shard_map/ppermute | solution.py:336
  57.5 0.2 collective-permute-start.6
  57.8 0.0 collective-permute-start.5
  57.8 1.2 %collective-permute-done.7 = f32[32,128]{1,0:T(8,128)S(1)} collective-permute-done((f32[32,128]{1,0:T(8,128)S(1)}, f32[32,128]{1,0:T(8,128)S(1)}, u32[]{:S(2)}, u32[]{:S(2)}) %collective-permute-start.7) | collective-permute-done | bytes 16416 | tf_op jit(solution)/shard_map/ppermute | solution.py:336
  59.0 2.3 %collective-permute-done.6 = f32[32,128]{1,0:T(8,128)S(1)} collective-permute-done((f32[32,128]{1,0:T(8,128)S(1)}, f32[32,128]{1,0:T(8,128)S(1)}, u32[]{:S(2)}, u32[]{:S(2)}) %collective-permute-start.6) | collective-permute-done | bytes 16416 | tf_op jit(solution)/shard_map/ppermute | solution.py:336
  61.3 1.6 %collective-permute-start.10 = (f32[32,128]{1,0:T(8,128)S(1)}, f32[32,128]{1,0:T(8,128)S(1)}, u32[]{:S(2)}, u32[]{:S(2)}) collective-permute-start(f32[32,128]{1,0:T(8,128)S(1)} %add_add_fusion.3), channel_id=1, source_target_pairs={{0,12},{1,13},{2,14},{3,15},{4,8},{5,9},{6,10},{7,11},{8,4},{9,5},... | collective-permute-start | bytes 49160 | tf_op jit(solution)/shard_map/ppermute | solution.py:336
  62.9 1.5 %collective-permute-start.9 = (f32[32,128]{1,0:T(8,128)S(1)}, f32[32,128]{1,0:T(8,128)S(1)}, u32[]{:S(2)}, u32[]{:S(2)}) collective-permute-start(f32[32,128]{1,0:T(8,128)S(1)} %add_add_fusion.3), channel_id=1, source_target_pairs={{0,8},{1,9},{2,10},{3,11},{4,12},{5,13},{6,14},{7,15},{8,0},{9,1},... | collective-permute-start | bytes 49160 | tf_op jit(solution)/shard_map/ppermute | solution.py:336
  64.4 1.4 %collective-permute-start.8 = (f32[32,128]{1,0:T(8,128)S(1)}, f32[32,128]{1,0:T(8,128)S(1)}, u32[]{:S(2)}, u32[]{:S(2)}) collective-permute-start(f32[32,128]{1,0:T(8,128)S(1)} %add_add_fusion.3), channel_id=1, source_target_pairs={{0,4},{1,5},{2,6},{3,7},{4,0},{5,1},{6,2},{7,3},{8,12},{9,13},{10,... | collective-permute-start | bytes 49160 | tf_op jit(solution)/shard_map/ppermute | solution.py:336
  65.7 1.1 %collective-permute-done.10 = f32[32,128]{1,0:T(8,128)S(1)} collective-permute-done((f32[32,128]{1,0:T(8,128)S(1)}, f32[32,128]{1,0:T(8,128)S(1)}, u32[]{:S(2)}, u32[]{:S(2)}) %collective-permute-start.10) | collective-permute-done | bytes 16416 | tf_op jit(solution)/shard_map/ppermute | solution.py:336
  66.9 0.6 collective-permute-done.9
  67.5 0.6 collective-permute-done.8
  68.1 16.6 %posterior_and_second_moments.1 = (bf16[16,32,24,128]{3,2,1,0:T(8,128)(2,1)}, f32[32,128]{1,0:T(8,128)S(1)}, f32[32,128]{1,0:T(8,128)S(1)}, f32[32,128]{1,0:T(8,128)S(1)}) custom-call(f32[9216,128]{1,0:T(8,128)S(1)} %get-tuple-element.16.refs_0_, f32[32,20]{1,0:T(8,128)S(1)} %copy.17.refs_9_.refs_1_, f32[32,20]{1,0:T(8,128)S(1)} %copy.18.refs_10_.refs_2_, ...), custom_call_target="tpu_custom_call" | custom-call | tf_op jit(solution)/shard_map/posterior_and_second_moments/pallas_call | solution.py:418
  84.7 1.3 %collective-permute-start.12 = (f32[32,128]{1,0:T(8,128)S(1)}, f32[32,128]{1,0:T(8,128)S(1)}, u32[]{:S(2)}, u32[]{:S(2)}) collective-permute-start(f32[32,128]{1,0:T(8,128)S(1)} %get-tuple-element.19), channel_id=1, source_target_pairs={{0,2},{1,3},{2,0},{3,1},{4,6},{5,7},{6,4},{7,5},{8,10},{9,11},{10,... | collective-permute-start | bytes 49160 | tf_op jit(solution)/shard_map/ppermute | solution.py:336
  86.0 0.6 collective-permute-start.11
  86.6 1.3 %collective-permute-done.13 = f32[32,128]{1,0:T(8,128)S(1)} collective-permute-done((f32[32,128]{1,0:T(8,128)S(1)}, f32[32,128]{1,0:T(8,128)S(1)}, u32[]{:S(2)}, u32[]{:S(2)}) %collective-permute-start.13) | collective-permute-done | bytes 16416 | tf_op jit(solution)/shard_map/ppermute | solution.py:336
  87.9 0.6 collective-permute-done.12
  88.5 2.5 %collective-permute-start.16 = (f32[32,128]{1,0:T(8,128)S(1)}, f32[32,128]{1,0:T(8,128)S(1)}, u32[]{:S(2)}, u32[]{:S(2)}) collective-permute-start(f32[32,128]{1,0:T(8,128)S(1)} %add_add_fusion.1), channel_id=1, source_target_pairs={{0,12},{1,13},{2,14},{3,15},{4,8},{5,9},{6,10},{7,11},{8,4},{9,5},... | collective-permute-start | bytes 49160 | tf_op jit(solution)/shard_map/ppermute | solution.py:336
  91.1 0.3 collective-permute-start.15
  91.4 1.6 %collective-permute-start.14 = (f32[32,128]{1,0:T(8,128)S(1)}, f32[32,128]{1,0:T(8,128)S(1)}, u32[]{:S(2)}, u32[]{:S(2)}) collective-permute-start(f32[32,128]{1,0:T(8,128)S(1)} %add_add_fusion.1), channel_id=1, source_target_pairs={{0,4},{1,5},{2,6},{3,7},{4,0},{5,1},{6,2},{7,3},{8,12},{9,13},{10,... | collective-permute-start | bytes 49160 | tf_op jit(solution)/shard_map/ppermute | solution.py:336
  93.0 1.3 %collective-permute-done.16 = f32[32,128]{1,0:T(8,128)S(1)} collective-permute-done((f32[32,128]{1,0:T(8,128)S(1)}, f32[32,128]{1,0:T(8,128)S(1)}, u32[]{:S(2)}, u32[]{:S(2)}) %collective-permute-start.16) | collective-permute-done | bytes 16416 | tf_op jit(solution)/shard_map/ppermute | solution.py:336
  94.3 1.4 %collective-permute-done.15 = f32[32,128]{1,0:T(8,128)S(1)} collective-permute-done((f32[32,128]{1,0:T(8,128)S(1)}, f32[32,128]{1,0:T(8,128)S(1)}, u32[]{:S(2)}, u32[]{:S(2)}) %collective-permute-start.15) | collective-permute-done | bytes 16416 | tf_op jit(solution)/shard_map/ppermute | solution.py:336
  95.7 0.2 slice_reduce_fusion
  95.9 0.5 add_multiply_fusion
  96.4 0.1 fusion.2
  96.5 0.7 copy.22
  97.2 0.7 copy.21
  (25 shorter events, 0.2 us)
Async XLA Ops:
  0.6 8.9 %collective-permute-start.1 = (bf16[16,24,128]{2,1,0:T(8,128)(2,1)}, bf16[16,24,128]{2,1,0:T(8,128)(2,1)S(1)}, u32[]{:S(2)}, u32[]{:S(2)}) collective-permute-start(bf16[16,24,128]{2,1,0:T(8,128)(2,1)} %refs_0_.1), channel_id=1, source_target_pairs={{0,2},{2,0},{4,6},{6,4},{8,10},{10,8},{12,14},{14,12},{1,3},{3,1},... | collective-permute-start | bytes 294920 | tf_op jit(solution)/shard_map/ppermute | solution.py:324
  3.7 9.7 %collective-permute-start = (bf16[16,24,128]{2,1,0:T(8,128)(2,1)}, bf16[16,24,128]{2,1,0:T(8,128)(2,1)S(1)}, u32[]{:S(2)}, u32[]{:S(2)}) collective-permute-start(bf16[16,24,128]{2,1,0:T(8,128)(2,1)} %refs_0_.1), channel_id=1, source_target_pairs={{0,1},{1,0},{2,3},{3,2},{4,5},{5,4},{6,7},{7,6},{8,9},{9,8},{10,11... | collective-permute-start | bytes 294920 | tf_op jit(solution)/shard_map/ppermute | solution.py:324
  3.7 6.5 %collective-permute-start.3 = (bf16[16,24,128]{2,1,0:T(8,128)(2,1)}, bf16[16,24,128]{2,1,0:T(8,128)(2,1)S(1)}, u32[]{:S(2)}, u32[]{:S(2)}) collective-permute-start(bf16[16,24,128]{2,1,0:T(8,128)(2,1)} %refs_0_.1), channel_id=1, source_target_pairs={{2,4},{4,2},{6,8},{8,6},{10,12},{12,10},{3,5},{5,3},{7,9},{9,7},{1... | collective-permute-start | bytes 294920 | tf_op jit(solution)/shard_map/ppermute | solution.py:324
  9.5 3.8 %collective-permute-start.2 = (bf16[16,24,128]{2,1,0:T(8,128)(2,1)S(1)}, bf16[16,24,128]{2,1,0:T(8,128)(2,1)S(1)}, u32[]{:S(2)}, u32[]{:S(2)}) collective-permute-start(bf16[16,24,128]{2,1,0:T(8,128)(2,1)S(1)} %collective-permute-done.1.refs_2_), channel_id=1, source_target_pairs={{0,1},{1,0},{2,3},{3,2},{4,5},{5,4},{6,7},{7,6},{8,9},{9,8},{10,11... | collective-permute-start | bytes 294920 | tf_op jit(solution)/shard_map/ppermute | solution.py:324
  10.1 3.2 %collective-permute-start.4 = (bf16[16,24,128]{2,1,0:T(8,128)(2,1)S(1)}, bf16[16,24,128]{2,1,0:T(8,128)(2,1)S(1)}, u32[]{:S(2)}, u32[]{:S(2)}) collective-permute-start(bf16[16,24,128]{2,1,0:T(8,128)(2,1)S(1)} %collective-permute-done.3.refs_4_), channel_id=1, source_target_pairs={{0,1},{1,0},{2,3},{3,2},{4,5},{5,4},{6,7},{7,6},{8,9},{9,8},{10,11... | collective-permute-start | bytes 294920 | tf_op jit(solution)/shard_map/ppermute | solution.py:324
  13.4 1.1 %copy-start = (bf16[10,128,256]{2,1,0:T(8,128)(2,1)S(1)}, bf16[10,128,256]{2,1,0:T(8,128)(2,1)}, u32[]{:S(2)}) copy-start(bf16[10,128,256]{2,1,0:T(8,128)(2,1)} %get-tuple-element.13.refs_6_) | copy-start | bytes 1966084
  14.4 0.9 copy-start.1
  15.4 0.9 copy-start.2
  16.3 0.9 copy-start.3
  17.2 0.7 copy-start.4
  53.4 5.5 %collective-permute-start.7 = (f32[32,128]{1,0:T(8,128)S(1)}, f32[32,128]{1,0:T(8,128)S(1)}, u32[]{:S(2)}, u32[]{:S(2)}) collective-permute-start(f32[32,128]{1,0:T(8,128)S(1)} %get-tuple-element.17), channel_id=1, source_target_pairs={{0,3},{1,2},{2,1},{3,0},{4,7},{5,6},{6,5},{7,4},{8,11},{9,10},{10,... | collective-permute-start | bytes 49160 | tf_op jit(solution)/shard_map/ppermute | solution.py:336
  57.5 3.7 %collective-permute-start.6 = (f32[32,128]{1,0:T(8,128)S(1)}, f32[32,128]{1,0:T(8,128)S(1)}, u32[]{:S(2)}, u32[]{:S(2)}) collective-permute-start(f32[32,128]{1,0:T(8,128)S(1)} %get-tuple-element.17), channel_id=1, source_target_pairs={{0,2},{1,3},{2,0},{3,1},{4,6},{5,7},{6,4},{7,5},{8,10},{9,11},{10,... | collective-permute-start | bytes 49160 | tf_op jit(solution)/shard_map/ppermute | solution.py:336
  57.8 3.5 %collective-permute-start.5 = (f32[32,128]{1,0:T(8,128)S(1)}, f32[32,128]{1,0:T(8,128)S(1)}, u32[]{:S(2)}, u32[]{:S(2)}) collective-permute-start(f32[32,128]{1,0:T(8,128)S(1)} %get-tuple-element.17), channel_id=1, source_target_pairs={{0,1},{1,0},{2,3},{3,2},{4,5},{5,4},{6,7},{7,6},{8,9},{9,8},{10,11... | collective-permute-start | bytes 49160 | tf_op jit(solution)/shard_map/ppermute | solution.py:336
  61.3 5.6 %collective-permute-start.10 = (f32[32,128]{1,0:T(8,128)S(1)}, f32[32,128]{1,0:T(8,128)S(1)}, u32[]{:S(2)}, u32[]{:S(2)}) collective-permute-start(f32[32,128]{1,0:T(8,128)S(1)} %add_add_fusion.3), channel_id=1, source_target_pairs={{0,12},{1,13},{2,14},{3,15},{4,8},{5,9},{6,10},{7,11},{8,4},{9,5},... | collective-permute-start | bytes 49160 | tf_op jit(solution)/shard_map/ppermute | solution.py:336
  62.9 4.6 %collective-permute-start.9 = (f32[32,128]{1,0:T(8,128)S(1)}, f32[32,128]{1,0:T(8,128)S(1)}, u32[]{:S(2)}, u32[]{:S(2)}) collective-permute-start(f32[32,128]{1,0:T(8,128)S(1)} %add_add_fusion.3), channel_id=1, source_target_pairs={{0,8},{1,9},{2,10},{3,11},{4,12},{5,13},{6,14},{7,15},{8,0},{9,1},... | collective-permute-start | bytes 49160 | tf_op jit(solution)/shard_map/ppermute | solution.py:336
  64.4 3.7 %collective-permute-start.8 = (f32[32,128]{1,0:T(8,128)S(1)}, f32[32,128]{1,0:T(8,128)S(1)}, u32[]{:S(2)}, u32[]{:S(2)}) collective-permute-start(f32[32,128]{1,0:T(8,128)S(1)} %add_add_fusion.3), channel_id=1, source_target_pairs={{0,4},{1,5},{2,6},{3,7},{4,0},{5,1},{6,2},{7,3},{8,12},{9,13},{10,... | collective-permute-start | bytes 49160 | tf_op jit(solution)/shard_map/ppermute | solution.py:336
  84.7 3.2 %collective-permute-start.13 = (f32[32,128]{1,0:T(8,128)S(1)}, f32[32,128]{1,0:T(8,128)S(1)}, u32[]{:S(2)}, u32[]{:S(2)}) collective-permute-start(f32[32,128]{1,0:T(8,128)S(1)} %get-tuple-element.19), channel_id=1, source_target_pairs={{0,3},{1,2},{2,1},{3,0},{4,7},{5,6},{6,5},{7,4},{8,11},{9,10},{10,... | collective-permute-start | bytes 49160 | tf_op jit(solution)/shard_map/ppermute | solution.py:336
  84.7 3.8 %collective-permute-start.12 = (f32[32,128]{1,0:T(8,128)S(1)}, f32[32,128]{1,0:T(8,128)S(1)}, u32[]{:S(2)}, u32[]{:S(2)}) collective-permute-start(f32[32,128]{1,0:T(8,128)S(1)} %get-tuple-element.19), channel_id=1, source_target_pairs={{0,2},{1,3},{2,0},{3,1},{4,6},{5,7},{6,4},{7,5},{8,10},{9,11},{10,... | collective-permute-start | bytes 49160 | tf_op jit(solution)/shard_map/ppermute | solution.py:336
  86.0 2.5 %collective-permute-start.11 = (f32[32,128]{1,0:T(8,128)S(1)}, f32[32,128]{1,0:T(8,128)S(1)}, u32[]{:S(2)}, u32[]{:S(2)}) collective-permute-start(f32[32,128]{1,0:T(8,128)S(1)} %get-tuple-element.19), channel_id=1, source_target_pairs={{0,1},{1,0},{2,3},{3,2},{4,5},{5,4},{6,7},{7,6},{8,9},{9,8},{10,11... | collective-permute-start | bytes 49160 | tf_op jit(solution)/shard_map/ppermute | solution.py:336
  88.5 5.7 %collective-permute-start.16 = (f32[32,128]{1,0:T(8,128)S(1)}, f32[32,128]{1,0:T(8,128)S(1)}, u32[]{:S(2)}, u32[]{:S(2)}) collective-permute-start(f32[32,128]{1,0:T(8,128)S(1)} %add_add_fusion.1), channel_id=1, source_target_pairs={{0,12},{1,13},{2,14},{3,15},{4,8},{5,9},{6,10},{7,11},{8,4},{9,5},... | collective-permute-start | bytes 49160 | tf_op jit(solution)/shard_map/ppermute | solution.py:336
  91.1 4.6 %collective-permute-start.15 = (f32[32,128]{1,0:T(8,128)S(1)}, f32[32,128]{1,0:T(8,128)S(1)}, u32[]{:S(2)}, u32[]{:S(2)}) collective-permute-start(f32[32,128]{1,0:T(8,128)S(1)} %add_add_fusion.1), channel_id=1, source_target_pairs={{0,8},{1,9},{2,10},{3,11},{4,12},{5,13},{6,14},{7,15},{8,0},{9,1},... | collective-permute-start | bytes 49160 | tf_op jit(solution)/shard_map/ppermute | solution.py:336
  91.4 4.3 %collective-permute-start.14 = (f32[32,128]{1,0:T(8,128)S(1)}, f32[32,128]{1,0:T(8,128)S(1)}, u32[]{:S(2)}, u32[]{:S(2)}) collective-permute-start(f32[32,128]{1,0:T(8,128)S(1)} %add_add_fusion.1), channel_id=1, source_target_pairs={{0,4},{1,5},{2,6},{3,7},{4,0},{5,1},{6,2},{7,3},{8,12},{9,13},{10,... | collective-permute-start | bytes 49160 | tf_op jit(solution)/shard_map/ppermute | solution.py:336

commit v2 on v1

v2 whole, which is shorter than its diff:
```python
import functools
import math

import jax
import jax.numpy as jnp
from jax import lax
from jax.experimental import pallas as pl
from jax.experimental.pallas import tpu as pltpu
from jax.sharding import PartitionSpec as P

TAPS = 31
HALF = 15
AZIMUTHS = 8
DIPS = 4
LANES = 128
SUBLANES = 8

eps_mag = 0.01
wavenumber = math.pi / 4.0


def round_up(value, step):
    return (value + step - 1) // step * step


def split(values, count):
    pieces = []
    for _ in range(count):
        pieces.append(values.astype(jnp.bfloat16))
        values = values - pieces[-1].astype(jnp.float32)
    return pieces


def tap_lines(directions_ref, orients):
    shape = (round_up(orients, SUBLANES), LANES)
    rows = lax.broadcasted_iota(jnp.int32, shape, 0)
    lanes = lax.broadcasted_iota(jnp.int32, shape, 1)
    direction = jnp.zeros(shape, jnp.int32)
    for orient in range(orients):
        direction = jnp.where(rows == orient, directions_ref[orient], direction)
    azimuth = lax.rem(direction, AZIMUTHS).astype(jnp.float32) * (math.pi / AZIMUTHS)
    dip_angle = (lax.div(direction, AZIMUTHS) + 1).astype(jnp.float32) * (math.pi / (2 * DIPS + 2))
    offsets = lanes.astype(jnp.float32) - HALF
    used = lanes < TAPS
    width_scale = HALF / 3.0
    envelope = jnp.exp(-offsets * offsets / (2.0 * width_scale * width_scale))
    envelope = jnp.where(used, envelope, 0.0)
    envelope = envelope / jnp.sqrt(jnp.sum(envelope * envelope, axis=1, keepdims=True))
    sine = jnp.sin(dip_angle)
    lines = []
    for wave, sign in (
        (wavenumber * (sine * jnp.cos(azimuth)), 1.0),
        (wavenumber * (sine * jnp.sin(azimuth)), 1.0),
        (wavenumber * jnp.cos(dip_angle), -1.0),
    ):
        phase = wave * (offsets * sign)
        pair = (envelope * jnp.cos(phase), envelope * jnp.sin(phase))
        lines.append([part.astype(jnp.bfloat16).astype(jnp.float32) for part in pair])
    return lines


def matrices_kernel(dims, directions_ref, time_ref, xline_ref, inline_ref):
    orients, samples, cols, rows, window = dims
    side = lax.axis_index("xline")
    lanes = lax.broadcasted_iota(jnp.int32, (SUBLANES, LANES), 1)[:1]
    lines = tap_lines(directions_ref, orients)

    def sheared(line, count, shift, width):
        if width > LANES:
            line = jnp.concatenate([line, jnp.zeros((1, width - LANES), jnp.float32)], axis=1)
        wide = jnp.broadcast_to(line, (count, width))
        return pltpu.roll(wide, shift % width, 1, stride=1, stride_axis=0)

    for orient in range(orients):
        line = lambda axis, part: lines[axis][part][orient : orient + 1]
        for part in range(2):
            time_ref[orient, :, part * samples : (part + 1) * samples] = sheared(
                line(2, part), samples, 2 * samples - HALF, 2 * samples
            )[:, :samples].astype(jnp.bfloat16)

        def xline_half(part, half, slot):
            shift = LANES - HALF + slot * cols
            if half:
                moved = jnp.where(
                    side == 0,
                    sheared(line(1, part), cols, shift + LANES - cols, LANES),
                    sheared(line(1, part), cols, shift + cols, LANES),
                )
            else:
                moved = sheared(line(1, part), cols, shift, LANES)
            return jnp.where((lanes >= slot * cols) & (lanes < (slot + 1) * cols), moved, 0.0)

        cosine = [xline_half(0, 0, p * 2) + xline_half(0, 1, p * 2 + 1) for p in range(2)]
        sine = [xline_half(1, 0, p * 2) + xline_half(1, 1, p * 2 + 1) for p in range(2)]
        xline_ref[orient] = jnp.concatenate(
            [
                cosine[0] - sine[1],
                sine[0] + cosine[1],
                cosine[0] + sine[1],
                sine[0] - cosine[1],
            ],
            axis=0,
        )[:, : 4 * cols].astype(jnp.bfloat16)

        def inline_part(part, slot):
            moved = sheared(line(0, part), rows, slot * window, LANES)
            return jnp.where((lanes >= slot * window) & (lanes < (slot + 1) * window), moved, 0.0)

        inline_ref[orient] = jnp.concatenate(
            [
                inline_part(0, 0) - inline_part(1, 1),
                inline_part(1, 0) + inline_part(0, 1),
            ],
            axis=0,
        )[:, : 2 * window].astype(jnp.bfloat16)


def score_matrix(centers, spreads, log_weights, feats, slot, levels):
    lanes = lax.broadcasted_iota(jnp.int32, centers.shape, 1)
    real = lanes < feats
    inverse = 1.0 / spreads
    widen = lambda values, count: [p.astype(jnp.float32) for p in split(values, count)]
    linear = widen(centers * inverse, levels)
    square = widen(-0.5 * inverse, levels)
    kept_linear, kept_square = sum(linear), sum(square)
    terms = jnp.log(2.0 * math.pi * spreads) - 0.5 * kept_linear * (kept_linear / kept_square)
    constant = log_weights - 0.5 * jnp.sum(jnp.where(real, terms, 0.0), axis=1, keepdims=True)
    constants = widen(constant, 3)
    groups = []
    for level in range(levels):
        first = jnp.where(real, linear[level], 0.0)
        first = jnp.where(lanes == feats, constants[level], first)
        if level == 0 and levels == 2:
            first = jnp.where(lanes == feats + 1, constants[2], first)
        both = first + pltpu.roll(jnp.where(real, square[level], 0.0), slot, 1)
        both = jnp.concatenate([both, jnp.zeros_like(both)], axis=1)
        groups.append(both + pltpu.roll(both, 2 * slot, 1) + pltpu.roll(both, 4 * slot, 1))
    return jnp.concatenate(groups, axis=0)[:, : 6 * slot].astype(jnp.bfloat16)


def score_stage(features, matrix, data_ref, scores_ref, place, components):
    both = jnp.concatenate([features, features * features], axis=0)
    data = jnp.concatenate(split(both, 3), axis=0)
    data_ref[:, place] = data[: data_ref.shape[0]]
    scores = jnp.dot(matrix, data, preferred_element_type=jnp.float32)
    scores_ref[:, place] = sum(
        scores[k : k + components] for k in range(0, matrix.shape[0], components)
    )


def moment_stage(data_ref, scores_ref, place):
    scores = scores_ref[:, place]
    exponent = jnp.exp(scores - jnp.max(scores, axis=0, keepdims=True))
    shares = exponent * (1.0 / jnp.sum(exponent, axis=0, keepdims=True))
    high = shares.astype(jnp.bfloat16)
    low = (shares - high.astype(jnp.float32)).astype(jnp.bfloat16)
    sums = lax.dot_general(
        data_ref[:, place],
        jnp.concatenate([high, low], axis=0),
        (((1,), (1,)), ((), ())),
        preferred_element_type=jnp.float32,
    )
    return shares, sums


def gathered(features_ref, row, rows, first, count, slot):
    place = lambda col: (col * rows + row) * (slot + 1)
    return jnp.concatenate(
        [features_ref[pl.ds(place(first + k), slot), :] for k in range(count)], axis=1
    )


def fold_sums(total, components, slot):
    both = total[:, :components] + total[:, components:]
    both = both[: 2 * slot] + both[2 * slot :]
    return jnp.concatenate(
        [both, jnp.zeros((LANES - 2 * slot, components), jnp.float32)], axis=0
    ).T


def features_kernel(dims, *refs):
    orients, samples, cols, rows, window, components, chunk, unit = dims
    halves, refs = refs[:6], refs[6:]
    time_ref, xline_ref, inline_ref, means_ref, variances_ref, weights_ref = refs[:6]
    features_ref, sums_ref, traces, across, params, total, data, scores, own, arrived = refs[6:]
    feats = 2 * orients
    slot = round_up(feats + 2, SUBLANES)
    orient = pl.program_id(0)
    @pl.when(orient == 0)
    def _():
        own_copy = pltpu.make_async_copy(halves[0], own, arrived)
        own_copy.start()
        own_copy.wait()
        other, swap_one, swap_one_other, swap_two, swap_two_other = halves[1:]
        even = lax.rem(lax.axis_index("inline"), 2) == 0

        def put(place, near, far):
            traces[pl.ds(place * 2 * cols, 2 * cols), :] = jnp.concatenate(
                [near.astype(jnp.float32), far.astype(jnp.float32)], axis=0
            ).astype(jnp.bfloat16)

        for row in range(rows):
            put(HALF + row, own[row], other[row])
            one = swap_one[row].astype(jnp.float32)
            one_far = swap_one_other[row].astype(jnp.float32)
            two = swap_two[row].astype(jnp.float32)
            two_far = swap_two_other[row].astype(jnp.float32)
            if row >= rows - HALF:
                put(row - (rows - HALF), jnp.where(even, two, one), jnp.where(even, two_far, one_far))
            if row < HALF:
                put(HALF + rows + row, jnp.where(even, one, two), jnp.where(even, one_far, two_far))
        for place in range(rows + 2 * HALF, window):
            traces[pl.ds(place * 2 * cols, 2 * cols), :] = jnp.zeros(
                (2 * cols, samples), jnp.bfloat16
            )
        for extra in range(feats, slot):
            filler = jnp.full((rows, samples), 1.0 if extra < feats + 2 else 0.0, jnp.float32)
            for col in range(cols):
                place = col * rows * (slot + 1) + extra
                features_ref[pl.ds(place, rows, stride=slot + 1), :] = filler

    lines = 2 * cols
    apart = window + 1
    group = window
    for pair in range(window // 2):
        if pair * 2 % group == 0:
            block = traces[pl.ds(pair * 2 * lines, group * lines), :]
            band = jnp.dot(block, time_ref[0], preferred_element_type=jnp.float32)
            band = band.astype(jnp.bfloat16)

        def piece(k, p):
            first = (pair * 2 % group + k) * lines
            return band[first : first + lines, p * samples : (p + 1) * samples]

        stacked = jnp.concatenate(
            [jnp.concatenate([piece(k, 0), piece(k, 1)], axis=0) for k in range(2)], axis=1
        )
        crossed = jnp.dot(xline_ref[0], stacked, preferred_element_type=jnp.float32)
        for k in range(2):
            across[pl.ds(2 * pair + k, 4 * cols, stride=apart), :] = crossed[
                :, k * samples : (k + 1) * samples
            ]
    for polarity in range(2):
        for col in range(0, cols, 2):

            def taken(k, part):
                place = ((polarity * 2 + part) * cols + col + k) * apart
                return across[pl.ds(place, window), :]

            stacked = jnp.concatenate(
                [jnp.concatenate([taken(k, 0), taken(k, 1)], axis=0) for k in range(2)], axis=1
            ).astype(jnp.bfloat16)
            found = jnp.dot(inline_ref[0], stacked, preferred_element_type=jnp.float32)
            real_part, imag_part = found[:rows], found[rows:]
            power = real_part * real_part + imag_part * imag_part + eps_mag
            size = power * lax.rsqrt(power)
            for k in range(2):
                place = (col + k) * rows * (slot + 1) + 2 * orient + polarity
                features_ref[pl.ds(place, rows, stride=slot + 1), :] = size[
                    :, k * samples : (k + 1) * samples
                ]

    @pl.when(orient == orients - 1)
    def _():
        params[...] = jnp.ones(params.shape, jnp.float32)
        params[:components, :feats] = means_ref[...]
        params[components:, :feats] = variances_ref[...]
        row_ids = lax.broadcasted_iota(jnp.int32, (components, 1), 0)
        weights = jnp.ones((components, 1), jnp.float32)
        for component in range(components):
            weights = jnp.where(row_ids == component, weights_ref[component], weights)
        log_weights = jnp.log(weights)
        matrix = score_matrix(
            params[:components], params[components:], log_weights, feats, slot, 3
        )
        total[...] = jnp.zeros(total.shape, jnp.float32)

        data[...] = jnp.zeros(data.shape, jnp.bfloat16)
        scores[...] = jnp.zeros(scores.shape, jnp.float32)

        @pl.loop(0, rows // unit + 1)
        def _(step):
            block = jnp.minimum(step, rows // unit - 1)
            partial = jnp.zeros(total.shape, jnp.float32)
            for start in range(0, unit * cols, chunk):
                place = slice(start * samples, (start + chunk) * samples)
                partial = partial + moment_stage(data, scores, place)[1]
                lines = gathered(features_ref, block * unit + start // cols, rows, start % cols, chunk, slot)
                score_stage(lines, matrix, data, scores, place, components)
            total[...] += partial

        sums_ref[...] = fold_sums(total[...], components, slot)


def new_params(sums, centers, spreads, feats, slot, cells):
    components = centers.shape[0]
    mass = sums[:, feats : feats + 1]
    first = sums
    second = pltpu.roll(sums, LANES - slot, 1)
    scale = 1.0 / (mass + 1.0)
    moved = (first + centers) * scale
    centred = second - 2.0 * moved * first + moved * moved * mass
    return moved, (centred + spreads) * scale, (mass + 1.0) / (cells + components)


def posterior_kernel(dims, *refs):
    orients, samples, cols, rows, components, chunk, unit, cells = dims
    features_ref, means_ref, variances_ref, before_ref = refs[:4]
    posterior_ref, sums_ref, centers_ref, spreads_ref, matrix, total, turned, data, scores = refs[4:]
    feats = 2 * orients
    slot = round_up(feats + 2, SUBLANES)
    step = pl.program_id(0)
    block = jnp.minimum(step, rows // unit - 1)

    @pl.when(step == 0)
    def _():
        centers_ref[...] = jnp.zeros(centers_ref.shape, jnp.float32)
        spreads_ref[...] = jnp.ones(spreads_ref.shape, jnp.float32)
        centers_ref[:, :feats] = means_ref[...]
        spreads_ref[:, :feats] = variances_ref[...]
        centers, spreads, weights = new_params(
            before_ref[...], centers_ref[...], spreads_ref[...], feats, slot, cells
        )
        lanes = lax.broadcasted_iota(jnp.int32, centers.shape, 1)
        centers = jnp.where(lanes < feats, centers, 0.0)
        spreads = jnp.where(lanes < feats, spreads, 1.0)
        centers_ref[...] = centers
        spreads_ref[...] = spreads
        matrix[...] = score_matrix(centers, spreads, jnp.log(weights), feats, slot, 2)
        total[...] = jnp.zeros(total.shape, jnp.float32)
        data[...] = jnp.zeros(data.shape, jnp.bfloat16)
        scores[...] = jnp.zeros(scores.shape, jnp.float32)

    partial = jnp.zeros(total.shape, jnp.float32)
    for start in range(0, unit * cols, chunk):
        place = slice(start * samples, (start + chunk) * samples)
        which, col = start // cols, start % cols
        shares, sums = moment_stage(data, scores, place)
        lines = gathered(features_ref, block * unit + which, rows, col, chunk, slot)
        score_stage(lines, matrix[...], data, scores, place, components)
        partial = partial + sums
        for k in range(chunk):
            turned[which, pl.ds(col + k, components, stride=cols + 1), :] = shares[
                :, k * samples : (k + 1) * samples
            ]
    total[...] += partial
    for which in range(unit):
        for component in range(components):
            posterior_ref[which, component] = turned[
                which, pl.ds(component * (cols + 1), cols), :
            ].astype(jnp.bfloat16)

    @pl.when(step == pl.num_programs(0) - 1)
    def _():
        sums_ref[...] = fold_sums(total[...], components, slot)


def exchange(values, axis, pairs):
    return lax.ppermute(values, axis, [p for a, b in pairs for p in ((a, b), (b, a))])


def group_sum(values):
    axes = ("inline", "xline")
    count = lax.axis_size("inline") * lax.axis_size("xline")
    if count & (count - 1):
        return lax.psum(values, axes)
    step = 1
    while step < count:
        radix = min(4, count // step)
        arrived = [
            lax.ppermute(values, axes, [(i, i ^ (step * d)) for i in range(count)])
            for d in range(1, radix)
        ]
        if radix == 4:
            values = (values + arrived[0]) + (arrived[1] + arrived[2])
        else:
            values = values + arrived[0]
        step *= radix
    return values


def per_device(traces, directions, init_means, init_variances, init_weights):
    rows, cols, samples = traces.shape
    orients = directions.shape[0]
    components = init_weights.shape[0]
    feats = 2 * orients
    slot = round_up(feats + 2, SUBLANES)
    window = round_up(rows + 2 * HALF, 16)
    inlines = lax.axis_size("inline")
    if lax.axis_size("xline") != 2 or samples != LANES or rows < HALF:
        raise ValueError("unsupported sizes")

    core_pairs = [(0, 1)]
    other = exchange(traces, "xline", core_pairs)
    swap_one = exchange(traces, "inline", [(i, i + 1) for i in range(0, inlines - 1, 2)])
    swap_two = exchange(traces, "inline", [(i, i + 1) for i in range(1, inlines - 1, 2)])
    vmem = pl.BlockSpec(memory_space=pltpu.VMEM)
    time_mats, xline_mats, inline_mats = pl.pallas_call(
        functools.partial(matrices_kernel, (orients, samples, cols, rows, window)),
        out_shape=(
            jax.ShapeDtypeStruct((orients, samples, 2 * samples), jnp.bfloat16),
            jax.ShapeDtypeStruct((orients, 4 * cols, 4 * cols), jnp.bfloat16),
            jax.ShapeDtypeStruct((orients, 2 * rows, 2 * window), jnp.bfloat16),
        ),
        in_specs=[pl.BlockSpec(memory_space=pltpu.SMEM)],
        out_specs=(vmem, vmem, vmem),
        compiler_params=pltpu.CompilerParams(vmem_limit_bytes=8 * 2**20),
        name="filter_matrices",
        cost_estimate=pl.CostEstimate(flops=0, bytes_accessed=4_000_000, transcendentals=0),
    )(directions)

    swap_one, swap_two, time_mats, xline_mats, inline_mats = lax.optimization_barrier(
        (swap_one, swap_two, time_mats, xline_mats, inline_mats)
    )
    swap_one_other = exchange(swap_one, "xline", core_pairs)
    swap_two_other = exchange(swap_two, "xline", core_pairs)

    whole = lambda *shape: pl.BlockSpec(shape, lambda o: (0,) * len(shape))
    chunk = 6
    unit = 2 if rows % 2 == 0 else 1
    features, sums = pl.pallas_call(
        functools.partial(
            features_kernel, (orients, samples, cols, rows, window, components, chunk, unit)
        ),
        grid=(orients,),
        out_shape=(
            jax.ShapeDtypeStruct((rows * cols * (slot + 1), samples), jnp.float32),
            jax.ShapeDtypeStruct((components, LANES), jnp.float32),
        ),
        in_specs=[pl.BlockSpec(memory_space=pltpu.HBM)]
        + [whole(rows, cols, samples)] * 5
        + [
            pl.BlockSpec((1, samples, 2 * samples), lambda o: (o, 0, 0)),
            pl.BlockSpec((1, 4 * cols, 4 * cols), lambda o: (o, 0, 0)),
            pl.BlockSpec((1, 2 * rows, 2 * window), lambda o: (o, 0, 0)),
            whole(components, feats),
            whole(components, feats),
            pl.BlockSpec(memory_space=pltpu.SMEM),
        ],
        out_specs=(whole(rows * cols * (slot + 1), samples), whole(components, LANES)),
        scratch_shapes=[
            pltpu.VMEM((window * 2 * cols, samples), jnp.bfloat16),
            pltpu.VMEM((4 * cols * (window + 1), samples), jnp.float32),
            pltpu.VMEM((2 * components, LANES), jnp.float32),
            pltpu.VMEM((4 * slot, 2 * components), jnp.float32),
            pltpu.VMEM((4 * slot, unit * cols * samples), jnp.bfloat16),
            pltpu.VMEM((components, unit * cols * samples), jnp.float32),
            pltpu.VMEM((rows, cols, samples), jnp.bfloat16),
            pltpu.SemaphoreType.DMA,
        ],
        compiler_params=pltpu.CompilerParams(vmem_limit_bytes=40 * 2**20),
        name="features_and_first_moments",
    )(
        traces, other, swap_one, swap_one_other, swap_two, swap_two_other,
        time_mats, xline_mats, inline_mats,
        init_means, init_variances, init_weights,
    )
    sums = group_sum(sums)
    cells = inlines * rows * lax.axis_size("xline") * cols * samples
    posterior, sums, centers, spreads = pl.pallas_call(
        functools.partial(
            posterior_kernel, (orients, samples, cols, rows, components, chunk, unit, cells)
        ),
        grid=(rows // unit + 1,),
        out_shape=(
            jax.ShapeDtypeStruct((rows, components, cols, samples), jnp.bfloat16),
            jax.ShapeDtypeStruct((components, LANES), jnp.float32),
            jax.ShapeDtypeStruct((components, LANES), jnp.float32),
            jax.ShapeDtypeStruct((components, LANES), jnp.float32),
        ),
        in_specs=[
            whole(rows * cols * (slot + 1), samples),
            whole(components, feats),
            whole(components, feats),
            whole(components, LANES),
        ],
        out_specs=(
            pl.BlockSpec((unit, components, cols, samples), lambda r: (jnp.maximum(r - 1, 0), 0, 0, 0)),
            whole(components, LANES),
            whole(components, LANES),
            whole(components, LANES),
        ),
        scratch_shapes=[
            pltpu.VMEM((2 * components, 6 * slot), jnp.bfloat16),
            pltpu.VMEM((4 * slot, 2 * components), jnp.float32),
            pltpu.VMEM((unit, components * (cols + 1), samples), jnp.float32),
            pltpu.VMEM((4 * slot, unit * cols * samples), jnp.bfloat16),
            pltpu.VMEM((components, unit * cols * samples), jnp.float32),
        ],
        compiler_params=pltpu.CompilerParams(vmem_limit_bytes=40 * 2**20),
        name="posterior_and_second_moments",
    )(features, init_means, init_variances, sums)
    sums = group_sum(sums)
    mass = sums[:, feats : feats + 1]
    first = sums[:, :feats]
    second = sums[:, slot : slot + feats]
    centers, spreads = centers[:, :feats], spreads[:, :feats]
    moved = (first + centers) / (mass + 1.0)
    centred = second - 2.0 * moved * first + moved * moved * mass
    final_spreads = (centred + spreads) / (mass + 1.0)
    return posterior, moved, final_spreads, (mass[:, 0] + 1.0) / (cells + components)


def solution(mesh):
    in_specs = (P(("slab", "inline"), "xline", None), P(), P(), P(), P())
    out_specs = (
        P(("slab", "inline"), None, "xline", None),
        P("slab", None),
        P("slab", None),
        P("slab"),
    )
    return jax.shard_map(
        per_device, mesh=mesh, in_specs=in_specs, out_specs=out_specs, check_vma=False
    )
```

time: 98.3 us -> 71.7 us (0.73)
  Pallas kernels: 54.6 us -> 33.2 us
  local copies, waits for them, and re-layouts: 8.23 us -> 5.11 us
  other arithmetic: 3.52 us -> 0.81 us
    pallas_call x1, Pallas kernels: 35.6 us -> 21.4 us  [per_device(): pl.pallas_call(functools.partial(features_kernel, (orients, samples, cols...]
    pallas_call x1, Pallas kernels: 16.6 us -> 10.5 us  [per_device(): pl.pallas_call(functools.partial(posterior_kernel, (orients, samples, col...]
    unnamed x14 -> x10, local copies, waits for them, and re-layouts: 7.38 us -> 5.11 us
    another operation x3 -> x0, other arithmetic: 1.28 us -> none  [the longest x2 0.76 us: tap_table(): jnp.stack([jnp.sin(dip_angle) * jnp.cos(azimuth), jnp.sin(dip_angle) * jn...]
    pallas_call x1, Pallas kernels: 2.45 us -> 1.27 us  [per_device(): pl.pallas_call(functools.partial(matrices_kernel, (orients, samples, cols...]
  transfers between devices with their start and end apart: 17 -> 17, of which waited for: 9 -> 10; matrix products, arithmetic and copies ran while one was open for 5% -> 2% of each run, Pallas kernels for 3% -> 2%
where the time goes in v2:
time: 71.7 us; the launch traced here: 71.3 us
  Pallas kernels  33.2 us (46%)
  starting transfers between devices  20.2 us (28%)
  waiting for transfers between devices  11.4 us (16%)
  local copies, waits for them, and re-layouts  5.11 us (7%)
  other arithmetic  0.81 us (1%)
  between operations  0.72 us (1%)
    pallas_call x1, Pallas kernels, per_device(): pl.pallas_call(functools.partial(features_kernel, (orients, samples, cols...  21.4 us
    ppermute x12, starting transfers between devices, group_sum(): lax.ppermute(values, axes, [(i, i ^ step * d) for i in range(count)])  15.9 us
    ppermute x12, waiting for transfers between devices, group_sum(): lax.ppermute(values, axes, [(i, i ^ step * d) for i in range(count)])  11 us
    pallas_call x1, Pallas kernels, per_device(): pl.pallas_call(functools.partial(posterior_kernel, (orients, samples, col...  10.5 us
    unnamed x10, local copies, waits for them, and re-layouts  5.11 us
    ppermute x5, starting transfers between devices, exchange(): lax.ppermute(values, axis, [p for a, b in pairs for p in ((a, b), (b, a))])  4.27 us
  transfers between devices with their start and end apart: 17, of which 10 were waited for; matrix products, arithmetic and copies ran while one was open for 2% of the time, Pallas kernels for 2%

profile of v2, /device:TPU:0, one launch (start us, length us, event | category | flops | bytes accessed | tf_op | source)
XLA Modules:
  0.0 71.3 jit_solution(3852301158574884970)
XLA Ops:
  0.6 3.0 %collective-permute-start.1 = (bf16[16,24,128]{2,1,0:T(8,128)(2,1)}, bf16[16,24,128]{2,1,0:T(8,128)(2,1)S(1)}, u32[]{:S(2)}, u32[]{:S(2)}) collective-permute-start(bf16[16,24,128]{2,1,0:T(8,128)(2,1)} %refs_0_.1), channel_id=1, source_target_pairs={{0,2},{2,0},{4,6},{6,4},{8,10},{10,8},{12,14},{14,12},{1,3},{3,1},... | collective-permute-start | bytes 294920 | tf_op jit(solution)/shard_map/ppermute | solution.py:359
  3.7 0.7 collective-permute-start.2
  4.3 0.1 collective-permute-start
  4.4 0.6 copy-done.2
  5.1 1.3 %filter_matrices.1 = (bf16[10,128,256]{2,1,0:T(8,128)(2,1)S(1)}, bf16[10,96,96]{2,1,0:T(8,128)(2,1)S(1)}, bf16[10,32,96]{2,1,0:T(8,128)(2,1)S(1)}) custom-call(s32[10]{0:T(128)S(1)} %copy-done.2), custom_call_target="tpu_custom_call" | custom-call | bytes 4000000 | tf_op jit(solution)/shard_map/filter_matrices/pallas_call | solution.py:398
  6.3 0.3 collective-permute-done.1.refs_2_
  6.7 0.0 collective-permute-done.2.refs_4_
  6.7 0.2 collective-permute-start.3
  6.9 0.3 collective-permute-start.4
  7.2 0.8 %copy.15.refs_9_.refs_1_ = f32[32,20]{1,0:T(8,128)S(1)} copy(f32[32,20]{0,1:T(8,128)} %param.7) | data formatting | bytes 5120 | tf_op args[2]
  8.0 0.8 %copy.16.refs_10_.refs_2_ = f32[32,20]{1,0:T(8,128)S(1)} copy(f32[32,20]{0,1:T(8,128)} %param.8) | data formatting | bytes 5120 | tf_op args[3]
  8.8 0.0 collective-permute-done.refs_1_
  8.8 0.0 collective-permute-done.3.refs_3_
  8.8 0.0 collective-permute-done.4.refs_5_
  8.8 0.0 copy-start
  8.8 0.9 %copy-done = bf16[16,24,128]{2,1,0:T(8,128)(2,1)S(1)} copy-done((bf16[16,24,128]{2,1,0:T(8,128)(2,1)S(1)}, bf16[16,24,128]{2,1,0:T(8,128)(2,1)}, u32[]{:S(2)}) %copy-start) | copy-done | bytes 98328
  9.7 0.7 copy-done.1
  10.3 21.4 %features_and_first_moments.1 = (f32[9600,128]{1,0:T(8,128)S(1)}, f32[32,128]{1,0:T(8,128)S(1)}) custom-call(bf16[16,24,128]{2,1,0:T(8,128)(2,1)S(1)} %copy-done, bf16[16,24,128]{2,1,0:T(8,128)(2,1)S(1)} %collective-permute-done.refs_1_, bf16[16,24,128]{2,1,0:T(8,128)(2,1)S(1)} %collective-permute-done.1.refs_2_, ...), custom_call_target="tpu_custom_call" | custom-call | tf_op jit(solution)/shard_map/features_and_first_moments/pallas_call | solution.py:421
  31.7 4.4 %collective-permute-start.7 = (f32[32,128]{1,0:T(8,128)S(1)}, f32[32,128]{1,0:T(8,128)S(1)}, u32[]{:S(2)}, u32[]{:S(2)}) collective-permute-start(f32[32,128]{1,0:T(8,128)S(1)} %get-tuple-element.27), channel_id=1, source_target_pairs={{0,3},{1,2},{2,1},{3,0},{4,7},{5,6},{6,5},{7,4},{8,11},{9,10},{10,... | collective-permute-start | bytes 49160 | tf_op jit(solution)/shard_map/ppermute | solution.py:371
  36.1 0.5 collective-permute-start.6
  36.6 0.0 collective-permute-start.5
  36.6 0.9 %collective-permute-done.7 = f32[32,128]{1,0:T(8,128)S(1)} collective-permute-done((f32[32,128]{1,0:T(8,128)S(1)}, f32[32,128]{1,0:T(8,128)S(1)}, u32[]{:S(2)}, u32[]{:S(2)}) %collective-permute-start.7) | collective-permute-done | bytes 16416 | tf_op jit(solution)/shard_map/ppermute | solution.py:371
  37.6 2.3 %collective-permute-done.6 = f32[32,128]{1,0:T(8,128)S(1)} collective-permute-done((f32[32,128]{1,0:T(8,128)S(1)}, f32[32,128]{1,0:T(8,128)S(1)}, u32[]{:S(2)}, u32[]{:S(2)}) %collective-permute-start.6) | collective-permute-done | bytes 16416 | tf_op jit(solution)/shard_map/ppermute | solution.py:371
  39.8 0.0 collective-permute-done.5
  39.9 4.0 %collective-permute-start.10 = (f32[32,128]{1,0:T(8,128)S(1)}, f32[32,128]{1,0:T(8,128)S(1)}, u32[]{:S(2)}, u32[]{:S(2)}) collective-permute-start(f32[32,128]{1,0:T(8,128)S(1)} %add_add_fusion.3), channel_id=1, source_target_pairs={{0,12},{1,13},{2,14},{3,15},{4,8},{5,9},{6,10},{7,11},{8,4},{9,5},... | collective-permute-start | bytes 49160 | tf_op jit(solution)/shard_map/ppermute | solution.py:371
  43.9 0.0 collective-permute-start.9
  43.9 0.6 collective-permute-start.8
  44.5 1.1 %collective-permute-done.10 = f32[32,128]{1,0:T(8,128)S(1)} collective-permute-done((f32[32,128]{1,0:T(8,128)S(1)}, f32[32,128]{1,0:T(8,128)S(1)}, u32[]{:S(2)}, u32[]{:S(2)}) %collective-permute-start.10) | collective-permute-done | bytes 16416 | tf_op jit(solution)/shard_map/ppermute | solution.py:371
  45.6 2.9 %collective-permute-done.9 = f32[32,128]{1,0:T(8,128)S(1)} collective-permute-done((f32[32,128]{1,0:T(8,128)S(1)}, f32[32,128]{1,0:T(8,128)S(1)}, u32[]{:S(2)}, u32[]{:S(2)}) %collective-permute-start.9) | collective-permute-done | bytes 16416 | tf_op jit(solution)/shard_map/ppermute | solution.py:371
  48.5 0.0 collective-permute-done.8
  48.5 10.5 %posterior_and_second_moments.1 = (bf16[16,32,24,128]{3,2,1,0:T(8,128)(2,1)}, f32[32,128]{1,0:T(8,128)S(1)}, f32[32,128]{1,0:T(8,128)S(1)}, f32[32,128]{1,0:T(8,128)S(1)}) custom-call(f32[9600,128]{1,0:T(8,128)S(1)} %get-tuple-element.26.refs_0_, f32[32,20]{1,0:T(8,128)S(1)} %copy.15.refs_9_.refs_1_, f32[32,20]{1,0:T(8,128)S(1)} %copy.16.refs_10_.refs_2_, ...), custom_call_target="tpu_custom_call" | custom-call | tf_op jit(solution)/shard_map/posterior_and_second_moments/pallas_call | solution.py:460
  59.0 0.0 collective-permute-start.13
  59.0 1.6 %collective-permute-start.12 = (f32[32,128]{1,0:T(8,128)S(1)}, f32[32,128]{1,0:T(8,128)S(1)}, u32[]{:S(2)}, u32[]{:S(2)}) collective-permute-start(f32[32,128]{1,0:T(8,128)S(1)} %get-tuple-element.29), channel_id=1, source_target_pairs={{0,2},{1,3},{2,0},{3,1},{4,6},{5,7},{6,4},{7,5},{8,10},{9,11},{10,... | collective-permute-start | bytes 49160 | tf_op jit(solution)/shard_map/ppermute | solution.py:371
  60.6 0.3 collective-permute-start.11
  60.9 1.4 %collective-permute-done.13 = f32[32,128]{1,0:T(8,128)S(1)} collective-permute-done((f32[32,128]{1,0:T(8,128)S(1)}, f32[32,128]{1,0:T(8,128)S(1)}, u32[]{:S(2)}, u32[]{:S(2)}) %collective-permute-start.13) | collective-permute-done | bytes 16416 | tf_op jit(solution)/shard_map/ppermute | solution.py:371
  62.3 0.5 collective-permute-done.12
  62.8 0.0 collective-permute-done.11
  62.8 1.5 %collective-permute-start.16 = (f32[32,128]{1,0:T(8,128)S(1)}, f32[32,128]{1,0:T(8,128)S(1)}, u32[]{:S(2)}, u32[]{:S(2)}) collective-permute-start(f32[32,128]{1,0:T(8,128)S(1)} %add_add_fusion.1), channel_id=1, source_target_pairs={{0,12},{1,13},{2,14},{3,15},{4,8},{5,9},{6,10},{7,11},{8,4},{9,5},... | collective-permute-start | bytes 49160 | tf_op jit(solution)/shard_map/ppermute | solution.py:371
  64.4 0.6 collective-permute-start.15
  65.0 2.3 %collective-permute-start.14 = (f32[32,128]{1,0:T(8,128)S(1)}, f32[32,128]{1,0:T(8,128)S(1)}, u32[]{:S(2)}, u32[]{:S(2)}) collective-permute-start(f32[32,128]{1,0:T(8,128)S(1)} %add_add_fusion.1), channel_id=1, source_target_pairs={{0,4},{1,5},{2,6},{3,7},{4,0},{5,1},{6,2},{7,3},{8,12},{9,13},{10,... | collective-permute-start | bytes 49160 | tf_op jit(solution)/shard_map/ppermute | solution.py:371
  67.3 1.2 %collective-permute-done.16 = f32[32,128]{1,0:T(8,128)S(1)} collective-permute-done((f32[32,128]{1,0:T(8,128)S(1)}, f32[32,128]{1,0:T(8,128)S(1)}, u32[]{:S(2)}, u32[]{:S(2)}) %collective-permute-start.16) | collective-permute-done | bytes 16416 | tf_op jit(solution)/shard_map/ppermute | solution.py:371
  68.5 0.6 collective-permute-done.15
  69.0 0.2 collective-permute-done.14
  69.2 0.2 slice_reduce_fusion
  69.4 0.5 add_multiply_fusion
  69.9 0.1 fusion.2
  70.0 0.7 copy.20
  70.6 0.7 copy.19
  (6 shorter events, 0.0 us)
Async XLA Ops:
  0.6 6.0 %collective-permute-start.1 = (bf16[16,24,128]{2,1,0:T(8,128)(2,1)}, bf16[16,24,128]{2,1,0:T(8,128)(2,1)S(1)}, u32[]{:S(2)}, u32[]{:S(2)}) collective-permute-start(bf16[16,24,128]{2,1,0:T(8,128)(2,1)} %refs_0_.1), channel_id=1, source_target_pairs={{0,2},{2,0},{4,6},{6,4},{8,10},{10,8},{12,14},{14,12},{1,3},{3,1},... | collective-permute-start | bytes 294920 | tf_op jit(solution)/shard_map/ppermute | solution.py:359
  3.7 3.0 %collective-permute-start.2 = (bf16[16,24,128]{2,1,0:T(8,128)(2,1)}, bf16[16,24,128]{2,1,0:T(8,128)(2,1)S(1)}, u32[]{:S(2)}, u32[]{:S(2)}) collective-permute-start(bf16[16,24,128]{2,1,0:T(8,128)(2,1)} %refs_0_.1), channel_id=1, source_target_pairs={{2,4},{4,2},{6,8},{8,6},{10,12},{12,10},{3,5},{5,3},{7,9},{9,7},{1... | collective-permute-start | bytes 294920 | tf_op jit(solution)/shard_map/ppermute | solution.py:359
  4.3 4.4 %collective-permute-start = (bf16[16,24,128]{2,1,0:T(8,128)(2,1)}, bf16[16,24,128]{2,1,0:T(8,128)(2,1)S(1)}, u32[]{:S(2)}, u32[]{:S(2)}) collective-permute-start(bf16[16,24,128]{2,1,0:T(8,128)(2,1)} %refs_0_.1), channel_id=1, source_target_pairs={{0,1},{1,0},{2,3},{3,2},{4,5},{5,4},{6,7},{7,6},{8,9},{9,8},{10,11... | collective-permute-start | bytes 294920 | tf_op jit(solution)/shard_map/ppermute | solution.py:359
  4.4 0.7 copy-start.2
  6.7 2.1 %collective-permute-start.3 = (bf16[16,24,128]{2,1,0:T(8,128)(2,1)S(1)}, bf16[16,24,128]{2,1,0:T(8,128)(2,1)S(1)}, u32[]{:S(2)}, u32[]{:S(2)}) collective-permute-start(bf16[16,24,128]{2,1,0:T(8,128)(2,1)S(1)} %collective-permute-done.1.refs_2_), channel_id=1, source_target_pairs={{0,1},{1,0},{2,3},{3,2},{4,5},{5,4},{6,7},{7,6},{8,9},{9,8},{10,11... | collective-permute-start | bytes 294920 | tf_op jit(solution)/shard_map/ppermute | solution.py:359
  6.9 1.8 %collective-permute-start.4 = (bf16[16,24,128]{2,1,0:T(8,128)(2,1)S(1)}, bf16[16,24,128]{2,1,0:T(8,128)(2,1)S(1)}, u32[]{:S(2)}, u32[]{:S(2)}) collective-permute-start(bf16[16,24,128]{2,1,0:T(8,128)(2,1)S(1)} %collective-permute-done.2.refs_4_), channel_id=1, source_target_pairs={{0,1},{1,0},{2,3},{3,2},{4,5},{5,4},{6,7},{7,6},{8,9},{9,8},{10,11... | collective-permute-start | bytes 294920 | tf_op jit(solution)/shard_map/ppermute | solution.py:359
  8.8 0.9 %copy-start = (bf16[16,24,128]{2,1,0:T(8,128)(2,1)S(1)}, bf16[16,24,128]{2,1,0:T(8,128)(2,1)}, u32[]{:S(2)}) copy-start(bf16[16,24,128]{2,1,0:T(8,128)(2,1)} %refs_0_.1) | copy-start | bytes 294916
  9.7 0.7 copy-start.1
  31.7 5.9 %collective-permute-start.7 = (f32[32,128]{1,0:T(8,128)S(1)}, f32[32,128]{1,0:T(8,128)S(1)}, u32[]{:S(2)}, u32[]{:S(2)}) collective-permute-start(f32[32,128]{1,0:T(8,128)S(1)} %get-tuple-element.27), channel_id=1, source_target_pairs={{0,3},{1,2},{2,1},{3,0},{4,7},{5,6},{6,5},{7,4},{8,11},{9,10},{10,... | collective-permute-start | bytes 49160 | tf_op jit(solution)/shard_map/ppermute | solution.py:371
  36.1 3.7 %collective-permute-start.6 = (f32[32,128]{1,0:T(8,128)S(1)}, f32[32,128]{1,0:T(8,128)S(1)}, u32[]{:S(2)}, u32[]{:S(2)}) collective-permute-start(f32[32,128]{1,0:T(8,128)S(1)} %get-tuple-element.27), channel_id=1, source_target_pairs={{0,2},{1,3},{2,0},{3,1},{4,6},{5,7},{6,4},{7,5},{8,10},{9,11},{10,... | collective-permute-start | bytes 49160 | tf_op jit(solution)/shard_map/ppermute | solution.py:371
  36.6 3.3 %collective-permute-start.5 = (f32[32,128]{1,0:T(8,128)S(1)}, f32[32,128]{1,0:T(8,128)S(1)}, u32[]{:S(2)}, u32[]{:S(2)}) collective-permute-start(f32[32,128]{1,0:T(8,128)S(1)} %get-tuple-element.27), channel_id=1, source_target_pairs={{0,1},{1,0},{2,3},{3,2},{4,5},{5,4},{6,7},{7,6},{8,9},{9,8},{10,11... | collective-permute-start | bytes 49160 | tf_op jit(solution)/shard_map/ppermute | solution.py:371
  39.9 5.7 %collective-permute-start.10 = (f32[32,128]{1,0:T(8,128)S(1)}, f32[32,128]{1,0:T(8,128)S(1)}, u32[]{:S(2)}, u32[]{:S(2)}) collective-permute-start(f32[32,128]{1,0:T(8,128)S(1)} %add_add_fusion.3), channel_id=1, source_target_pairs={{0,12},{1,13},{2,14},{3,15},{4,8},{5,9},{6,10},{7,11},{8,4},{9,5},... | collective-permute-start | bytes 49160 | tf_op jit(solution)/shard_map/ppermute | solution.py:371
  43.9 4.6 %collective-permute-start.9 = (f32[32,128]{1,0:T(8,128)S(1)}, f32[32,128]{1,0:T(8,128)S(1)}, u32[]{:S(2)}, u32[]{:S(2)}) collective-permute-start(f32[32,128]{1,0:T(8,128)S(1)} %add_add_fusion.3), channel_id=1, source_target_pairs={{0,8},{1,9},{2,10},{3,11},{4,12},{5,13},{6,14},{7,15},{8,0},{9,1},... | collective-permute-start | bytes 49160 | tf_op jit(solution)/shard_map/ppermute | solution.py:371
  43.9 4.6 %collective-permute-start.8 = (f32[32,128]{1,0:T(8,128)S(1)}, f32[32,128]{1,0:T(8,128)S(1)}, u32[]{:S(2)}, u32[]{:S(2)}) collective-permute-start(f32[32,128]{1,0:T(8,128)S(1)} %add_add_fusion.3), channel_id=1, source_target_pairs={{0,4},{1,5},{2,6},{3,7},{4,0},{5,1},{6,2},{7,3},{8,12},{9,13},{10,... | collective-permute-start | bytes 49160 | tf_op jit(solution)/shard_map/ppermute | solution.py:371
  59.0 3.2 %collective-permute-start.13 = (f32[32,128]{1,0:T(8,128)S(1)}, f32[32,128]{1,0:T(8,128)S(1)}, u32[]{:S(2)}, u32[]{:S(2)}) collective-permute-start(f32[32,128]{1,0:T(8,128)S(1)} %get-tuple-element.29), channel_id=1, source_target_pairs={{0,3},{1,2},{2,1},{3,0},{4,7},{5,6},{6,5},{7,4},{8,11},{9,10},{10,... | collective-permute-start | bytes 49160 | tf_op jit(solution)/shard_map/ppermute | solution.py:371
  59.0 3.8 %collective-permute-start.12 = (f32[32,128]{1,0:T(8,128)S(1)}, f32[32,128]{1,0:T(8,128)S(1)}, u32[]{:S(2)}, u32[]{:S(2)}) collective-permute-start(f32[32,128]{1,0:T(8,128)S(1)} %get-tuple-element.29), channel_id=1, source_target_pairs={{0,2},{1,3},{2,0},{3,1},{4,6},{5,7},{6,4},{7,5},{8,10},{9,11},{10,... | collective-permute-start | bytes 49160 | tf_op jit(solution)/shard_map/ppermute | solution.py:371
  60.6 2.2 %collective-permute-start.11 = (f32[32,128]{1,0:T(8,128)S(1)}, f32[32,128]{1,0:T(8,128)S(1)}, u32[]{:S(2)}, u32[]{:S(2)}) collective-permute-start(f32[32,128]{1,0:T(8,128)S(1)} %get-tuple-element.29), channel_id=1, source_target_pairs={{0,1},{1,0},{2,3},{3,2},{4,5},{5,4},{6,7},{7,6},{8,9},{9,8},{10,11... | collective-permute-start | bytes 49160 | tf_op jit(solution)/shard_map/ppermute | solution.py:371
  62.8 5.6 %collective-permute-start.16 = (f32[32,128]{1,0:T(8,128)S(1)}, f32[32,128]{1,0:T(8,128)S(1)}, u32[]{:S(2)}, u32[]{:S(2)}) collective-permute-start(f32[32,128]{1,0:T(8,128)S(1)} %add_add_fusion.1), channel_id=1, source_target_pairs={{0,12},{1,13},{2,14},{3,15},{4,8},{5,9},{6,10},{7,11},{8,4},{9,5},... | collective-permute-start | bytes 49160 | tf_op jit(solution)/shard_map/ppermute | solution.py:371
  64.4 4.7 %collective-permute-start.15 = (f32[32,128]{1,0:T(8,128)S(1)}, f32[32,128]{1,0:T(8,128)S(1)}, u32[]{:S(2)}, u32[]{:S(2)}) collective-permute-start(f32[32,128]{1,0:T(8,128)S(1)} %add_add_fusion.1), channel_id=1, source_target_pairs={{0,8},{1,9},{2,10},{3,11},{4,12},{5,13},{6,14},{7,15},{8,0},{9,1},... | collective-permute-start | bytes 49160 | tf_op jit(solution)/shard_map/ppermute | solution.py:371
  65.0 4.2 %collective-permute-start.14 = (f32[32,128]{1,0:T(8,128)S(1)}, f32[32,128]{1,0:T(8,128)S(1)}, u32[]{:S(2)}, u32[]{:S(2)}) collective-permute-start(f32[32,128]{1,0:T(8,128)S(1)} %add_add_fusion.1), channel_id=1, source_target_pairs={{0,4},{1,5},{2,6},{3,7},{4,0},{5,1},{6,2},{7,3},{8,12},{9,13},{10,... | collective-permute-start | bytes 49160 | tf_op jit(solution)/shard_map/ppermute | solution.py:371

commit v3 on v2

--- a/solution.py
+++ b/solution.py
@@ -59,11 +59,12 @@
     return lines
 
 
-def matrices_kernel(dims, directions_ref, time_ref, xline_ref, inline_ref):
+def matrices_kernel(dims, directions_ref, own_ref, time_ref, xline_ref, inline_ref, kept_ref):
     orients, samples, cols, rows, window = dims
     side = lax.axis_index("xline")
     lanes = lax.broadcasted_iota(jnp.int32, (SUBLANES, LANES), 1)[:1]
     lines = tap_lines(directions_ref, orients)
+    kept_ref[...] = own_ref[...]
 
     def sheared(line, count, shift, width):
         if width > LANES:
@@ -181,17 +182,14 @@
 def features_kernel(dims, *refs):
     orients, samples, cols, rows, window, components, chunk, unit = dims
     halves, refs = refs[:6], refs[6:]
-    time_ref, xline_ref, inline_ref, means_ref, variances_ref, weights_ref = refs[:6]
-    features_ref, sums_ref, traces, across, params, total, data, scores, own, arrived = refs[6:]
+    time_ref, xline_ref, inline_ref, params_ref = refs[:4]
+    features_ref, sums_ref, traces, across_even, across_odd, total, data, scores = refs[4:]
     feats = 2 * orients
     slot = round_up(feats + 2, SUBLANES)
-    orient = pl.program_id(0)
-    @pl.when(orient == 0)
+    twice = pl.program_id(0)
+    @pl.when(twice == 0)
     def _():
-        own_copy = pltpu.make_async_copy(halves[0], own, arrived)
-        own_copy.start()
-        own_copy.wait()
-        other, swap_one, swap_one_other, swap_two, swap_two_other = halves[1:]
+        own, other, swap_one, swap_one_other, swap_two, swap_two_other = halves
         even = lax.rem(lax.axis_index("inline"), 2) == 0
 
         def put(place, near, far):
@@ -221,57 +219,65 @@
 
     lines = 2 * cols
     apart = window + 1
-    group = window
-    for pair in range(window // 2):
-        if pair * 2 % group == 0:
-            block = traces[pl.ds(pair * 2 * lines, group * lines), :]
-            band = jnp.dot(block, time_ref[0], preferred_element_type=jnp.float32)
-            band = band.astype(jnp.bfloat16)
-
-        def piece(k, p):
-            first = (pair * 2 % group + k) * lines
-            return band[first : first + lines, p * samples : (p + 1) * samples]
+
+    def magnitudes(orient, across, piece):
+        polarity, col = piece // (cols // 2), piece % (cols // 2) * 2
+
+        def taken(k, part):
+            place = ((polarity * 2 + part) * cols + col + k) * apart
+            return across[pl.ds(place, window), :]
 
         stacked = jnp.concatenate(
-            [jnp.concatenate([piece(k, 0), piece(k, 1)], axis=0) for k in range(2)], axis=1
-        )
-        crossed = jnp.dot(xline_ref[0], stacked, preferred_element_type=jnp.float32)
+            [jnp.concatenate([taken(k, 0), taken(k, 1)], axis=0) for k in range(2)], axis=1
+        ).astype(jnp.bfloat16)
+        found = jnp.dot(inline_ref[orient], stacked, preferred_element_type=jnp.float32)
+        real_part, imag_part = found[:rows], found[rows:]
+        power = real_part * real_part + imag_part * imag_part + eps_mag
+        size = power * lax.rsqrt(power)
         for k in range(2):
-            across[pl.ds(2 * pair + k, 4 * cols, stride=apart), :] = crossed[
+            place = (col + k) * rows * (slot + 1) + 2 * orient + polarity
+            features_ref[pl.ds(place, rows, stride=slot + 1), :] = size[
                 :, k * samples : (k + 1) * samples
             ]
-    for polarity in range(2):
-        for col in range(0, cols, 2):
-
-            def taken(k, part):
-                place = ((polarity * 2 + part) * cols + col + k) * apart
-                return across[pl.ds(place, window), :]
+
+    def filtered(which, across, before, across_before):
+        band = jnp.dot(traces[...], time_ref[which], preferred_element_type=jnp.float32)
+        band = band.astype(jnp.bfloat16)
+        done = 0
+        for pair in range(window // 2):
+
+            def piece(k, p):
+                first = (pair * 2 + k) * lines
+                return band[first : first + lines, p * samples : (p + 1) * samples]
 
             stacked = jnp.concatenate(
-                [jnp.concatenate([taken(k, 0), taken(k, 1)], axis=0) for k in range(2)], axis=1
-            ).astype(jnp.bfloat16)
-            found = jnp.dot(inline_ref[0], stacked, preferred_element_type=jnp.float32)
-            real_part, imag_part = found[:rows], found[rows:]
-            power = real_part * real_part + imag_part * imag_part + eps_mag
-            size = power * lax.rsqrt(power)
+                [jnp.concatenate([piece(k, 0), piece(k, 1)], axis=0) for k in range(2)], axis=1
+            )
+            crossed = jnp.dot(xline_ref[which], stacked, preferred_element_type=jnp.float32)
             for k in range(2):
-                place = (col + k) * rows * (slot + 1) + 2 * orient + polarity
-                features_ref[pl.ds(place, rows, stride=slot + 1), :] = size[
+                across[pl.ds(2 * pair + k, 4 * cols, stride=apart), :] = crossed[
                     :, k * samples : (k + 1) * samples
                 ]
-
-    @pl.when(orient == orients - 1)
+            until = cols * (pair + 1) // (window // 2)
+            for other in range(done, until):
+                magnitudes(before, across_before, other)
+            done = until
+
+    filtered(0, across_even, jnp.maximum(2 * twice - 1, 0), across_odd)
+    filtered(1, across_odd, 2 * twice, across_even)
+
+    @pl.when(twice == orients // 2 - 1)
     def _():
-        params[...] = jnp.ones(params.shape, jnp.float32)
-        params[:components, :feats] = means_ref[...]
-        params[components:, :feats] = variances_ref[...]
-        row_ids = lax.broadcasted_iota(jnp.int32, (components, 1), 0)
-        weights = jnp.ones((components, 1), jnp.float32)
-        for component in range(components):
-            weights = jnp.where(row_ids == component, weights_ref[component], weights)
-        log_weights = jnp.log(weights)
+        for piece in range(cols):
+            magnitudes(orients - 1, across_odd, piece)
+
+    @pl.when(twice == orients // 2 - 1)
+    def _():
         matrix = score_matrix(
-            params[:components], params[components:], log_weights, feats, slot, 3
+            params_ref[:components],
+            params_ref[components : 2 * components],
+            jnp.log(params_ref[2 * components :, :1]),
+            feats, slot, 3,
         )
         total[...] = jnp.zeros(total.shape, jnp.float32)
 
@@ -305,8 +311,8 @@
 
 def posterior_kernel(dims, *refs):
     orients, samples, cols, rows, components, chunk, unit, cells = dims
-    features_ref, means_ref, variances_ref, before_ref = refs[:4]
-    posterior_ref, sums_ref, centers_ref, spreads_ref, matrix, total, turned, data, scores = refs[4:]
+    features_ref, params_ref, before_ref = refs[:3]
+    posterior_ref, sums_ref, centers_ref, spreads_ref, matrix, total, turned, data, scores = refs[3:]
     feats = 2 * orients
     slot = round_up(feats + 2, SUBLANES)
     step = pl.program_id(0)
@@ -314,12 +320,11 @@
 
     @pl.when(step == 0)
     def _():
-        centers_ref[...] = jnp.zeros(centers_ref.shape, jnp.float32)
-        spreads_ref[...] = jnp.ones(spreads_ref.shape, jnp.float32)
-        centers_ref[:, :feats] = means_ref[...]
-        spreads_ref[:, :feats] = variances_ref[...]
         centers, spreads, weights = new_params(
-            before_ref[...], centers_ref[...], spreads_ref[...], feats, slot, cells
+            before_ref[...],
+            params_ref[:components],
+            params_ref[components : 2 * components],
+            feats, slot, cells,
         )
         lanes = lax.broadcasted_iota(jnp.int32, centers.shape, 1)
         centers = jnp.where(lanes < feats, centers, 0.0)
@@ -355,6 +360,25 @@
         sums_ref[...] = fold_sums(total[...], components, slot)
 
 
+def update_kernel(dims, sums_ref, centers_ref, spreads_ref, means_ref, variances_ref, weights_ref):
+    feats, slot, cells = dims
+    components = sums_ref.shape[0]
+    rest = jnp.zeros((LANES - 3 * components, LANES), jnp.float32)
+    turned = jnp.concatenate(
+        [sums_ref[...], centers_ref[...], spreads_ref[...], rest], axis=0
+    ).T
+    part = lambda first, group: turned[
+        first : first + feats, group * components : (group + 1) * components
+    ]
+    mass = turned[feats : feats + 1, :components]
+    first, second, centers, spreads = part(0, 0), part(slot, 0), part(0, 1), part(0, 2)
+    moved = (first + centers) / (mass + 1.0)
+    centred = second - 2.0 * moved * first + moved * moved * mass
+    means_ref[...] = moved
+    variances_ref[...] = (centred + spreads) / (mass + 1.0)
+    weights_ref[...] = (mass + 1.0) / (cells + components)
+
+
 def exchange(values, axis, pairs):
     return lax.ppermute(values, axis, [p for a, b in pairs for p in ((a, b), (b, a))])
 
@@ -364,9 +388,15 @@
     count = lax.axis_size("inline") * lax.axis_size("xline")
     if count & (count - 1):
         return lax.psum(values, axes)
-    step = 1
-    while step < count:
-        radix = min(4, count // step)
+    rounds = []
+    while count > 1:
+        rounds.append(min(4, count))
+        count //= rounds[-1]
+    for radix in rounds:
+        count *= radix
+    step = count
+    for radix in rounds:
+        step //= radix
         arrived = [
             lax.ppermute(values, axes, [(i, i ^ (step * d)) for i in range(count)])
             for d in range(1, radix)
@@ -375,7 +405,6 @@
             values = (values + arrived[0]) + (arrived[1] + arrived[2])
         else:
             values = values + arrived[0]
-        step *= radix
     return values
 
 
@@ -387,7 +416,7 @@
     slot = round_up(feats + 2, SUBLANES)
     window = round_up(rows + 2 * HALF, 16)
     inlines = lax.axis_size("inline")
-    if lax.axis_size("xline") != 2 or samples != LANES or rows < HALF:
+    if lax.axis_size("xline") != 2 or samples != LANES or rows < HALF or orients % 2 or cols % 2:
         raise ValueError("unsupported sizes")
 
     core_pairs = [(0, 1)]
@@ -395,26 +424,38 @@
     swap_one = exchange(traces, "inline", [(i, i + 1) for i in range(0, inlines - 1, 2)])
     swap_two = exchange(traces, "inline", [(i, i + 1) for i in range(1, inlines - 1, 2)])
     vmem = pl.BlockSpec(memory_space=pltpu.VMEM)
-    time_mats, xline_mats, inline_mats = pl.pallas_call(
+    time_mats, xline_mats, inline_mats, own = pl.pallas_call(
         functools.partial(matrices_kernel, (orients, samples, cols, rows, window)),
         out_shape=(
             jax.ShapeDtypeStruct((orients, samples, 2 * samples), jnp.bfloat16),
             jax.ShapeDtypeStruct((orients, 4 * cols, 4 * cols), jnp.bfloat16),
             jax.ShapeDtypeStruct((orients, 2 * rows, 2 * window), jnp.bfloat16),
-        ),
-        in_specs=[pl.BlockSpec(memory_space=pltpu.SMEM)],
-        out_specs=(vmem, vmem, vmem),
+            jax.ShapeDtypeStruct(traces.shape, traces.dtype),
+        ),
+        in_specs=[pl.BlockSpec(memory_space=pltpu.SMEM), vmem],
+        out_specs=(vmem, vmem, vmem, vmem),
         compiler_params=pltpu.CompilerParams(vmem_limit_bytes=8 * 2**20),
         name="filter_matrices",
         cost_estimate=pl.CostEstimate(flops=0, bytes_accessed=4_000_000, transcendentals=0),
-    )(directions)
-
-    swap_one, swap_two, time_mats, xline_mats, inline_mats = lax.optimization_barrier(
-        (swap_one, swap_two, time_mats, xline_mats, inline_mats)
+    )(directions, traces)
+
+    swap_one, swap_two, time_mats, xline_mats, inline_mats, own = lax.optimization_barrier(
+        (swap_one, swap_two, time_mats, xline_mats, inline_mats, own)
     )
     swap_one_other = exchange(swap_one, "xline", core_pairs)
     swap_two_other = exchange(swap_two, "xline", core_pairs)
 
+    spread_out = lambda values, fill: jnp.pad(
+        values, ((0, 0), (0, LANES - values.shape[1])), constant_values=fill
+    )
+    params = jnp.concatenate(
+        [
+            spread_out(init_means, 0.0),
+            spread_out(init_variances, 1.0),
+            jnp.broadcast_to(init_weights[:, None], (components, LANES)),
+        ],
+        axis=0,
+    )
     whole = lambda *shape: pl.BlockSpec(shape, lambda o: (0,) * len(shape))
     chunk = 6
     unit = 2 if rows % 2 == 0 else 1
@@ -422,38 +463,33 @@
         functools.partial(
             features_kernel, (orients, samples, cols, rows, window, components, chunk, unit)
         ),
-        grid=(orients,),
+        grid=(orients // 2,),
         out_shape=(
             jax.ShapeDtypeStruct((rows * cols * (slot + 1), samples), jnp.float32),
             jax.ShapeDtypeStruct((components, LANES), jnp.float32),
         ),
-        in_specs=[pl.BlockSpec(memory_space=pltpu.HBM)]
-        + [whole(rows, cols, samples)] * 5
+        in_specs=[whole(rows, cols, samples)] * 6
         + [
-            pl.BlockSpec((1, samples, 2 * samples), lambda o: (o, 0, 0)),
-            pl.BlockSpec((1, 4 * cols, 4 * cols), lambda o: (o, 0, 0)),
-            pl.BlockSpec((1, 2 * rows, 2 * window), lambda o: (o, 0, 0)),
-            whole(components, feats),
-            whole(components, feats),
-            pl.BlockSpec(memory_space=pltpu.SMEM),
+            pl.BlockSpec((2, samples, 2 * samples), lambda o: (o, 0, 0)),
+            pl.BlockSpec((2, 4 * cols, 4 * cols), lambda o: (o, 0, 0)),
+            whole(orients, 2 * rows, 2 * window),
+            whole(3 * components, LANES),
         ],
         out_specs=(whole(rows * cols * (slot + 1), samples), whole(components, LANES)),
         scratch_shapes=[
             pltpu.VMEM((window * 2 * cols, samples), jnp.bfloat16),
             pltpu.VMEM((4 * cols * (window + 1), samples), jnp.float32),
-            pltpu.VMEM((2 * components, LANES), jnp.float32),
+            pltpu.VMEM((4 * cols * (window + 1), samples), jnp.float32),
             pltpu.VMEM((4 * slot, 2 * components), jnp.float32),
             pltpu.VMEM((4 * slot, unit * cols * samples), jnp.bfloat16),
             pltpu.VMEM((components, unit * cols * samples), jnp.float32),
-            pltpu.VMEM((rows, cols, samples), jnp.bfloat16),
-            pltpu.SemaphoreType.DMA,
         ],
         compiler_params=pltpu.CompilerParams(vmem_limit_bytes=40 * 2**20),
         name="features_and_first_moments",
     )(
-        traces, other, swap_one, swap_one_other, swap_two, swap_two_other,
+        own, other, swap_one, swap_one_other, swap_two, swap_two_other,
         time_mats, xline_mats, inline_mats,
-        init_means, init_variances, init_weights,
+        params,
     )
     sums = group_sum(sums)
     cells = inlines * rows * lax.axis_size("xline") * cols * samples
@@ -470,8 +506,7 @@
         ),
         in_specs=[
             whole(rows * cols * (slot + 1), samples),
-            whole(components, feats),
-            whole(components, feats),
+            whole(3 * components, LANES),
             whole(components, LANES),
         ],
         out_specs=(
@@ -489,16 +524,21 @@
         ],
         compiler_params=pltpu.CompilerParams(vmem_limit_bytes=40 * 2**20),
         name="posterior_and_second_moments",
-    )(features, init_means, init_variances, sums)
+    )(features, params, sums)
     sums = group_sum(sums)
-    mass = sums[:, feats : feats + 1]
-    first = sums[:, :feats]
-    second = sums[:, slot : slot + feats]
-    centers, spreads = centers[:, :feats], spreads[:, :feats]
-    moved = (first + centers) / (mass + 1.0)
-    centred = second - 2.0 * moved * first + moved * moved * mass
-    final_spreads = (centred + spreads) / (mass + 1.0)
-    return posterior, moved, final_spreads, (mass[:, 0] + 1.0) / (cells + components)
+    means, variances, weights = pl.pallas_call(
+        functools.partial(update_kernel, (feats, slot, cells)),
+        out_shape=(
+            jax.ShapeDtypeStruct((feats, components), jnp.float32),
+            jax.ShapeDtypeStruct((feats, components), jnp.float32),
+            jax.ShapeDtypeStruct((1, components), jnp.float32),
+        ),
+        in_specs=[vmem, vmem, vmem],
+        out_specs=(vmem, vmem, vmem),
+        compiler_params=pltpu.CompilerParams(vmem_limit_bytes=8 * 2**20),
+        name="last_update",
+    )(sums, centers, spreads)
+    return posterior, means.T, variances.T, weights.reshape(components)
 
 
 def solution(mesh):

time: 71.7 us -> 66 us (0.921)
  Pallas kernels: 33.2 us -> 30.9 us
  local copies, waits for them, and re-layouts: 5.11 us -> 3.85 us
  waiting for transfers between devices: 11.4 us -> 10.4 us
    ppermute x12, starting transfers between devices: 15.9 us -> 12.6 us  [group_sum(): lax.ppermute(values, axes, [(i, i ^ step * d) for i in range(count)])]
    pallas_call x1, Pallas kernels: 21.4 us -> 18.4 us  [per_device(): pl.pallas_call(functools.partial(features_kernel, (orients, samples, cols...]
    ppermute x5, starting transfers between devices: 4.27 us -> 7.07 us  [exchange(): lax.ppermute(values, axis, [p for a, b in pairs for p in ((a, b), (b, a))])]
    unnamed x10 -> x6, local copies, waits for them, and re-layouts: 5.11 us -> 3.11 us
    ppermute x12, waiting for transfers between devices: 11 us -> 9.27 us  [group_sum(): lax.ppermute(values, axes, [(i, i ^ step * d) for i in range(count)])]
    ppermute x5, waiting for transfers between devices: 0.34 us -> 1.15 us  [exchange(): lax.ppermute(values, axis, [p for a, b in pairs for p in ((a, b), (b, a))])]
    pallas_call x0 -> x1, Pallas kernels: none -> 0.75 us  [per_device(): pl.pallas_call(functools.partial(update_kernel, (feats, slot, cells)), ou...]
    concatenate x0 -> x1, local copies, waits for them, and re-layouts: none -> 0.73 us  [per_device(): jnp.concatenate([spread_out(init_means, 0.0), spread_out(init_variances,...]
  transfers between devices with their start and end apart: 17 -> 17, of which waited for: 10 -> 10; matrix products, arithmetic and copies ran while one was open for 2% -> 4% of each run, Pallas kernels for 2% -> 2%
where the time goes in v3:
time: 66 us; the launch traced here: 65.7 us
  Pallas kernels  30.9 us (47%)
  starting transfers between devices  19.7 us (30%)
  waiting for transfers between devices  10.4 us (16%)
  local copies, waits for them, and re-layouts  3.85 us (6%)
  between operations  0.7 us (1%)
    pallas_call x1, Pallas kernels, per_device(): pl.pallas_call(functools.partial(features_kernel, (orients, samples, cols...  18.4 us
    ppermute x12, starting transfers between devices, group_sum(): lax.ppermute(values, axes, [(i, i ^ step * d) for i in range(count)])  12.6 us
    pallas_call x1, Pallas kernels, per_device(): pl.pallas_call(functools.partial(posterior_kernel, (orients, samples, col...  10.5 us
    ppermute x12, waiting for transfers between devices, group_sum(): lax.ppermute(values, axes, [(i, i ^ step * d) for i in range(count)])  9.27 us
    ppermute x5, starting transfers between devices, exchange(): lax.ppermute(values, axis, [p for a, b in pairs for p in ((a, b), (b, a))])  7.07 us
    unnamed x6, local copies, waits for them, and re-layouts  3.11 us
  transfers between devices with their start and end apart: 17, of which 10 were waited for; matrix products, arithmetic and copies ran while one was open for 4% of the time, Pallas kernels for 2%

profile of v3, /device:TPU:0, one launch (start us, length us, event | category | flops | bytes accessed | tf_op | source)
XLA Modules:
  0.0 65.7 jit_solution(13893095221381830833)
XLA Ops:
  0.6 0.7 %collective-permute-start.1 = (bf16[16,24,128]{2,1,0:T(8,128)(2,1)}, bf16[16,24,128]{2,1,0:T(8,128)(2,1)S(1)}, u32[]{:S(2)}, u32[]{:S(2)}) collective-permute-start(bf16[16,24,128]{2,1,0:T(8,128)(2,1)} %own_ref.1), channel_id=1, source_target_pairs={{2,4},{4,2},{6,8},{8,6},{10,12},{12,10},{3,5},{5,3},{7,9},{9,7},{1... | collective-permute-start | bytes 294920 | tf_op jit(solution)/shard_map/ppermute | solution.py:383
  1.3 5.8 %collective-permute-start = (bf16[16,24,128]{2,1,0:T(8,128)(2,1)}, bf16[16,24,128]{2,1,0:T(8,128)(2,1)S(1)}, u32[]{:S(2)}, u32[]{:S(2)}) collective-permute-start(bf16[16,24,128]{2,1,0:T(8,128)(2,1)} %own_ref.1), channel_id=1, source_target_pairs={{0,2},{2,0},{4,6},{6,4},{8,10},{10,8},{12,14},{14,12},{1,3},{3,1},... | collective-permute-start | bytes 294920 | tf_op jit(solution)/shard_map/ppermute | solution.py:383
  7.1 0.0 collective-permute-start.2
  7.1 0.8 %copy.9 = f32[32,20]{1,0:T(8,128)S(1)} copy(f32[32,20]{0,1:T(8,128)} %param.7) | data formatting | bytes 5120 | tf_op args[2]
  7.9 0.8 %copy.10 = f32[32,20]{1,0:T(8,128)S(1)} copy(f32[32,20]{0,1:T(8,128)} %param.8) | data formatting | bytes 5120 | tf_op args[3]
  8.7 0.0 copy-start
  8.7 0.9 %copy-done = bf16[16,24,128]{2,1,0:T(8,128)(2,1)S(1)} copy-done((bf16[16,24,128]{2,1,0:T(8,128)(2,1)S(1)}, bf16[16,24,128]{2,1,0:T(8,128)(2,1)}, u32[]{:S(2)}) %copy-start) | copy-done | bytes 98328
  9.6 0.0 copy-start.1
  9.6 0.7 copy-done.1
  10.2 1.3 %filter_matrices.1 = (bf16[10,128,256]{2,1,0:T(8,128)(2,1)S(1)}, bf16[10,96,96]{2,1,0:T(8,128)(2,1)S(1)}, bf16[10,32,96]{2,1,0:T(8,128)(2,1)S(1)}, bf16[16,24,128]{2,1,0:T(8,128)(2,1)S(1)}) custom-call(s32[10]{0:T(128)S(1)} %copy-done.1, bf16[16,24,128]{2,1,0:T(8,128)(2,1)S(1)} %copy-done), custom_call_target="tpu_custom_call" | custom-call | bytes 4000000 | tf_op jit(solution)/shard_map/filter_matrices/pallas_call | solution.py:427
  11.5 0.7 %pad.11.clone = f32[96]{0:T(128)S(1)} pad(f32[32]{0:T(128)} %param.9, f32[]{:T(128)} %constant.8), padding=64_0 | pad | bytes 516 | tf_op jit(solution)/shard_map/concatenate | solution.py:451
  12.2 0.0 collective-permute-done.1.refs_4_
  12.2 0.0 collective-permute-done.refs_2_
  12.2 0.5 collective-permute-start.3
  12.8 0.1 collective-permute-start.4
  12.8 0.1 fusion.refs_9_.refs_1_
  12.9 0.0 collective-permute-done.2.refs_1_
  12.9 0.8 %collective-permute-done.3.refs_3_ = bf16[16,24,128]{2,1,0:T(8,128)(2,1)S(1)} collective-permute-done((bf16[16,24,128]{2,1,0:T(8,128)(2,1)S(1)}, bf16[16,24,128]{2,1,0:T(8,128)(2,1)S(1)}, u32[]{:S(2)}, u32[]{:S(2)}) %collective-permute-start.3) | collective-permute-done | bytes 98336 | tf_op jit(solution)/shard_map/ppermute | solution.py:383
  13.7 0.4 collective-permute-done.4.refs_5_
  14.1 18.4 %features_and_first_moments.1 = (f32[9600,128]{1,0:T(8,128)S(1)}, f32[32,128]{1,0:T(8,128)S(1)}) custom-call(bf16[16,24,128]{2,1,0:T(8,128)(2,1)S(1)} %get-tuple-element.27.refs_0_, bf16[16,24,128]{2,1,0:T(8,128)(2,1)S(1)} %collective-permute-done.2.refs_1_, bf16[16,24,128]{2,1,0:T(8,128)(2,1)S(1)} %collective-permute-done.refs_2_, ...), custom_call_target="tpu_custom_call" | custom-call | tf_op jit(solution)/shard_map/features_and_first_moments/pallas_call | solution.py:462
  32.4 2.8 %collective-permute-start.7 = (f32[32,128]{1,0:T(8,128)S(1)}, f32[32,128]{1,0:T(8,128)S(1)}, u32[]{:S(2)}, u32[]{:S(2)}) collective-permute-start(f32[32,128]{1,0:T(8,128)S(1)} %get-tuple-element.34), channel_id=1, source_target_pairs={{0,12},{1,13},{2,14},{3,15},{4,8},{5,9},{6,10},{7,11},{8,4},{9,5},... | collective-permute-start | bytes 49160 | tf_op jit(solution)/shard_map/ppermute | solution.py:401
  35.2 0.3 collective-permute-start.6
  35.5 1.3 %collective-permute-start.5 = (f32[32,128]{1,0:T(8,128)S(1)}, f32[32,128]{1,0:T(8,128)S(1)}, u32[]{:S(2)}, u32[]{:S(2)}) collective-permute-start(f32[32,128]{1,0:T(8,128)S(1)} %get-tuple-element.34), channel_id=1, source_target_pairs={{0,4},{1,5},{2,6},{3,7},{4,0},{5,1},{6,2},{7,3},{8,12},{9,13},{10,... | collective-permute-start | bytes 49160 | tf_op jit(solution)/shard_map/ppermute | solution.py:401
  36.9 1.2 %collective-permute-done.7 = f32[32,128]{1,0:T(8,128)S(1)} collective-permute-done((f32[32,128]{1,0:T(8,128)S(1)}, f32[32,128]{1,0:T(8,128)S(1)}, u32[]{:S(2)}, u32[]{:S(2)}) %collective-permute-start.7) | collective-permute-done | bytes 16416 | tf_op jit(solution)/shard_map/ppermute | solution.py:401
  38.0 1.8 %collective-permute-done.6 = f32[32,128]{1,0:T(8,128)S(1)} collective-permute-done((f32[32,128]{1,0:T(8,128)S(1)}, f32[32,128]{1,0:T(8,128)S(1)}, u32[]{:S(2)}, u32[]{:S(2)}) %collective-permute-start.6) | collective-permute-done | bytes 16416 | tf_op jit(solution)/shard_map/ppermute | solution.py:401
  39.9 0.0 collective-permute-done.5
  39.9 0.1 collective-permute-start.10
  40.0 1.3 %collective-permute-start.9 = (f32[32,128]{1,0:T(8,128)S(1)}, f32[32,128]{1,0:T(8,128)S(1)}, u32[]{:S(2)}, u32[]{:S(2)}) collective-permute-start(f32[32,128]{1,0:T(8,128)S(1)} %add_add_fusion.3), channel_id=1, source_target_pairs={{0,2},{1,3},{2,0},{3,1},{4,6},{5,7},{6,4},{7,5},{8,10},{9,11},{10,... | collective-permute-start | bytes 49160 | tf_op jit(solution)/shard_map/ppermute | solution.py:401
  41.3 0.5 collective-permute-start.8
  41.8 1.3 %collective-permute-done.10 = f32[32,128]{1,0:T(8,128)S(1)} collective-permute-done((f32[32,128]{1,0:T(8,128)S(1)}, f32[32,128]{1,0:T(8,128)S(1)}, u32[]{:S(2)}, u32[]{:S(2)}) %collective-permute-start.10) | collective-permute-done | bytes 16416 | tf_op jit(solution)/shard_map/ppermute | solution.py:401
  43.1 0.7 collective-permute-done.9
  43.8 0.0 collective-permute-done.8
  43.8 10.5 %posterior_and_second_moments.1 = (bf16[16,32,24,128]{3,2,1,0:T(8,128)(2,1)}, f32[32,128]{1,0:T(8,128)S(1)}, f32[32,128]{1,0:T(8,128)S(1)}, f32[32,128]{1,0:T(8,128)S(1)}) custom-call(f32[9600,128]{1,0:T(8,128)S(1)} %get-tuple-element.33.refs_0_, f32[96,128]{1,0:T(8,128)S(1)} %fusion.refs_9_.refs_1_, f32[32,128]{1,0:T(8,128)S(1)} %add_add_fusion.2.refs_2_), custom_call_target="tpu_custom_call" | custom-call | tf_op jit(solution)/shard_map/posterior_and_second_moments/pallas_call | solution.py:496
  54.3 1.9 %collective-permute-start.13 = (f32[32,128]{1,0:T(8,128)S(1)}, f32[32,128]{1,0:T(8,128)S(1)}, u32[]{:S(2)}, u32[]{:S(2)}) collective-permute-start(f32[32,128]{1,0:T(8,128)S(1)} %get-tuple-element.36), channel_id=1, source_target_pairs={{0,12},{1,13},{2,14},{3,15},{4,8},{5,9},{6,10},{7,11},{8,4},{9,5},... | collective-permute-start | bytes 49160 | tf_op jit(solution)/shard_map/ppermute | solution.py:401
  56.2 0.2 collective-permute-start.12
  56.5 2.2 %collective-permute-start.11 = (f32[32,128]{1,0:T(8,128)S(1)}, f32[32,128]{1,0:T(8,128)S(1)}, u32[]{:S(2)}, u32[]{:S(2)}) collective-permute-start(f32[32,128]{1,0:T(8,128)S(1)} %get-tuple-element.36), channel_id=1, source_target_pairs={{0,4},{1,5},{2,6},{3,7},{4,0},{5,1},{6,2},{7,3},{8,12},{9,13},{10,... | collective-permute-start | bytes 49160 | tf_op jit(solution)/shard_map/ppermute | solution.py:401
  58.7 1.3 %collective-permute-done.13 = f32[32,128]{1,0:T(8,128)S(1)} collective-permute-done((f32[32,128]{1,0:T(8,128)S(1)}, f32[32,128]{1,0:T(8,128)S(1)}, u32[]{:S(2)}, u32[]{:S(2)}) %collective-permute-start.13) | collective-permute-done | bytes 16416 | tf_op jit(solution)/shard_map/ppermute | solution.py:401
  60.0 1.0 %collective-permute-done.12 = f32[32,128]{1,0:T(8,128)S(1)} collective-permute-done((f32[32,128]{1,0:T(8,128)S(1)}, f32[32,128]{1,0:T(8,128)S(1)}, u32[]{:S(2)}, u32[]{:S(2)}) %collective-permute-start.12) | collective-permute-done | bytes 16416 | tf_op jit(solution)/shard_map/ppermute | solution.py:401
  61.0 0.0 collective-permute-done.11
  61.0 0.1 collective-permute-start.16
  61.0 0.9 %collective-permute-start.15 = (f32[32,128]{1,0:T(8,128)S(1)}, f32[32,128]{1,0:T(8,128)S(1)}, u32[]{:S(2)}, u32[]{:S(2)}) collective-permute-start(f32[32,128]{1,0:T(8,128)S(1)} %add_add_fusion.1), channel_id=1, source_target_pairs={{0,2},{1,3},{2,0},{3,1},{4,6},{5,7},{6,4},{7,5},{8,10},{9,11},{10,... | collective-permute-start | bytes 49160 | tf_op jit(solution)/shard_map/ppermute | solution.py:401
  61.9 1.0 %collective-permute-start.14 = (f32[32,128]{1,0:T(8,128)S(1)}, f32[32,128]{1,0:T(8,128)S(1)}, u32[]{:S(2)}, u32[]{:S(2)}) collective-permute-start(f32[32,128]{1,0:T(8,128)S(1)} %add_add_fusion.1), channel_id=1, source_target_pairs={{0,1},{1,0},{2,3},{3,2},{4,5},{5,4},{6,7},{7,6},{8,9},{9,8},{10,11... | collective-permute-start | bytes 49160 | tf_op jit(solution)/shard_map/ppermute | solution.py:401
  62.9 1.3 %collective-permute-done.16 = f32[32,128]{1,0:T(8,128)S(1)} collective-permute-done((f32[32,128]{1,0:T(8,128)S(1)}, f32[32,128]{1,0:T(8,128)S(1)}, u32[]{:S(2)}, u32[]{:S(2)}) %collective-permute-start.16) | collective-permute-done | bytes 16416 | tf_op jit(solution)/shard_map/ppermute | solution.py:401
  64.2 0.7 %collective-permute-done.15 = f32[32,128]{1,0:T(8,128)S(1)} collective-permute-done((f32[32,128]{1,0:T(8,128)S(1)}, f32[32,128]{1,0:T(8,128)S(1)}, u32[]{:S(2)}, u32[]{:S(2)}) %collective-permute-start.15) | collective-permute-done | bytes 16416 | tf_op jit(solution)/shard_map/ppermute | solution.py:401
  64.9 0.0 collective-permute-done.14
  64.9 0.8 %last_update.1 = (f32[20,32]{1,0:T(8,128)}, f32[20,32]{1,0:T(8,128)}, f32[1,32]{1,0:T(1,128)}) custom-call(f32[32,128]{1,0:T(8,128)S(1)} %add_add_fusion.sums_ref, f32[32,128]{1,0:T(8,128)S(1)} %get-tuple-element.37.centers_ref, f32[32,128]{1,0:T(8,128)S(1)} %get-tuple-element.38.spreads_ref), custom_call_target="tpu_custom_call" | custom-call | tf_op jit(solution)/shard_map/last_update/pallas_call | solution.py:529
  (4 shorter events, 0.0 us)
Async XLA Ops:
  0.6 11.6 %collective-permute-start.1 = (bf16[16,24,128]{2,1,0:T(8,128)(2,1)}, bf16[16,24,128]{2,1,0:T(8,128)(2,1)S(1)}, u32[]{:S(2)}, u32[]{:S(2)}) collective-permute-start(bf16[16,24,128]{2,1,0:T(8,128)(2,1)} %own_ref.1), channel_id=1, source_target_pairs={{2,4},{4,2},{6,8},{8,6},{10,12},{12,10},{3,5},{5,3},{7,9},{9,7},{1... | collective-permute-start | bytes 294920 | tf_op jit(solution)/shard_map/ppermute | solution.py:383
  1.3 10.9 %collective-permute-start = (bf16[16,24,128]{2,1,0:T(8,128)(2,1)}, bf16[16,24,128]{2,1,0:T(8,128)(2,1)S(1)}, u32[]{:S(2)}, u32[]{:S(2)}) collective-permute-start(bf16[16,24,128]{2,1,0:T(8,128)(2,1)} %own_ref.1), channel_id=1, source_target_pairs={{0,2},{2,0},{4,6},{6,4},{8,10},{10,8},{12,14},{14,12},{1,3},{3,1},... | collective-permute-start | bytes 294920 | tf_op jit(solution)/shard_map/ppermute | solution.py:383
  7.1 5.8 %collective-permute-start.2 = (bf16[16,24,128]{2,1,0:T(8,128)(2,1)}, bf16[16,24,128]{2,1,0:T(8,128)(2,1)S(1)}, u32[]{:S(2)}, u32[]{:S(2)}) collective-permute-start(bf16[16,24,128]{2,1,0:T(8,128)(2,1)} %own_ref.1), channel_id=1, source_target_pairs={{0,1},{1,0},{2,3},{3,2},{4,5},{5,4},{6,7},{7,6},{8,9},{9,8},{10,11... | collective-permute-start | bytes 294920 | tf_op jit(solution)/shard_map/ppermute | solution.py:383
  8.7 0.9 %copy-start = (bf16[16,24,128]{2,1,0:T(8,128)(2,1)S(1)}, bf16[16,24,128]{2,1,0:T(8,128)(2,1)}, u32[]{:S(2)}) copy-start(bf16[16,24,128]{2,1,0:T(8,128)(2,1)} %own_ref.1) | copy-start | bytes 294916
  9.6 0.7 copy-start.1
  12.2 1.5 %collective-permute-start.3 = (bf16[16,24,128]{2,1,0:T(8,128)(2,1)S(1)}, bf16[16,24,128]{2,1,0:T(8,128)(2,1)S(1)}, u32[]{:S(2)}, u32[]{:S(2)}) collective-permute-start(bf16[16,24,128]{2,1,0:T(8,128)(2,1)S(1)} %collective-permute-done.refs_2_), channel_id=1, source_target_pairs={{0,1},{1,0},{2,3},{3,2},{4,5},{5,4},{6,7},{7,6},{8,9},{9,8},{10,11... | collective-permute-start | bytes 294920 | tf_op jit(solution)/shard_map/ppermute | solution.py:383
  12.8 1.3 %collective-permute-start.4 = (bf16[16,24,128]{2,1,0:T(8,128)(2,1)S(1)}, bf16[16,24,128]{2,1,0:T(8,128)(2,1)S(1)}, u32[]{:S(2)}, u32[]{:S(2)}) collective-permute-start(bf16[16,24,128]{2,1,0:T(8,128)(2,1)S(1)} %collective-permute-done.1.refs_4_), channel_id=1, source_target_pairs={{0,1},{1,0},{2,3},{3,2},{4,5},{5,4},{6,7},{7,6},{8,9},{9,8},{10,11... | collective-permute-start | bytes 294920 | tf_op jit(solution)/shard_map/ppermute | solution.py:383
  32.4 5.6 %collective-permute-start.7 = (f32[32,128]{1,0:T(8,128)S(1)}, f32[32,128]{1,0:T(8,128)S(1)}, u32[]{:S(2)}, u32[]{:S(2)}) collective-permute-start(f32[32,128]{1,0:T(8,128)S(1)} %get-tuple-element.34), channel_id=1, source_target_pairs={{0,12},{1,13},{2,14},{3,15},{4,8},{5,9},{6,10},{7,11},{8,4},{9,5},... | collective-permute-start | bytes 49160 | tf_op jit(solution)/shard_map/ppermute | solution.py:401
  35.2 4.7 %collective-permute-start.6 = (f32[32,128]{1,0:T(8,128)S(1)}, f32[32,128]{1,0:T(8,128)S(1)}, u32[]{:S(2)}, u32[]{:S(2)}) collective-permute-start(f32[32,128]{1,0:T(8,128)S(1)} %get-tuple-element.34), channel_id=1, source_target_pairs={{0,8},{1,9},{2,10},{3,11},{4,12},{5,13},{6,14},{7,15},{8,0},{9,1},... | collective-permute-start | bytes 49160 | tf_op jit(solution)/shard_map/ppermute | solution.py:401
  35.5 4.4 %collective-permute-start.5 = (f32[32,128]{1,0:T(8,128)S(1)}, f32[32,128]{1,0:T(8,128)S(1)}, u32[]{:S(2)}, u32[]{:S(2)}) collective-permute-start(f32[32,128]{1,0:T(8,128)S(1)} %get-tuple-element.34), channel_id=1, source_target_pairs={{0,4},{1,5},{2,6},{3,7},{4,0},{5,1},{6,2},{7,3},{8,12},{9,13},{10,... | collective-permute-start | bytes 49160 | tf_op jit(solution)/shard_map/ppermute | solution.py:401
  39.9 3.2 %collective-permute-start.10 = (f32[32,128]{1,0:T(8,128)S(1)}, f32[32,128]{1,0:T(8,128)S(1)}, u32[]{:S(2)}, u32[]{:S(2)}) collective-permute-start(f32[32,128]{1,0:T(8,128)S(1)} %add_add_fusion.3), channel_id=1, source_target_pairs={{0,3},{1,2},{2,1},{3,0},{4,7},{5,6},{6,5},{7,4},{8,11},{9,10},{10,... | collective-permute-start | bytes 49160 | tf_op jit(solution)/shard_map/ppermute | solution.py:401
  40.0 3.8 %collective-permute-start.9 = (f32[32,128]{1,0:T(8,128)S(1)}, f32[32,128]{1,0:T(8,128)S(1)}, u32[]{:S(2)}, u32[]{:S(2)}) collective-permute-start(f32[32,128]{1,0:T(8,128)S(1)} %add_add_fusion.3), channel_id=1, source_target_pairs={{0,2},{1,3},{2,0},{3,1},{4,6},{5,7},{6,4},{7,5},{8,10},{9,11},{10,... | collective-permute-start | bytes 49160 | tf_op jit(solution)/shard_map/ppermute | solution.py:401
  41.3 2.5 %collective-permute-start.8 = (f32[32,128]{1,0:T(8,128)S(1)}, f32[32,128]{1,0:T(8,128)S(1)}, u32[]{:S(2)}, u32[]{:S(2)}) collective-permute-start(f32[32,128]{1,0:T(8,128)S(1)} %add_add_fusion.3), channel_id=1, source_target_pairs={{0,1},{1,0},{2,3},{3,2},{4,5},{5,4},{6,7},{7,6},{8,9},{9,8},{10,11... | collective-permute-start | bytes 49160 | tf_op jit(solution)/shard_map/ppermute | solution.py:401
  54.3 5.7 %collective-permute-start.13 = (f32[32,128]{1,0:T(8,128)S(1)}, f32[32,128]{1,0:T(8,128)S(1)}, u32[]{:S(2)}, u32[]{:S(2)}) collective-permute-start(f32[32,128]{1,0:T(8,128)S(1)} %get-tuple-element.36), channel_id=1, source_target_pairs={{0,12},{1,13},{2,14},{3,15},{4,8},{5,9},{6,10},{7,11},{8,4},{9,5},... | collective-permute-start | bytes 49160 | tf_op jit(solution)/shard_map/ppermute | solution.py:401
  56.2 4.7 %collective-permute-start.12 = (f32[32,128]{1,0:T(8,128)S(1)}, f32[32,128]{1,0:T(8,128)S(1)}, u32[]{:S(2)}, u32[]{:S(2)}) collective-permute-start(f32[32,128]{1,0:T(8,128)S(1)} %get-tuple-element.36), channel_id=1, source_target_pairs={{0,8},{1,9},{2,10},{3,11},{4,12},{5,13},{6,14},{7,15},{8,0},{9,1},... | collective-permute-start | bytes 49160 | tf_op jit(solution)/shard_map/ppermute | solution.py:401
  56.5 4.5 %collective-permute-start.11 = (f32[32,128]{1,0:T(8,128)S(1)}, f32[32,128]{1,0:T(8,128)S(1)}, u32[]{:S(2)}, u32[]{:S(2)}) collective-permute-start(f32[32,128]{1,0:T(8,128)S(1)} %get-tuple-element.36), channel_id=1, source_target_pairs={{0,4},{1,5},{2,6},{3,7},{4,0},{5,1},{6,2},{7,3},{8,12},{9,13},{10,... | collective-permute-start | bytes 49160 | tf_op jit(solution)/shard_map/ppermute | solution.py:401
  61.0 3.2 %collective-permute-start.16 = (f32[32,128]{1,0:T(8,128)S(1)}, f32[32,128]{1,0:T(8,128)S(1)}, u32[]{:S(2)}, u32[]{:S(2)}) collective-permute-start(f32[32,128]{1,0:T(8,128)S(1)} %add_add_fusion.1), channel_id=1, source_target_pairs={{0,3},{1,2},{2,1},{3,0},{4,7},{5,6},{6,5},{7,4},{8,11},{9,10},{10,... | collective-permute-start | bytes 49160 | tf_op jit(solution)/shard_map/ppermute | solution.py:401
  61.0 3.9 %collective-permute-start.15 = (f32[32,128]{1,0:T(8,128)S(1)}, f32[32,128]{1,0:T(8,128)S(1)}, u32[]{:S(2)}, u32[]{:S(2)}) collective-permute-start(f32[32,128]{1,0:T(8,128)S(1)} %add_add_fusion.1), channel_id=1, source_target_pairs={{0,2},{1,3},{2,0},{3,1},{4,6},{5,7},{6,4},{7,5},{8,10},{9,11},{10,... | collective-permute-start | bytes 49160 | tf_op jit(solution)/shard_map/ppermute | solution.py:401
  61.9 3.0 %collective-permute-start.14 = (f32[32,128]{1,0:T(8,128)S(1)}, f32[32,128]{1,0:T(8,128)S(1)}, u32[]{:S(2)}, u32[]{:S(2)}) collective-permute-start(f32[32,128]{1,0:T(8,128)S(1)} %add_add_fusion.1), channel_id=1, source_target_pairs={{0,1},{1,0},{2,3},{3,2},{4,5},{5,4},{6,7},{7,6},{8,9},{9,8},{10,11... | collective-permute-start | bytes 49160 | tf_op jit(solution)/shard_map/ppermute | solution.py:401

commit v4 on v3

--- a/solution.py
+++ b/solution.py
@@ -139,24 +139,26 @@
     return jnp.concatenate(groups, axis=0)[:, : 6 * slot].astype(jnp.bfloat16)
 
 
-def score_stage(features, matrix, data_ref, scores_ref, place, components):
+def split_features(features):
     both = jnp.concatenate([features, features * features], axis=0)
-    data = jnp.concatenate(split(both, 3), axis=0)
-    data_ref[:, place] = data[: data_ref.shape[0]]
+    return jnp.concatenate(split(both, 3), axis=0)
+
+
+def score_stage(data, matrix, scores_ref, place, components):
     scores = jnp.dot(matrix, data, preferred_element_type=jnp.float32)
     scores_ref[:, place] = sum(
         scores[k : k + components] for k in range(0, matrix.shape[0], components)
     )
 
 
-def moment_stage(data_ref, scores_ref, place):
+def moment_stage(data, scores_ref, place):
     scores = scores_ref[:, place]
     exponent = jnp.exp(scores - jnp.max(scores, axis=0, keepdims=True))
     shares = exponent * (1.0 / jnp.sum(exponent, axis=0, keepdims=True))
     high = shares.astype(jnp.bfloat16)
     low = (shares - high.astype(jnp.float32)).astype(jnp.bfloat16)
     sums = lax.dot_general(
-        data_ref[:, place],
+        data,
         jnp.concatenate([high, low], axis=0),
         (((1,), (1,)), ((), ())),
         preferred_element_type=jnp.float32,
@@ -183,7 +185,7 @@
     orients, samples, cols, rows, window, components, chunk, unit = dims
     halves, refs = refs[:6], refs[6:]
     time_ref, xline_ref, inline_ref, params_ref = refs[:4]
-    features_ref, sums_ref, traces, across_even, across_odd, total, data, scores = refs[4:]
+    split_ref, sums_ref, features_ref, traces, across_even, across_odd, total, data, scores = refs[4:]
     feats = 2 * orients
     slot = round_up(feats + 2, SUBLANES)
     twice = pl.program_id(0)
@@ -281,20 +283,30 @@
         )
         total[...] = jnp.zeros(total.shape, jnp.float32)
 
-        data[...] = jnp.zeros(data.shape, jnp.bfloat16)
-        scores[...] = jnp.zeros(scores.shape, jnp.float32)
-
-        @pl.loop(0, rows // unit + 1)
-        def _(step):
-            block = jnp.minimum(step, rows // unit - 1)
+
+        def sweep(block, moments, scoring):
             partial = jnp.zeros(total.shape, jnp.float32)
             for start in range(0, unit * cols, chunk):
                 place = slice(start * samples, (start + chunk) * samples)
-                partial = partial + moment_stage(data, scores, place)[1]
-                lines = gathered(features_ref, block * unit + start // cols, rows, start % cols, chunk, slot)
-                score_stage(lines, matrix, data, scores, place, components)
-            total[...] += partial
-
+                if moments:
+                    partial = partial + moment_stage(data[:, place], scores, place)[1]
+                if scoring:
+                    row = block * unit + start // cols
+                    lines = gathered(features_ref, row, rows, start % cols, chunk, slot)
+                    pieces = split_features(lines)
+                    data[:, place] = pieces[: data.shape[0]]
+                    split_ref[block, :, place] = pieces
+                    score_stage(pieces, matrix, scores, place, components)
+            if moments:
+                total[...] += partial
+
+        sweep(0, False, True)
+
+        @pl.loop(1, rows // unit)
+        def _(block):
+            sweep(block, True, True)
+
+        sweep(0, True, False)
         sums_ref[...] = fold_sums(total[...], components, slot)
 
 
@@ -311,12 +323,11 @@
 
 def posterior_kernel(dims, *refs):
     orients, samples, cols, rows, components, chunk, unit, cells = dims
-    features_ref, params_ref, before_ref = refs[:3]
-    posterior_ref, sums_ref, centers_ref, spreads_ref, matrix, total, turned, data, scores = refs[3:]
+    split_ref, params_ref, before_ref = refs[:3]
+    posterior_ref, sums_ref, centers_ref, spreads_ref, matrix, total, turned, scores = refs[3:]
     feats = 2 * orients
     slot = round_up(feats + 2, SUBLANES)
     step = pl.program_id(0)
-    block = jnp.minimum(step, rows // unit - 1)
 
     @pl.when(step == 0)
     def _():
@@ -333,27 +344,35 @@
         spreads_ref[...] = spreads
         matrix[...] = score_matrix(centers, spreads, jnp.log(weights), feats, slot, 2)
         total[...] = jnp.zeros(total.shape, jnp.float32)
-        data[...] = jnp.zeros(data.shape, jnp.bfloat16)
-        scores[...] = jnp.zeros(scores.shape, jnp.float32)
-
-    partial = jnp.zeros(total.shape, jnp.float32)
-    for start in range(0, unit * cols, chunk):
-        place = slice(start * samples, (start + chunk) * samples)
-        which, col = start // cols, start % cols
-        shares, sums = moment_stage(data, scores, place)
-        lines = gathered(features_ref, block * unit + which, rows, col, chunk, slot)
-        score_stage(lines, matrix[...], data, scores, place, components)
-        partial = partial + sums
-        for k in range(chunk):
-            turned[which, pl.ds(col + k, components, stride=cols + 1), :] = shares[
-                :, k * samples : (k + 1) * samples
-            ]
-    total[...] += partial
-    for which in range(unit):
-        for component in range(components):
-            posterior_ref[which, component] = turned[
-                which, pl.ds(component * (cols + 1), cols), :
-            ].astype(jnp.bfloat16)
+
+    def sweep(moments, scoring):
+        partial = jnp.zeros(total.shape, jnp.float32)
+        for start in range(0, unit * cols, chunk):
+            place = slice(start * samples, (start + chunk) * samples)
+            which, col = start // cols, start % cols
+            if moments:
+                before = split_ref[step - 1, : 4 * slot, place]
+                shares, sums = moment_stage(before, scores, place)
+            if scoring:
+                score_stage(split_ref[step, :, place], matrix[...], scores, place, components)
+            if moments:
+                partial = partial + sums
+                for k in range(chunk):
+                    turned[which, pl.ds(col + k, components, stride=cols + 1), :] = shares[
+                        :, k * samples : (k + 1) * samples
+                    ]
+        if moments:
+            total[...] += partial
+            for which in range(unit):
+                for component in range(components):
+                    posterior_ref[which, component] = turned[
+                        which, pl.ds(component * (cols + 1), cols), :
+                    ].astype(jnp.bfloat16)
+
+    last = rows // unit
+    pl.when(step == 0)(lambda: sweep(False, True))
+    pl.when((step > 0) & (step < last))(lambda: sweep(True, True))
+    pl.when(step == last)(lambda: sweep(True, False))
 
     @pl.when(step == pl.num_programs(0) - 1)
     def _():
@@ -459,13 +478,14 @@
     whole = lambda *shape: pl.BlockSpec(shape, lambda o: (0,) * len(shape))
     chunk = 6
     unit = 2 if rows % 2 == 0 else 1
-    features, sums = pl.pallas_call(
+    split_shape = (rows // unit, 6 * slot, unit * cols * samples)
+    pieces, sums = pl.pallas_call(
         functools.partial(
             features_kernel, (orients, samples, cols, rows, window, components, chunk, unit)
         ),
         grid=(orients // 2,),
         out_shape=(
-            jax.ShapeDtypeStruct((rows * cols * (slot + 1), samples), jnp.float32),
+            jax.ShapeDtypeStruct(split_shape, jnp.bfloat16),
             jax.ShapeDtypeStruct((components, LANES), jnp.float32),
         ),
         in_specs=[whole(rows, cols, samples)] * 6
@@ -475,8 +495,9 @@
             whole(orients, 2 * rows, 2 * window),
             whole(3 * components, LANES),
         ],
-        out_specs=(whole(rows * cols * (slot + 1), samples), whole(components, LANES)),
+        out_specs=(whole(*split_shape), whole(components, LANES)),
         scratch_shapes=[
+            pltpu.VMEM((rows * cols * (slot + 1), samples), jnp.float32),
             pltpu.VMEM((window * 2 * cols, samples), jnp.bfloat16),
             pltpu.VMEM((4 * cols * (window + 1), samples), jnp.float32),
             pltpu.VMEM((4 * cols * (window + 1), samples), jnp.float32),
@@ -484,7 +505,7 @@
             pltpu.VMEM((4 * slot, unit * cols * samples), jnp.bfloat16),
             pltpu.VMEM((components, unit * cols * samples), jnp.float32),
         ],
-        compiler_params=pltpu.CompilerParams(vmem_limit_bytes=40 * 2**20),
+        compiler_params=pltpu.CompilerParams(vmem_limit_bytes=28 * 2**20),
         name="features_and_first_moments",
     )(
         own, other, swap_one, swap_one_other, swap_two, swap_two_other,
@@ -505,7 +526,7 @@
             jax.ShapeDtypeStruct((components, LANES), jnp.float32),
         ),
         in_specs=[
-            whole(rows * cols * (slot + 1), samples),
+            whole(*split_shape),
             whole(3 * components, LANES),
             whole(components, LANES),
         ],
@@ -519,12 +540,11 @@
             pltpu.VMEM((2 * components, 6 * slot), jnp.bfloat16),
             pltpu.VMEM((4 * slot, 2 * components), jnp.float32),
             pltpu.VMEM((unit, components * (cols + 1), samples), jnp.float32),
-            pltpu.VMEM((4 * slot, unit * cols * samples), jnp.bfloat16),
             pltpu.VMEM((components, unit * cols * samples), jnp.float32),
         ],
-        compiler_params=pltpu.CompilerParams(vmem_limit_bytes=40 * 2**20),
+        compiler_params=pltpu.CompilerParams(vmem_limit_bytes=28 * 2**20),
         name="posterior_and_second_moments",
-    )(features, params, sums)
+    )(pieces, params, sums)
     sums = group_sum(sums)
     means, variances, weights = pl.pallas_call(
         functools.partial(update_kernel, (feats, slot, cells)),

time: 66 us -> 63 us (0.955)
  Pallas kernels: 30.9 us -> 27.9 us
    pallas_call x1, Pallas kernels: 10.5 us -> 7.71 us  [per_device(): pl.pallas_call(functools.partial(posterior_kernel, (orients, samples, col...]
where the time goes in v4:
time: 63 us; the launch traced here: 62.7 us
  Pallas kernels  27.9 us (44%)
  starting transfers between devices  19.7 us (31%)
  waiting for transfers between devices  10.4 us (17%)
  local copies, waits for them, and re-layouts  3.85 us (6%)
  between operations  0.7 us (1%)
    pallas_call x1, Pallas kernels, per_device(): pl.pallas_call(functools.partial(features_kernel, (orients, samples, cols...  18.2 us
    ppermute x12, starting transfers between devices, group_sum(): lax.ppermute(values, axes, [(i, i ^ step * d) for i in range(count)])  12.6 us
    ppermute x12, waiting for transfers between devices, group_sum(): lax.ppermute(values, axes, [(i, i ^ step * d) for i in range(count)])  9.27 us
    pallas_call x1, Pallas kernels, per_device(): pl.pallas_call(functools.partial(posterior_kernel, (orients, samples, col...  7.71 us
    ppermute x5, starting transfers between devices, exchange(): lax.ppermute(values, axis, [p for a, b in pairs for p in ((a, b), (b, a))])  7.07 us
    unnamed x6, local copies, waits for them, and re-layouts  3.11 us
    pallas_call x1, Pallas kernels, per_device(): pl.pallas_call(functools.partial(matrices_kernel, (orients, samples, cols...  1.27 us
  transfers between devices with their start and end apart: 17, of which 10 were waited for; matrix products, arithmetic and copies ran while one was open for 4% of the time, Pallas kernels for 2%

profile of v4, /device:TPU:0, one launch (start us, length us, event | category | flops | bytes accessed | tf_op | source)
XLA Modules:
  0.0 62.7 jit_solution(7170231004189869702)
XLA Ops:
  0.6 0.7 %collective-permute-start.1 = (bf16[16,24,128]{2,1,0:T(8,128)(2,1)}, bf16[16,24,128]{2,1,0:T(8,128)(2,1)S(1)}, u32[]{:S(2)}, u32[]{:S(2)}) collective-permute-start(bf16[16,24,128]{2,1,0:T(8,128)(2,1)} %own_ref.1), channel_id=1, source_target_pairs={{2,4},{4,2},{6,8},{8,6},{10,12},{12,10},{3,5},{5,3},{7,9},{9,7},{1... | collective-permute-start | bytes 294920 | tf_op jit(solution)/shard_map/ppermute | solution.py:402
  1.3 5.8 %collective-permute-start = (bf16[16,24,128]{2,1,0:T(8,128)(2,1)}, bf16[16,24,128]{2,1,0:T(8,128)(2,1)S(1)}, u32[]{:S(2)}, u32[]{:S(2)}) collective-permute-start(bf16[16,24,128]{2,1,0:T(8,128)(2,1)} %own_ref.1), channel_id=1, source_target_pairs={{0,2},{2,0},{4,6},{6,4},{8,10},{10,8},{12,14},{14,12},{1,3},{3,1},... | collective-permute-start | bytes 294920 | tf_op jit(solution)/shard_map/ppermute | solution.py:402
  7.1 0.0 collective-permute-start.2
  7.1 0.8 %copy.9 = f32[32,20]{1,0:T(8,128)S(1)} copy(f32[32,20]{0,1:T(8,128)} %param.7) | data formatting | bytes 5120 | tf_op args[2]
  7.9 0.8 %copy.10 = f32[32,20]{1,0:T(8,128)S(1)} copy(f32[32,20]{0,1:T(8,128)} %param.8) | data formatting | bytes 5120 | tf_op args[3]
  8.7 0.0 copy-start
  8.7 0.9 %copy-done = bf16[16,24,128]{2,1,0:T(8,128)(2,1)S(1)} copy-done((bf16[16,24,128]{2,1,0:T(8,128)(2,1)S(1)}, bf16[16,24,128]{2,1,0:T(8,128)(2,1)}, u32[]{:S(2)}) %copy-start) | copy-done | bytes 98328
  9.6 0.0 copy-start.1
  9.6 0.7 %copy-done.1 = s32[10]{0:T(128)S(1)} copy-done((s32[10]{0:T(128)S(1)}, s32[10]{0:T(128)}, u32[]{:S(2)}) %copy-start.1) | copy-done | bytes 64
  10.2 1.3 %filter_matrices.1 = (bf16[10,128,256]{2,1,0:T(8,128)(2,1)S(1)}, bf16[10,96,96]{2,1,0:T(8,128)(2,1)S(1)}, bf16[10,32,96]{2,1,0:T(8,128)(2,1)S(1)}, bf16[16,24,128]{2,1,0:T(8,128)(2,1)S(1)}) custom-call(s32[10]{0:T(128)S(1)} %copy-done.1, bf16[16,24,128]{2,1,0:T(8,128)(2,1)S(1)} %copy-done), custom_call_target="tpu_custom_call" | custom-call | bytes 4000000 | tf_op jit(solution)/shard_map/filter_matrices/pallas_call | solution.py:446
  11.5 0.7 %pad.11.clone = f32[96]{0:T(128)S(1)} pad(f32[32]{0:T(128)} %param.9, f32[]{:T(128)} %constant.8), padding=64_0 | pad | bytes 516 | tf_op jit(solution)/shard_map/concatenate | solution.py:470
  12.2 0.0 collective-permute-done.1.refs_4_
  12.2 0.0 collective-permute-done.refs_2_
  12.2 0.5 collective-permute-start.3
  12.8 0.1 collective-permute-start.4
  12.8 0.1 fusion.refs_9_.refs_1_
  12.9 0.0 collective-permute-done.2.refs_1_
  12.9 0.8 %collective-permute-done.3.refs_3_ = bf16[16,24,128]{2,1,0:T(8,128)(2,1)S(1)} collective-permute-done((bf16[16,24,128]{2,1,0:T(8,128)(2,1)S(1)}, bf16[16,24,128]{2,1,0:T(8,128)(2,1)S(1)}, u32[]{:S(2)}, u32[]{:S(2)}) %collective-permute-start.3) | collective-permute-done | bytes 98336 | tf_op jit(solution)/shard_map/ppermute | solution.py:402
  13.7 0.4 collective-permute-done.4.refs_5_
  14.1 18.2 %features_and_first_moments.1 = (bf16[8,144,6144]{2,1,0:T(8,128)(2,1)S(1)}, f32[32,128]{1,0:T(8,128)S(1)}) custom-call(bf16[16,24,128]{2,1,0:T(8,128)(2,1)S(1)} %get-tuple-element.27.refs_0_, bf16[16,24,128]{2,1,0:T(8,128)(2,1)S(1)} %collective-permute-done.2.refs_1_, bf16[16,24,128]{2,1,0:T(8,128)(2,1)S(1)} %collective-permute-done.refs_2_, ...), custom_call_target="tpu_custom_call" | custom-call | tf_op jit(solution)/shard_map/features_and_first_moments/pallas_call | solution.py:482
  32.3 2.8 %collective-permute-start.7 = (f32[32,128]{1,0:T(8,128)S(1)}, f32[32,128]{1,0:T(8,128)S(1)}, u32[]{:S(2)}, u32[]{:S(2)}) collective-permute-start(f32[32,128]{1,0:T(8,128)S(1)} %get-tuple-element.34), channel_id=1, source_target_pairs={{0,12},{1,13},{2,14},{3,15},{4,8},{5,9},{6,10},{7,11},{8,4},{9,5},... | collective-permute-start | bytes 49160 | tf_op jit(solution)/shard_map/ppermute | solution.py:420
  35.0 0.3 collective-permute-start.6
  35.3 1.3 %collective-permute-start.5 = (f32[32,128]{1,0:T(8,128)S(1)}, f32[32,128]{1,0:T(8,128)S(1)}, u32[]{:S(2)}, u32[]{:S(2)}) collective-permute-start(f32[32,128]{1,0:T(8,128)S(1)} %get-tuple-element.34), channel_id=1, source_target_pairs={{0,4},{1,5},{2,6},{3,7},{4,0},{5,1},{6,2},{7,3},{8,12},{9,13},{10,... | collective-permute-start | bytes 49160 | tf_op jit(solution)/shard_map/ppermute | solution.py:420
  36.7 1.2 %collective-permute-done.7 = f32[32,128]{1,0:T(8,128)S(1)} collective-permute-done((f32[32,128]{1,0:T(8,128)S(1)}, f32[32,128]{1,0:T(8,128)S(1)}, u32[]{:S(2)}, u32[]{:S(2)}) %collective-permute-start.7) | collective-permute-done | bytes 16416 | tf_op jit(solution)/shard_map/ppermute | solution.py:420
  37.8 1.8 %collective-permute-done.6 = f32[32,128]{1,0:T(8,128)S(1)} collective-permute-done((f32[32,128]{1,0:T(8,128)S(1)}, f32[32,128]{1,0:T(8,128)S(1)}, u32[]{:S(2)}, u32[]{:S(2)}) %collective-permute-start.6) | collective-permute-done | bytes 16416 | tf_op jit(solution)/shard_map/ppermute | solution.py:420
  39.7 0.0 collective-permute-done.5
  39.7 0.1 collective-permute-start.10
  39.8 1.3 %collective-permute-start.9 = (f32[32,128]{1,0:T(8,128)S(1)}, f32[32,128]{1,0:T(8,128)S(1)}, u32[]{:S(2)}, u32[]{:S(2)}) collective-permute-start(f32[32,128]{1,0:T(8,128)S(1)} %add_add_fusion.3), channel_id=1, source_target_pairs={{0,2},{1,3},{2,0},{3,1},{4,6},{5,7},{6,4},{7,5},{8,10},{9,11},{10,... | collective-permute-start | bytes 49160 | tf_op jit(solution)/shard_map/ppermute | solution.py:420
  41.1 0.5 collective-permute-start.8
  41.6 1.3 %collective-permute-done.10 = f32[32,128]{1,0:T(8,128)S(1)} collective-permute-done((f32[32,128]{1,0:T(8,128)S(1)}, f32[32,128]{1,0:T(8,128)S(1)}, u32[]{:S(2)}, u32[]{:S(2)}) %collective-permute-start.10) | collective-permute-done | bytes 16416 | tf_op jit(solution)/shard_map/ppermute | solution.py:420
  42.9 0.7 %collective-permute-done.9 = f32[32,128]{1,0:T(8,128)S(1)} collective-permute-done((f32[32,128]{1,0:T(8,128)S(1)}, f32[32,128]{1,0:T(8,128)S(1)}, u32[]{:S(2)}, u32[]{:S(2)}) %collective-permute-start.9) | collective-permute-done | bytes 16416 | tf_op jit(solution)/shard_map/ppermute | solution.py:420
  43.6 0.0 collective-permute-done.8
  43.6 7.7 %posterior_and_second_moments.1 = (bf16[16,32,24,128]{3,2,1,0:T(8,128)(2,1)}, f32[32,128]{1,0:T(8,128)S(1)}, f32[32,128]{1,0:T(8,128)S(1)}, f32[32,128]{1,0:T(8,128)S(1)}) custom-call(bf16[8,144,6144]{2,1,0:T(8,128)(2,1)S(1)} %get-tuple-element.33.refs_0_, f32[96,128]{1,0:T(8,128)S(1)} %fusion.refs_9_.refs_1_, f32[32,128]{1,0:T(8,128)S(1)} %add_add_fusion.2.refs_2_), custom_call_target="tpu_custom_call" | custom-call | tf_op jit(solution)/shard_map/posterior_and_second_moments/pallas_call | solution.py:517
  51.3 1.9 %collective-permute-start.13 = (f32[32,128]{1,0:T(8,128)S(1)}, f32[32,128]{1,0:T(8,128)S(1)}, u32[]{:S(2)}, u32[]{:S(2)}) collective-permute-start(f32[32,128]{1,0:T(8,128)S(1)} %get-tuple-element.36), channel_id=1, source_target_pairs={{0,12},{1,13},{2,14},{3,15},{4,8},{5,9},{6,10},{7,11},{8,4},{9,5},... | collective-permute-start | bytes 49160 | tf_op jit(solution)/shard_map/ppermute | solution.py:420
  53.2 0.3 collective-permute-start.12
  53.5 2.2 %collective-permute-start.11 = (f32[32,128]{1,0:T(8,128)S(1)}, f32[32,128]{1,0:T(8,128)S(1)}, u32[]{:S(2)}, u32[]{:S(2)}) collective-permute-start(f32[32,128]{1,0:T(8,128)S(1)} %get-tuple-element.36), channel_id=1, source_target_pairs={{0,4},{1,5},{2,6},{3,7},{4,0},{5,1},{6,2},{7,3},{8,12},{9,13},{10,... | collective-permute-start | bytes 49160 | tf_op jit(solution)/shard_map/ppermute | solution.py:420
  55.7 1.3 %collective-permute-done.13 = f32[32,128]{1,0:T(8,128)S(1)} collective-permute-done((f32[32,128]{1,0:T(8,128)S(1)}, f32[32,128]{1,0:T(8,128)S(1)}, u32[]{:S(2)}, u32[]{:S(2)}) %collective-permute-start.13) | collective-permute-done | bytes 16416 | tf_op jit(solution)/shard_map/ppermute | solution.py:420
  57.0 1.0 %collective-permute-done.12 = f32[32,128]{1,0:T(8,128)S(1)} collective-permute-done((f32[32,128]{1,0:T(8,128)S(1)}, f32[32,128]{1,0:T(8,128)S(1)}, u32[]{:S(2)}, u32[]{:S(2)}) %collective-permute-start.12) | collective-permute-done | bytes 16416 | tf_op jit(solution)/shard_map/ppermute | solution.py:420
  58.0 0.0 collective-permute-done.11
  58.0 0.1 collective-permute-start.16
  58.1 0.9 %collective-permute-start.15 = (f32[32,128]{1,0:T(8,128)S(1)}, f32[32,128]{1,0:T(8,128)S(1)}, u32[]{:S(2)}, u32[]{:S(2)}) collective-permute-start(f32[32,128]{1,0:T(8,128)S(1)} %add_add_fusion.1), channel_id=1, source_target_pairs={{0,2},{1,3},{2,0},{3,1},{4,6},{5,7},{6,4},{7,5},{8,10},{9,11},{10,... | collective-permute-start | bytes 49160 | tf_op jit(solution)/shard_map/ppermute | solution.py:420
  59.0 1.0 %collective-permute-start.14 = (f32[32,128]{1,0:T(8,128)S(1)}, f32[32,128]{1,0:T(8,128)S(1)}, u32[]{:S(2)}, u32[]{:S(2)}) collective-permute-start(f32[32,128]{1,0:T(8,128)S(1)} %add_add_fusion.1), channel_id=1, source_target_pairs={{0,1},{1,0},{2,3},{3,2},{4,5},{5,4},{6,7},{7,6},{8,9},{9,8},{10,11... | collective-permute-start | bytes 49160 | tf_op jit(solution)/shard_map/ppermute | solution.py:420
  59.9 1.3 %collective-permute-done.16 = f32[32,128]{1,0:T(8,128)S(1)} collective-permute-done((f32[32,128]{1,0:T(8,128)S(1)}, f32[32,128]{1,0:T(8,128)S(1)}, u32[]{:S(2)}, u32[]{:S(2)}) %collective-permute-start.16) | collective-permute-done | bytes 16416 | tf_op jit(solution)/shard_map/ppermute | solution.py:420
  61.2 0.7 %collective-permute-done.15 = f32[32,128]{1,0:T(8,128)S(1)} collective-permute-done((f32[32,128]{1,0:T(8,128)S(1)}, f32[32,128]{1,0:T(8,128)S(1)}, u32[]{:S(2)}, u32[]{:S(2)}) %collective-permute-start.15) | collective-permute-done | bytes 16416 | tf_op jit(solution)/shard_map/ppermute | solution.py:420
  61.9 0.0 collective-permute-done.14
  62.0 0.8 %last_update.1 = (f32[20,32]{1,0:T(8,128)}, f32[20,32]{1,0:T(8,128)}, f32[1,32]{1,0:T(1,128)}) custom-call(f32[32,128]{1,0:T(8,128)S(1)} %add_add_fusion.sums_ref, f32[32,128]{1,0:T(8,128)S(1)} %get-tuple-element.37.centers_ref, f32[32,128]{1,0:T(8,128)S(1)} %get-tuple-element.38.spreads_ref), custom_call_target="tpu_custom_call" | custom-call | tf_op jit(solution)/shard_map/last_update/pallas_call | solution.py:549
  (4 shorter events, 0.0 us)
Async XLA Ops:
  0.6 11.6 %collective-permute-start.1 = (bf16[16,24,128]{2,1,0:T(8,128)(2,1)}, bf16[16,24,128]{2,1,0:T(8,128)(2,1)S(1)}, u32[]{:S(2)}, u32[]{:S(2)}) collective-permute-start(bf16[16,24,128]{2,1,0:T(8,128)(2,1)} %own_ref.1), channel_id=1, source_target_pairs={{2,4},{4,2},{6,8},{8,6},{10,12},{12,10},{3,5},{5,3},{7,9},{9,7},{1... | collective-permute-start | bytes 294920 | tf_op jit(solution)/shard_map/ppermute | solution.py:402
  1.3 10.9 %collective-permute-start = (bf16[16,24,128]{2,1,0:T(8,128)(2,1)}, bf16[16,24,128]{2,1,0:T(8,128)(2,1)S(1)}, u32[]{:S(2)}, u32[]{:S(2)}) collective-permute-start(bf16[16,24,128]{2,1,0:T(8,128)(2,1)} %own_ref.1), channel_id=1, source_target_pairs={{0,2},{2,0},{4,6},{6,4},{8,10},{10,8},{12,14},{14,12},{1,3},{3,1},... | collective-permute-start | bytes 294920 | tf_op jit(solution)/shard_map/ppermute | solution.py:402
  7.1 5.8 %collective-permute-start.2 = (bf16[16,24,128]{2,1,0:T(8,128)(2,1)}, bf16[16,24,128]{2,1,0:T(8,128)(2,1)S(1)}, u32[]{:S(2)}, u32[]{:S(2)}) collective-permute-start(bf16[16,24,128]{2,1,0:T(8,128)(2,1)} %own_ref.1), channel_id=1, source_target_pairs={{0,1},{1,0},{2,3},{3,2},{4,5},{5,4},{6,7},{7,6},{8,9},{9,8},{10,11... | collective-permute-start | bytes 294920 | tf_op jit(solution)/shard_map/ppermute | solution.py:402
  8.7 0.9 %copy-start = (bf16[16,24,128]{2,1,0:T(8,128)(2,1)S(1)}, bf16[16,24,128]{2,1,0:T(8,128)(2,1)}, u32[]{:S(2)}) copy-start(bf16[16,24,128]{2,1,0:T(8,128)(2,1)} %own_ref.1) | copy-start | bytes 294916
  9.6 0.7 %copy-start.1 = (s32[10]{0:T(128)S(1)}, s32[10]{0:T(128)}, u32[]{:S(2)}) copy-start(s32[10]{0:T(128)} %directions_ref.1) | copy-start | bytes 124
  12.2 1.5 %collective-permute-start.3 = (bf16[16,24,128]{2,1,0:T(8,128)(2,1)S(1)}, bf16[16,24,128]{2,1,0:T(8,128)(2,1)S(1)}, u32[]{:S(2)}, u32[]{:S(2)}) collective-permute-start(bf16[16,24,128]{2,1,0:T(8,128)(2,1)S(1)} %collective-permute-done.refs_2_), channel_id=1, source_target_pairs={{0,1},{1,0},{2,3},{3,2},{4,5},{5,4},{6,7},{7,6},{8,9},{9,8},{10,11... | collective-permute-start | bytes 294920 | tf_op jit(solution)/shard_map/ppermute | solution.py:402
  12.8 1.3 %collective-permute-start.4 = (bf16[16,24,128]{2,1,0:T(8,128)(2,1)S(1)}, bf16[16,24,128]{2,1,0:T(8,128)(2,1)S(1)}, u32[]{:S(2)}, u32[]{:S(2)}) collective-permute-start(bf16[16,24,128]{2,1,0:T(8,128)(2,1)S(1)} %collective-permute-done.1.refs_4_), channel_id=1, source_target_pairs={{0,1},{1,0},{2,3},{3,2},{4,5},{5,4},{6,7},{7,6},{8,9},{9,8},{10,11... | collective-permute-start | bytes 294920 | tf_op jit(solution)/shard_map/ppermute | solution.py:402
  32.3 5.6 %collective-permute-start.7 = (f32[32,128]{1,0:T(8,128)S(1)}, f32[32,128]{1,0:T(8,128)S(1)}, u32[]{:S(2)}, u32[]{:S(2)}) collective-permute-start(f32[32,128]{1,0:T(8,128)S(1)} %get-tuple-element.34), channel_id=1, source_target_pairs={{0,12},{1,13},{2,14},{3,15},{4,8},{5,9},{6,10},{7,11},{8,4},{9,5},... | collective-permute-start | bytes 49160 | tf_op jit(solution)/shard_map/ppermute | solution.py:420
  35.0 4.7 %collective-permute-start.6 = (f32[32,128]{1,0:T(8,128)S(1)}, f32[32,128]{1,0:T(8,128)S(1)}, u32[]{:S(2)}, u32[]{:S(2)}) collective-permute-start(f32[32,128]{1,0:T(8,128)S(1)} %get-tuple-element.34), channel_id=1, source_target_pairs={{0,8},{1,9},{2,10},{3,11},{4,12},{5,13},{6,14},{7,15},{8,0},{9,1},... | collective-permute-start | bytes 49160 | tf_op jit(solution)/shard_map/ppermute | solution.py:420
  35.3 4.4 %collective-permute-start.5 = (f32[32,128]{1,0:T(8,128)S(1)}, f32[32,128]{1,0:T(8,128)S(1)}, u32[]{:S(2)}, u32[]{:S(2)}) collective-permute-start(f32[32,128]{1,0:T(8,128)S(1)} %get-tuple-element.34), channel_id=1, source_target_pairs={{0,4},{1,5},{2,6},{3,7},{4,0},{5,1},{6,2},{7,3},{8,12},{9,13},{10,... | collective-permute-start | bytes 49160 | tf_op jit(solution)/shard_map/ppermute | solution.py:420
  39.7 3.2 %collective-permute-start.10 = (f32[32,128]{1,0:T(8,128)S(1)}, f32[32,128]{1,0:T(8,128)S(1)}, u32[]{:S(2)}, u32[]{:S(2)}) collective-permute-start(f32[32,128]{1,0:T(8,128)S(1)} %add_add_fusion.3), channel_id=1, source_target_pairs={{0,3},{1,2},{2,1},{3,0},{4,7},{5,6},{6,5},{7,4},{8,11},{9,10},{10,... | collective-permute-start | bytes 49160 | tf_op jit(solution)/shard_map/ppermute | solution.py:420
  39.8 3.8 %collective-permute-start.9 = (f32[32,128]{1,0:T(8,128)S(1)}, f32[32,128]{1,0:T(8,128)S(1)}, u32[]{:S(2)}, u32[]{:S(2)}) collective-permute-start(f32[32,128]{1,0:T(8,128)S(1)} %add_add_fusion.3), channel_id=1, source_target_pairs={{0,2},{1,3},{2,0},{3,1},{4,6},{5,7},{6,4},{7,5},{8,10},{9,11},{10,... | collective-permute-start | bytes 49160 | tf_op jit(solution)/shard_map/ppermute | solution.py:420
  41.1 2.5 %collective-permute-start.8 = (f32[32,128]{1,0:T(8,128)S(1)}, f32[32,128]{1,0:T(8,128)S(1)}, u32[]{:S(2)}, u32[]{:S(2)}) collective-permute-start(f32[32,128]{1,0:T(8,128)S(1)} %add_add_fusion.3), channel_id=1, source_target_pairs={{0,1},{1,0},{2,3},{3,2},{4,5},{5,4},{6,7},{7,6},{8,9},{9,8},{10,11... | collective-permute-start | bytes 49160 | tf_op jit(solution)/shard_map/ppermute | solution.py:420
  51.3 5.7 %collective-permute-start.13 = (f32[32,128]{1,0:T(8,128)S(1)}, f32[32,128]{1,0:T(8,128)S(1)}, u32[]{:S(2)}, u32[]{:S(2)}) collective-permute-start(f32[32,128]{1,0:T(8,128)S(1)} %get-tuple-element.36), channel_id=1, source_target_pairs={{0,12},{1,13},{2,14},{3,15},{4,8},{5,9},{6,10},{7,11},{8,4},{9,5},... | collective-permute-start | bytes 49160 | tf_op jit(solution)/shard_map/ppermute | solution.py:420
  53.2 4.7 %collective-permute-start.12 = (f32[32,128]{1,0:T(8,128)S(1)}, f32[32,128]{1,0:T(8,128)S(1)}, u32[]{:S(2)}, u32[]{:S(2)}) collective-permute-start(f32[32,128]{1,0:T(8,128)S(1)} %get-tuple-element.36), channel_id=1, source_target_pairs={{0,8},{1,9},{2,10},{3,11},{4,12},{5,13},{6,14},{7,15},{8,0},{9,1},... | collective-permute-start | bytes 49160 | tf_op jit(solution)/shard_map/ppermute | solution.py:420
  53.5 4.5 %collective-permute-start.11 = (f32[32,128]{1,0:T(8,128)S(1)}, f32[32,128]{1,0:T(8,128)S(1)}, u32[]{:S(2)}, u32[]{:S(2)}) collective-permute-start(f32[32,128]{1,0:T(8,128)S(1)} %get-tuple-element.36), channel_id=1, source_target_pairs={{0,4},{1,5},{2,6},{3,7},{4,0},{5,1},{6,2},{7,3},{8,12},{9,13},{10,... | collective-permute-start | bytes 49160 | tf_op jit(solution)/shard_map/ppermute | solution.py:420
  58.0 3.2 %collective-permute-start.16 = (f32[32,128]{1,0:T(8,128)S(1)}, f32[32,128]{1,0:T(8,128)S(1)}, u32[]{:S(2)}, u32[]{:S(2)}) collective-permute-start(f32[32,128]{1,0:T(8,128)S(1)} %add_add_fusion.1), channel_id=1, source_target_pairs={{0,3},{1,2},{2,1},{3,0},{4,7},{5,6},{6,5},{7,4},{8,11},{9,10},{10,... | collective-permute-start | bytes 49160 | tf_op jit(solution)/shard_map/ppermute | solution.py:420
  58.1 3.9 %collective-permute-start.15 = (f32[32,128]{1,0:T(8,128)S(1)}, f32[32,128]{1,0:T(8,128)S(1)}, u32[]{:S(2)}, u32[]{:S(2)}) collective-permute-start(f32[32,128]{1,0:T(8,128)S(1)} %add_add_fusion.1), channel_id=1, source_target_pairs={{0,2},{1,3},{2,0},{3,1},{4,6},{5,7},{6,4},{7,5},{8,10},{9,11},{10,... | collective-permute-start | bytes 49160 | tf_op jit(solution)/shard_map/ppermute | solution.py:420
  59.0 3.0 %collective-permute-start.14 = (f32[32,128]{1,0:T(8,128)S(1)}, f32[32,128]{1,0:T(8,128)S(1)}, u32[]{:S(2)}, u32[]{:S(2)}) collective-permute-start(f32[32,128]{1,0:T(8,128)S(1)} %add_add_fusion.1), channel_id=1, source_target_pairs={{0,1},{1,0},{2,3},{3,2},{4,5},{5,4},{6,7},{7,6},{8,9},{9,8},{10,11... | collective-permute-start | bytes 49160 | tf_op jit(solution)/shard_map/ppermute | solution.py:420

commit v5 on v4

--- a/solution.py
+++ b/solution.py
@@ -477,7 +477,7 @@
     )
     whole = lambda *shape: pl.BlockSpec(shape, lambda o: (0,) * len(shape))
     chunk = 6
-    unit = 2 if rows % 2 == 0 else 1
+    unit = next(count for count in (8, 4, 2, 1) if rows % count == 0)
     split_shape = (rows // unit, 6 * slot, unit * cols * samples)
     pieces, sums = pl.pallas_call(
         functools.partial(

time: 63 us -> 60.9 us (0.967)
  Pallas kernels: 27.9 us -> 25.8 us
    pallas_call x1, Pallas kernels: 18.2 us -> 16.4 us  [per_device(): pl.pallas_call(functools.partial(features_kernel, (orients, samples, cols...]
where the time goes in v5:
time: 60.9 us; the launch traced here: 60.6 us
  Pallas kernels  25.8 us (42%)
  starting transfers between devices  19.7 us (32%)
  waiting for transfers between devices  10.4 us (17%)
  local copies, waits for them, and re-layouts  3.85 us (6%)
  between operations  0.7 us (1%)
    pallas_call x1, Pallas kernels, per_device(): pl.pallas_call(functools.partial(features_kernel, (orients, samples, cols...  16.4 us
    ppermute x12, starting transfers between devices, group_sum(): lax.ppermute(values, axes, [(i, i ^ step * d) for i in range(count)])  12.6 us
    ppermute x12, waiting for transfers between devices, group_sum(): lax.ppermute(values, axes, [(i, i ^ step * d) for i in range(count)])  9.27 us
    pallas_call x1, Pallas kernels, per_device(): pl.pallas_call(functools.partial(posterior_kernel, (orients, samples, col...  7.43 us
    ppermute x5, starting transfers between devices, exchange(): lax.ppermute(values, axis, [p for a, b in pairs for p in ((a, b), (b, a))])  7.07 us
    unnamed x6, local copies, waits for them, and re-layouts  3.11 us
    pallas_call x1, Pallas kernels, per_device(): pl.pallas_call(functools.partial(matrices_kernel, (orients, samples, cols...  1.27 us
  transfers between devices with their start and end apart: 17, of which 10 were waited for; matrix products, arithmetic and copies ran while one was open for 4% of the time, Pallas kernels for 2%

profile of v5, /device:TPU:0, one launch (start us, length us, event | category | flops | bytes accessed | tf_op | source)
XLA Modules:
  0.0 60.6 jit_solution(1752175929564165584)
XLA Ops:
  0.6 0.7 %collective-permute-start.1 = (bf16[16,24,128]{2,1,0:T(8,128)(2,1)}, bf16[16,24,128]{2,1,0:T(8,128)(2,1)S(1)}, u32[]{:S(2)}, u32[]{:S(2)}) collective-permute-start(bf16[16,24,128]{2,1,0:T(8,128)(2,1)} %own_ref.1), channel_id=1, source_target_pairs={{2,4},{4,2},{6,8},{8,6},{10,12},{12,10},{3,5},{5,3},{7,9},{9,7},{1... | collective-permute-start | bytes 294920 | tf_op jit(solution)/shard_map/ppermute | solution.py:402
  1.3 5.8 %collective-permute-start = (bf16[16,24,128]{2,1,0:T(8,128)(2,1)}, bf16[16,24,128]{2,1,0:T(8,128)(2,1)S(1)}, u32[]{:S(2)}, u32[]{:S(2)}) collective-permute-start(bf16[16,24,128]{2,1,0:T(8,128)(2,1)} %own_ref.1), channel_id=1, source_target_pairs={{0,2},{2,0},{4,6},{6,4},{8,10},{10,8},{12,14},{14,12},{1,3},{3,1},... | collective-permute-start | bytes 294920 | tf_op jit(solution)/shard_map/ppermute | solution.py:402
  7.1 0.0 collective-permute-start.2
  7.1 0.8 %copy.9 = f32[32,20]{1,0:T(8,128)S(1)} copy(f32[32,20]{0,1:T(8,128)} %param.7) | data formatting | bytes 5120 | tf_op args[2]
  7.9 0.8 %copy.10 = f32[32,20]{1,0:T(8,128)S(1)} copy(f32[32,20]{0,1:T(8,128)} %param.8) | data formatting | bytes 5120 | tf_op args[3]
  8.7 0.0 copy-start
  8.7 0.9 %copy-done = bf16[16,24,128]{2,1,0:T(8,128)(2,1)S(1)} copy-done((bf16[16,24,128]{2,1,0:T(8,128)(2,1)S(1)}, bf16[16,24,128]{2,1,0:T(8,128)(2,1)}, u32[]{:S(2)}) %copy-start) | copy-done | bytes 98328
  9.6 0.0 copy-start.1
  9.6 0.7 %copy-done.1 = s32[10]{0:T(128)S(1)} copy-done((s32[10]{0:T(128)S(1)}, s32[10]{0:T(128)}, u32[]{:S(2)}) %copy-start.1) | copy-done | bytes 64
  10.2 1.3 %filter_matrices.1 = (bf16[10,128,256]{2,1,0:T(8,128)(2,1)S(1)}, bf16[10,96,96]{2,1,0:T(8,128)(2,1)S(1)}, bf16[10,32,96]{2,1,0:T(8,128)(2,1)S(1)}, bf16[16,24,128]{2,1,0:T(8,128)(2,1)S(1)}) custom-call(s32[10]{0:T(128)S(1)} %copy-done.1, bf16[16,24,128]{2,1,0:T(8,128)(2,1)S(1)} %copy-done), custom_call_target="tpu_custom_call" | custom-call | bytes 4000000 | tf_op jit(solution)/shard_map/filter_matrices/pallas_call | solution.py:446
  11.5 0.7 %pad.11.clone = f32[96]{0:T(128)S(1)} pad(f32[32]{0:T(128)} %param.9, f32[]{:T(128)} %constant.8), padding=64_0 | pad | bytes 516 | tf_op jit(solution)/shard_map/concatenate | solution.py:470
  12.2 0.0 collective-permute-done.1.refs_4_
  12.2 0.0 collective-permute-done.refs_2_
  12.2 0.5 collective-permute-start.3
  12.8 0.1 collective-permute-start.4
  12.8 0.1 fusion.refs_9_.refs_1_
  12.9 0.0 collective-permute-done.2.refs_1_
  12.9 0.8 %collective-permute-done.3.refs_3_ = bf16[16,24,128]{2,1,0:T(8,128)(2,1)S(1)} collective-permute-done((bf16[16,24,128]{2,1,0:T(8,128)(2,1)S(1)}, bf16[16,24,128]{2,1,0:T(8,128)(2,1)S(1)}, u32[]{:S(2)}, u32[]{:S(2)}) %collective-permute-start.3) | collective-permute-done | bytes 98336 | tf_op jit(solution)/shard_map/ppermute | solution.py:402
  13.7 0.4 collective-permute-done.4.refs_5_
  14.1 16.4 %features_and_first_moments.1 = (bf16[2,144,24576]{2,1,0:T(8,128)(2,1)S(1)}, f32[32,128]{1,0:T(8,128)S(1)}) custom-call(bf16[16,24,128]{2,1,0:T(8,128)(2,1)S(1)} %get-tuple-element.27.refs_0_, bf16[16,24,128]{2,1,0:T(8,128)(2,1)S(1)} %collective-permute-done.2.refs_1_, bf16[16,24,128]{2,1,0:T(8,128)(2,1)S(1)} %collective-permute-done.refs_2_, ...), custom_call_target="tpu_custom_call" | custom-call | tf_op jit(solution)/shard_map/features_and_first_moments/pallas_call | solution.py:482
  30.4 2.8 %collective-permute-start.7 = (f32[32,128]{1,0:T(8,128)S(1)}, f32[32,128]{1,0:T(8,128)S(1)}, u32[]{:S(2)}, u32[]{:S(2)}) collective-permute-start(f32[32,128]{1,0:T(8,128)S(1)} %get-tuple-element.34), channel_id=1, source_target_pairs={{0,12},{1,13},{2,14},{3,15},{4,8},{5,9},{6,10},{7,11},{8,4},{9,5},... | collective-permute-start | bytes 49160 | tf_op jit(solution)/shard_map/ppermute | solution.py:420
  33.2 0.3 collective-permute-start.6
  33.5 1.3 %collective-permute-start.5 = (f32[32,128]{1,0:T(8,128)S(1)}, f32[32,128]{1,0:T(8,128)S(1)}, u32[]{:S(2)}, u32[]{:S(2)}) collective-permute-start(f32[32,128]{1,0:T(8,128)S(1)} %get-tuple-element.34), channel_id=1, source_target_pairs={{0,4},{1,5},{2,6},{3,7},{4,0},{5,1},{6,2},{7,3},{8,12},{9,13},{10,... | collective-permute-start | bytes 49160 | tf_op jit(solution)/shard_map/ppermute | solution.py:420
  34.9 1.2 %collective-permute-done.7 = f32[32,128]{1,0:T(8,128)S(1)} collective-permute-done((f32[32,128]{1,0:T(8,128)S(1)}, f32[32,128]{1,0:T(8,128)S(1)}, u32[]{:S(2)}, u32[]{:S(2)}) %collective-permute-start.7) | collective-permute-done | bytes 16416 | tf_op jit(solution)/shard_map/ppermute | solution.py:420
  36.0 1.9 %collective-permute-done.6 = f32[32,128]{1,0:T(8,128)S(1)} collective-permute-done((f32[32,128]{1,0:T(8,128)S(1)}, f32[32,128]{1,0:T(8,128)S(1)}, u32[]{:S(2)}, u32[]{:S(2)}) %collective-permute-start.6) | collective-permute-done | bytes 16416 | tf_op jit(solution)/shard_map/ppermute | solution.py:420
  37.9 0.0 collective-permute-done.5
  37.9 0.1 collective-permute-start.10
  38.0 1.3 %collective-permute-start.9 = (f32[32,128]{1,0:T(8,128)S(1)}, f32[32,128]{1,0:T(8,128)S(1)}, u32[]{:S(2)}, u32[]{:S(2)}) collective-permute-start(f32[32,128]{1,0:T(8,128)S(1)} %add_add_fusion.3), channel_id=1, source_target_pairs={{0,2},{1,3},{2,0},{3,1},{4,6},{5,7},{6,4},{7,5},{8,10},{9,11},{10,... | collective-permute-start | bytes 49160 | tf_op jit(solution)/shard_map/ppermute | solution.py:420
  39.3 0.6 collective-permute-start.8
  39.8 1.3 %collective-permute-done.10 = f32[32,128]{1,0:T(8,128)S(1)} collective-permute-done((f32[32,128]{1,0:T(8,128)S(1)}, f32[32,128]{1,0:T(8,128)S(1)}, u32[]{:S(2)}, u32[]{:S(2)}) %collective-permute-start.10) | collective-permute-done | bytes 16416 | tf_op jit(solution)/shard_map/ppermute | solution.py:420
  41.1 0.7 %collective-permute-done.9 = f32[32,128]{1,0:T(8,128)S(1)} collective-permute-done((f32[32,128]{1,0:T(8,128)S(1)}, f32[32,128]{1,0:T(8,128)S(1)}, u32[]{:S(2)}, u32[]{:S(2)}) %collective-permute-start.9) | collective-permute-done | bytes 16416 | tf_op jit(solution)/shard_map/ppermute | solution.py:420
  41.8 0.0 collective-permute-done.8
  41.8 7.4 %posterior_and_second_moments.1 = (bf16[16,32,24,128]{3,2,1,0:T(8,128)(2,1)}, f32[32,128]{1,0:T(8,128)S(1)}, f32[32,128]{1,0:T(8,128)S(1)}, f32[32,128]{1,0:T(8,128)S(1)}) custom-call(bf16[2,144,24576]{2,1,0:T(8,128)(2,1)S(1)} %get-tuple-element.33.refs_0_, f32[96,128]{1,0:T(8,128)S(1)} %fusion.refs_9_.refs_1_, f32[32,128]{1,0:T(8,128)S(1)} %add_add_fusion.2.refs_2_), custom_call_target="tpu_custom_call" | custom-call | tf_op jit(solution)/shard_map/posterior_and_second_moments/pallas_call | solution.py:517
  49.2 1.9 %collective-permute-start.13 = (f32[32,128]{1,0:T(8,128)S(1)}, f32[32,128]{1,0:T(8,128)S(1)}, u32[]{:S(2)}, u32[]{:S(2)}) collective-permute-start(f32[32,128]{1,0:T(8,128)S(1)} %get-tuple-element.36), channel_id=1, source_target_pairs={{0,12},{1,13},{2,14},{3,15},{4,8},{5,9},{6,10},{7,11},{8,4},{9,5},... | collective-permute-start | bytes 49160 | tf_op jit(solution)/shard_map/ppermute | solution.py:420
  51.1 0.2 collective-permute-start.12
  51.4 2.2 %collective-permute-start.11 = (f32[32,128]{1,0:T(8,128)S(1)}, f32[32,128]{1,0:T(8,128)S(1)}, u32[]{:S(2)}, u32[]{:S(2)}) collective-permute-start(f32[32,128]{1,0:T(8,128)S(1)} %get-tuple-element.36), channel_id=1, source_target_pairs={{0,4},{1,5},{2,6},{3,7},{4,0},{5,1},{6,2},{7,3},{8,12},{9,13},{10,... | collective-permute-start | bytes 49160 | tf_op jit(solution)/shard_map/ppermute | solution.py:420
  53.6 1.3 %collective-permute-done.13 = f32[32,128]{1,0:T(8,128)S(1)} collective-permute-done((f32[32,128]{1,0:T(8,128)S(1)}, f32[32,128]{1,0:T(8,128)S(1)}, u32[]{:S(2)}, u32[]{:S(2)}) %collective-permute-start.13) | collective-permute-done | bytes 16416 | tf_op jit(solution)/shard_map/ppermute | solution.py:420
  54.9 1.0 %collective-permute-done.12 = f32[32,128]{1,0:T(8,128)S(1)} collective-permute-done((f32[32,128]{1,0:T(8,128)S(1)}, f32[32,128]{1,0:T(8,128)S(1)}, u32[]{:S(2)}, u32[]{:S(2)}) %collective-permute-start.12) | collective-permute-done | bytes 16416 | tf_op jit(solution)/shard_map/ppermute | solution.py:420
  55.9 0.0 collective-permute-done.11
  55.9 0.1 collective-permute-start.16
  56.0 0.9 %collective-permute-start.15 = (f32[32,128]{1,0:T(8,128)S(1)}, f32[32,128]{1,0:T(8,128)S(1)}, u32[]{:S(2)}, u32[]{:S(2)}) collective-permute-start(f32[32,128]{1,0:T(8,128)S(1)} %add_add_fusion.1), channel_id=1, source_target_pairs={{0,2},{1,3},{2,0},{3,1},{4,6},{5,7},{6,4},{7,5},{8,10},{9,11},{10,... | collective-permute-start | bytes 49160 | tf_op jit(solution)/shard_map/ppermute | solution.py:420
  56.9 0.9 %collective-permute-start.14 = (f32[32,128]{1,0:T(8,128)S(1)}, f32[32,128]{1,0:T(8,128)S(1)}, u32[]{:S(2)}, u32[]{:S(2)}) collective-permute-start(f32[32,128]{1,0:T(8,128)S(1)} %add_add_fusion.1), channel_id=1, source_target_pairs={{0,1},{1,0},{2,3},{3,2},{4,5},{5,4},{6,7},{7,6},{8,9},{9,8},{10,11... | collective-permute-start | bytes 49160 | tf_op jit(solution)/shard_map/ppermute | solution.py:420
  57.8 1.3 %collective-permute-done.16 = f32[32,128]{1,0:T(8,128)S(1)} collective-permute-done((f32[32,128]{1,0:T(8,128)S(1)}, f32[32,128]{1,0:T(8,128)S(1)}, u32[]{:S(2)}, u32[]{:S(2)}) %collective-permute-start.16) | collective-permute-done | bytes 16416 | tf_op jit(solution)/shard_map/ppermute | solution.py:420
  59.1 0.7 %collective-permute-done.15 = f32[32,128]{1,0:T(8,128)S(1)} collective-permute-done((f32[32,128]{1,0:T(8,128)S(1)}, f32[32,128]{1,0:T(8,128)S(1)}, u32[]{:S(2)}, u32[]{:S(2)}) %collective-permute-start.15) | collective-permute-done | bytes 16416 | tf_op jit(solution)/shard_map/ppermute | solution.py:420
  59.8 0.0 collective-permute-done.14
  59.9 0.8 %last_update.1 = (f32[20,32]{1,0:T(8,128)}, f32[20,32]{1,0:T(8,128)}, f32[1,32]{1,0:T(1,128)}) custom-call(f32[32,128]{1,0:T(8,128)S(1)} %add_add_fusion.sums_ref, f32[32,128]{1,0:T(8,128)S(1)} %get-tuple-element.37.centers_ref, f32[32,128]{1,0:T(8,128)S(1)} %get-tuple-element.38.spreads_ref), custom_call_target="tpu_custom_call" | custom-call | tf_op jit(solution)/shard_map/last_update/pallas_call | solution.py:549
  (4 shorter events, 0.0 us)
Async XLA Ops:
  0.6 11.6 %collective-permute-start.1 = (bf16[16,24,128]{2,1,0:T(8,128)(2,1)}, bf16[16,24,128]{2,1,0:T(8,128)(2,1)S(1)}, u32[]{:S(2)}, u32[]{:S(2)}) collective-permute-start(bf16[16,24,128]{2,1,0:T(8,128)(2,1)} %own_ref.1), channel_id=1, source_target_pairs={{2,4},{4,2},{6,8},{8,6},{10,12},{12,10},{3,5},{5,3},{7,9},{9,7},{1... | collective-permute-start | bytes 294920 | tf_op jit(solution)/shard_map/ppermute | solution.py:402
  1.3 10.9 %collective-permute-start = (bf16[16,24,128]{2,1,0:T(8,128)(2,1)}, bf16[16,24,128]{2,1,0:T(8,128)(2,1)S(1)}, u32[]{:S(2)}, u32[]{:S(2)}) collective-permute-start(bf16[16,24,128]{2,1,0:T(8,128)(2,1)} %own_ref.1), channel_id=1, source_target_pairs={{0,2},{2,0},{4,6},{6,4},{8,10},{10,8},{12,14},{14,12},{1,3},{3,1},... | collective-permute-start | bytes 294920 | tf_op jit(solution)/shard_map/ppermute | solution.py:402
  7.1 5.8 %collective-permute-start.2 = (bf16[16,24,128]{2,1,0:T(8,128)(2,1)}, bf16[16,24,128]{2,1,0:T(8,128)(2,1)S(1)}, u32[]{:S(2)}, u32[]{:S(2)}) collective-permute-start(bf16[16,24,128]{2,1,0:T(8,128)(2,1)} %own_ref.1), channel_id=1, source_target_pairs={{0,1},{1,0},{2,3},{3,2},{4,5},{5,4},{6,7},{7,6},{8,9},{9,8},{10,11... | collective-permute-start | bytes 294920 | tf_op jit(solution)/shard_map/ppermute | solution.py:402
  8.7 0.9 %copy-start = (bf16[16,24,128]{2,1,0:T(8,128)(2,1)S(1)}, bf16[16,24,128]{2,1,0:T(8,128)(2,1)}, u32[]{:S(2)}) copy-start(bf16[16,24,128]{2,1,0:T(8,128)(2,1)} %own_ref.1) | copy-start | bytes 294916
  9.6 0.7 %copy-start.1 = (s32[10]{0:T(128)S(1)}, s32[10]{0:T(128)}, u32[]{:S(2)}) copy-start(s32[10]{0:T(128)} %directions_ref.1) | copy-start | bytes 124
  12.2 1.5 %collective-permute-start.3 = (bf16[16,24,128]{2,1,0:T(8,128)(2,1)S(1)}, bf16[16,24,128]{2,1,0:T(8,128)(2,1)S(1)}, u32[]{:S(2)}, u32[]{:S(2)}) collective-permute-start(bf16[16,24,128]{2,1,0:T(8,128)(2,1)S(1)} %collective-permute-done.refs_2_), channel_id=1, source_target_pairs={{0,1},{1,0},{2,3},{3,2},{4,5},{5,4},{6,7},{7,6},{8,9},{9,8},{10,11... | collective-permute-start | bytes 294920 | tf_op jit(solution)/shard_map/ppermute | solution.py:402
  12.8 1.3 %collective-permute-start.4 = (bf16[16,24,128]{2,1,0:T(8,128)(2,1)S(1)}, bf16[16,24,128]{2,1,0:T(8,128)(2,1)S(1)}, u32[]{:S(2)}, u32[]{:S(2)}) collective-permute-start(bf16[16,24,128]{2,1,0:T(8,128)(2,1)S(1)} %collective-permute-done.1.refs_4_), channel_id=1, source_target_pairs={{0,1},{1,0},{2,3},{3,2},{4,5},{5,4},{6,7},{7,6},{8,9},{9,8},{10,11... | collective-permute-start | bytes 294920 | tf_op jit(solution)/shard_map/ppermute | solution.py:402
  30.4 5.6 %collective-permute-start.7 = (f32[32,128]{1,0:T(8,128)S(1)}, f32[32,128]{1,0:T(8,128)S(1)}, u32[]{:S(2)}, u32[]{:S(2)}) collective-permute-start(f32[32,128]{1,0:T(8,128)S(1)} %get-tuple-element.34), channel_id=1, source_target_pairs={{0,12},{1,13},{2,14},{3,15},{4,8},{5,9},{6,10},{7,11},{8,4},{9,5},... | collective-permute-start | bytes 49160 | tf_op jit(solution)/shard_map/ppermute | solution.py:420
  33.2 4.7 %collective-permute-start.6 = (f32[32,128]{1,0:T(8,128)S(1)}, f32[32,128]{1,0:T(8,128)S(1)}, u32[]{:S(2)}, u32[]{:S(2)}) collective-permute-start(f32[32,128]{1,0:T(8,128)S(1)} %get-tuple-element.34), channel_id=1, source_target_pairs={{0,8},{1,9},{2,10},{3,11},{4,12},{5,13},{6,14},{7,15},{8,0},{9,1},... | collective-permute-start | bytes 49160 | tf_op jit(solution)/shard_map/ppermute | solution.py:420
  33.5 4.4 %collective-permute-start.5 = (f32[32,128]{1,0:T(8,128)S(1)}, f32[32,128]{1,0:T(8,128)S(1)}, u32[]{:S(2)}, u32[]{:S(2)}) collective-permute-start(f32[32,128]{1,0:T(8,128)S(1)} %get-tuple-element.34), channel_id=1, source_target_pairs={{0,4},{1,5},{2,6},{3,7},{4,0},{5,1},{6,2},{7,3},{8,12},{9,13},{10,... | collective-permute-start | bytes 49160 | tf_op jit(solution)/shard_map/ppermute | solution.py:420
  37.9 3.2 %collective-permute-start.10 = (f32[32,128]{1,0:T(8,128)S(1)}, f32[32,128]{1,0:T(8,128)S(1)}, u32[]{:S(2)}, u32[]{:S(2)}) collective-permute-start(f32[32,128]{1,0:T(8,128)S(1)} %add_add_fusion.3), channel_id=1, source_target_pairs={{0,3},{1,2},{2,1},{3,0},{4,7},{5,6},{6,5},{7,4},{8,11},{9,10},{10,... | collective-permute-start | bytes 49160 | tf_op jit(solution)/shard_map/ppermute | solution.py:420
  38.0 3.8 %collective-permute-start.9 = (f32[32,128]{1,0:T(8,128)S(1)}, f32[32,128]{1,0:T(8,128)S(1)}, u32[]{:S(2)}, u32[]{:S(2)}) collective-permute-start(f32[32,128]{1,0:T(8,128)S(1)} %add_add_fusion.3), channel_id=1, source_target_pairs={{0,2},{1,3},{2,0},{3,1},{4,6},{5,7},{6,4},{7,5},{8,10},{9,11},{10,... | collective-permute-start | bytes 49160 | tf_op jit(solution)/shard_map/ppermute | solution.py:420
  39.3 2.5 %collective-permute-start.8 = (f32[32,128]{1,0:T(8,128)S(1)}, f32[32,128]{1,0:T(8,128)S(1)}, u32[]{:S(2)}, u32[]{:S(2)}) collective-permute-start(f32[32,128]{1,0:T(8,128)S(1)} %add_add_fusion.3), channel_id=1, source_target_pairs={{0,1},{1,0},{2,3},{3,2},{4,5},{5,4},{6,7},{7,6},{8,9},{9,8},{10,11... | collective-permute-start | bytes 49160 | tf_op jit(solution)/shard_map/ppermute | solution.py:420
  49.2 5.7 %collective-permute-start.13 = (f32[32,128]{1,0:T(8,128)S(1)}, f32[32,128]{1,0:T(8,128)S(1)}, u32[]{:S(2)}, u32[]{:S(2)}) collective-permute-start(f32[32,128]{1,0:T(8,128)S(1)} %get-tuple-element.36), channel_id=1, source_target_pairs={{0,12},{1,13},{2,14},{3,15},{4,8},{5,9},{6,10},{7,11},{8,4},{9,5},... | collective-permute-start | bytes 49160 | tf_op jit(solution)/shard_map/ppermute | solution.py:420
  51.1 4.7 %collective-permute-start.12 = (f32[32,128]{1,0:T(8,128)S(1)}, f32[32,128]{1,0:T(8,128)S(1)}, u32[]{:S(2)}, u32[]{:S(2)}) collective-permute-start(f32[32,128]{1,0:T(8,128)S(1)} %get-tuple-element.36), channel_id=1, source_target_pairs={{0,8},{1,9},{2,10},{3,11},{4,12},{5,13},{6,14},{7,15},{8,0},{9,1},... | collective-permute-start | bytes 49160 | tf_op jit(solution)/shard_map/ppermute | solution.py:420
  51.4 4.5 %collective-permute-start.11 = (f32[32,128]{1,0:T(8,128)S(1)}, f32[32,128]{1,0:T(8,128)S(1)}, u32[]{:S(2)}, u32[]{:S(2)}) collective-permute-start(f32[32,128]{1,0:T(8,128)S(1)} %get-tuple-element.36), channel_id=1, source_target_pairs={{0,4},{1,5},{2,6},{3,7},{4,0},{5,1},{6,2},{7,3},{8,12},{9,13},{10,... | collective-permute-start | bytes 49160 | tf_op jit(solution)/shard_map/ppermute | solution.py:420
  55.9 3.2 %collective-permute-start.16 = (f32[32,128]{1,0:T(8,128)S(1)}, f32[32,128]{1,0:T(8,128)S(1)}, u32[]{:S(2)}, u32[]{:S(2)}) collective-permute-start(f32[32,128]{1,0:T(8,128)S(1)} %add_add_fusion.1), channel_id=1, source_target_pairs={{0,3},{1,2},{2,1},{3,0},{4,7},{5,6},{6,5},{7,4},{8,11},{9,10},{10,... | collective-permute-start | bytes 49160 | tf_op jit(solution)/shard_map/ppermute | solution.py:420
  56.0 3.9 %collective-permute-start.15 = (f32[32,128]{1,0:T(8,128)S(1)}, f32[32,128]{1,0:T(8,128)S(1)}, u32[]{:S(2)}, u32[]{:S(2)}) collective-permute-start(f32[32,128]{1,0:T(8,128)S(1)} %add_add_fusion.1), channel_id=1, source_target_pairs={{0,2},{1,3},{2,0},{3,1},{4,6},{5,7},{6,4},{7,5},{8,10},{9,11},{10,... | collective-permute-start | bytes 49160 | tf_op jit(solution)/shard_map/ppermute | solution.py:420
  56.9 3.0 %collective-permute-start.14 = (f32[32,128]{1,0:T(8,128)S(1)}, f32[32,128]{1,0:T(8,128)S(1)}, u32[]{:S(2)}, u32[]{:S(2)}) collective-permute-start(f32[32,128]{1,0:T(8,128)S(1)} %add_add_fusion.1), channel_id=1, source_target_pairs={{0,1},{1,0},{2,3},{3,2},{4,5},{5,4},{6,7},{7,6},{8,9},{9,8},{10,11... | collective-permute-start | bytes 49160 | tf_op jit(solution)/shard_map/ppermute | solution.py:420
